TPU v7x, 32 devices: a whole 2x2x4 slice. The times are simulated.
32 devices in a mesh: seq: 16 (over z, x, core), wt: 2 (over y).
Axes of the slice: x: 2, y: 2, z: 4, core: 2. Of those that a mesh axis runs over, the one named last changes fastest.
Arguments:
- tokens: bfloat16 [2, 2048, 1600], P('wt', 'seq'), may hold values from -6 to 6
- segment_ids: int32 [2, 2048], P('wt'), may hold values from 0 to 2, as said below
- cotangent: bfloat16 [2, 2048, 1600], P('wt', 'seq'), may hold values from -6 to 6
- norm_gain: float32 [1600], replicated, may hold values from 0.5 to 1.5
- query_weight: bfloat16 [1600, 1600], P(None, 'wt'), may hold values from -0.15625 to 0.15625
- key_weight: bfloat16 [1600, 320], P(None, 'wt'), may hold values from -0.15625 to 0.15625
- value_weight: bfloat16 [1600, 320], P(None, 'wt'), may hold values from -0.15625 to 0.15625
- head_weight: bfloat16 [1600, 1600], P(None, 'wt'), may hold values from -0.15625 to 0.15625
- input_weight: bfloat16 [1600, 6400], P(None, 'wt'), may hold values from -0.15625 to 0.15625
- filter_weight: float32 [4, 3200], replicated, may hold values from -3 to 3
- filter_bias: float32 [3200], replicated, may hold values from -3 to 3
- select_weight: bfloat16 [3200, 132], P(None, 'wt'), may hold values from -0.109375 to 0.109375
- step_weight: bfloat16 [3200, 100], P(None, 'wt'), may hold values from -0.625 to 0.625
- step_offset: float32 [3200], replicated, may hold values from -4 to -2
- decay_log: float32 [16, 3200], replicated, may hold values from -11 to 1
- direct_skip_weight: float32 [3200], replicated, may hold values from 0.5 to 1.5
- mixer_weight: bfloat16 [3200, 1600], P(None, 'wt'), may hold values from -0.109375 to 0.109375
- attend_gain: float32 [1600], replicated, may hold values from 0.5 to 1.5
- state_gain: float32 [1600], replicated, may hold values from 0.5 to 1.5
- feed_gain: float32 [1600], replicated, may hold values from 0.5 to 1.5
- gate_weight: bfloat16 [1600, 5504], P(None, 'wt'), may hold values from -0.15625 to 0.15625
- up_weight: bfloat16 [1600, 5504], P(None, 'wt'), may hold values from -0.15625 to 0.15625
- down_weight: bfloat16 [1600, 5504], P(None, 'wt'), may hold values from -0.078125 to 0.078125
Outputs:
- result: bfloat16 [2, 2048, 1600], P('wt', 'seq')
- tokens_gradient: float32 [2, 2048, 1600], P('wt', 'seq')
- norm_gradient: float32 [1600], replicated
- query_gradient: float32 [1600, 1600], P('seq', 'wt')
- key_gradient: float32 [1600, 320], P('seq', 'wt')
- value_gradient: float32 [1600, 320], P('seq', 'wt')
- head_gradient: float32 [1600, 1600], P('seq', 'wt')
- input_gradient: float32 [1600, 6400], P('seq', 'wt')
- filter_gradient: float32 [4, 3200], replicated
- bias_gradient: float32 [3200], replicated
- select_gradient: float32 [3200, 132], P('seq', 'wt')
- step_gradient: float32 [3200, 100], P('seq', 'wt')
- offset_gradient: float32 [3200], replicated
- decay_gradient: float32 [16, 3200], replicated
- skip_gradient: float32 [3200], replicated
- mixer_gradient: float32 [3200, 1600], P('seq', 'wt')
- attend_gradient: float32 [1600], replicated
- state_gradient: float32 [1600], replicated
- feed_gradient: float32 [1600], replicated
- gate_gradient: float32 [1600, 5504], P('seq', 'wt')
- up_gradient: float32 [1600, 5504], P('seq', 'wt')
- down_gradient: float32 [1600, 5504], P('seq', 'wt')
Inputs may be any that keep to these rules, and one draw needn't show every extreme that they name: `segment_ids`: along each sequence the ids never fall: document 0 ends within the first 128 tokens, document 2 begins within the last 128 tokens, and document 1 lies between.
All inputs are finite; a program needn't handle non-finite values.
Results may differ from a plain program's by a relative error of at most 0.015.
The roundings to bfloat16 on the way count: a program that leaves them out, or rounds other values in their place, can miss the bound.
Values may be sent and summed in bfloat16 or wider, within the bound.
A program may use at most 768 MiB of HBM per device.

v0:
```python
import math

import jax
import jax.numpy as jnp
from jax import lax
from jax.sharding import PartitionSpec as P

HEAD_SIZE = 64
WINDOW = 1024


epsilon = 1e-06
masked = -1e30


def for_sending(shard):
    return jax.tree.map(lambda a: a.astype(jnp.bfloat16) if a.dtype == jnp.float32 else a, shard)


def passed_along(block, axis, distance):
    devices = range(lax.axis_size(axis))
    route = [(i - distance, i) for i in devices if i - distance in devices]
    return lax.ppermute(block, axis, route)


def carried_in(part, axis, combine, identity, reverse):
    count = lax.axis_size(axis)
    place = lax.axis_index(axis)
    ahead = count - 1 - place if reverse else place
    gathered = jax.tree.map(lambda a: lax.all_gather(a, axis), part)
    state = jax.tree.map(lambda a, e: jnp.zeros_like(a) + jnp.asarray(e, a.dtype), part, identity)

    def one(turn, state):
        source = count - 1 - turn if reverse else turn
        return combine(
            state, jax.tree.map(lambda a: lax.dynamic_index_in_dim(a, source, 0, False), gathered)
        )

    return lax.fori_loop(0, ahead, one, state)


def product(left, right):
    return jnp.dot(left, right, preferred_element_type=jnp.float32)


def left_product(left, right):
    return lax.dot_general(
        left, right, (((0,), (0,)), ((), ())), preferred_element_type=jnp.float32
    )


def right_product(left, right):
    return lax.dot_general(
        left, right, (((1,), (1,)), ((), ())), preferred_element_type=jnp.float32
    )


def inverse_norm(value):
    return lax.rsqrt(jnp.mean(value * value, axis=-1, keepdims=True) + epsilon)


def norm_back(value, scale, incoming):
    return scale * incoming - scale * scale * scale * value * jnp.mean(
        incoming * value, axis=-1, keepdims=True
    )


def silu_slope(value):
    sigma = jax.nn.sigmoid(value)
    return sigma * (1.0 + value * (1.0 - sigma))


def link(earlier, later):
    return (earlier[0] * later[0], later[0] * earlier[1] + later[1])


def factors(size, value, into, keep, decay):
    factor = jnp.exp(size[:, None, :] * decay[None]) * keep[:, None, None]
    inject = (size * value)[:, None, :] * into[:, :, None]
    return (factor, inject)


def fetch(shards):
    return jax.tree.map(
        lambda part, own: part.astype(own.dtype),
        lax.all_gather(for_sending(shards), "wt", axis=1, tiled=True),
        shards,
    )


def reduce_terms(terms):
    terms = lax.psum_scatter(terms, "wt", scatter_dimension=1, tiled=True)
    return lax.psum_scatter(terms, "seq", scatter_dimension=0, tiled=True)


def feed_block(second_rows, back_rows, gate_cols, up_cols, down_cols):
    gate_raw = product(second_rows, gate_cols)
    up_raw = product(second_rows, up_cols)
    sigma_gate = jax.nn.sigmoid(gate_raw)
    activated = (gate_raw * sigma_gate * up_raw).astype(jnp.bfloat16)
    feed_out = right_product(activated, down_cols)
    delta_act = product(back_rows, down_cols)
    delta_gate = (delta_act * up_raw * silu_slope(gate_raw)).astype(jnp.bfloat16)
    delta_up = (delta_act * gate_raw * sigma_gate).astype(jnp.bfloat16)
    delta_second = right_product(delta_gate, gate_cols) + right_product(delta_up, up_cols)
    terms = (
        left_product(second_rows, delta_gate),
        left_product(second_rows, delta_up),
        left_product(back_rows, activated),
    )
    return (feed_out, delta_second, terms)


def per_device(
    tokens,
    segment_ids,
    cotangent,
    norm_gain,
    query_weight,
    key_weight,
    value_weight,
    head_weight,
    input_weight,
    filter_weight,
    filter_bias,
    select_weight,
    step_weight,
    step_offset,
    decay_log,
    direct_skip_weight,
    mixer_weight,
    attend_gain,
    state_gain,
    feed_gain,
    gate_weight,
    up_weight,
    down_weight,
):
    rows = tokens.shape[1]
    model = tokens.shape[2]
    inner = filter_weight.shape[1]
    kernel = filter_weight.shape[0]
    states = decay_log.shape[0]
    start = lax.axis_index("seq") * rows
    whole_segment = segment_ids[0]
    padded_segment = jnp.concatenate([jnp.full((WINDOW,), -1, jnp.int32), whole_segment])
    segment = lax.dynamic_slice_in_dim(whole_segment, start, rows)
    inputs = tokens[0].astype(jnp.float32)
    upstream = cotangent[0].astype(jnp.float32)
    mixer_shards = (
        query_weight,
        key_weight,
        value_weight,
        head_weight,
        input_weight,
        select_weight,
        step_weight,
        mixer_weight,
    )
    query_full, key_full, value_full, head_full, input_full, select_full, step_full, mixer_full = (
        fetch(mixer_shards)
    )
    rank = step_full.shape[1]
    key_heads = key_full.shape[1] // HEAD_SIZE
    groups = query_full.shape[1] // key_full.shape[1]
    first_scale = inverse_norm(inputs)
    normed = (inputs * first_scale * norm_gain).astype(jnp.bfloat16)
    query = product(normed, query_full).astype(jnp.bfloat16)
    grouped = query.reshape(rows, key_heads, groups, HEAD_SIZE)
    pairs = jnp.stack([product(normed, key_full), product(normed, value_full)]).astype(jnp.bfloat16)
    reach = WINDOW // rows
    pieces = []
    for offset in range(reach, 0, -1):
        pieces.append(passed_along(pairs, "seq", offset))
    pieces.append(pairs)
    near = jnp.concatenate(pieces, axis=1)
    span = near.shape[1]
    near_keys = near[0].reshape(span, key_heads, HEAD_SIZE)
    near_values = near[1].reshape(span, key_heads, HEAD_SIZE)
    near_segment = lax.dynamic_slice_in_dim(padded_segment, start, span)
    distance = (
        jnp.arange(rows, dtype=jnp.int32)[:, None]
        + reach * rows
        - jnp.arange(span, dtype=jnp.int32)[None, :]
    )
    allowed = (distance >= 0) & (distance < WINDOW) & (segment[:, None] == near_segment[None, :])

    def score_table():
        raw = (
            jnp.einsum("tkgd,mkd->kgtm", grouped, near_keys, preferred_element_type=jnp.float32)
            * 0.125
        )
        return jnp.where(allowed, raw, masked)

    scores = score_table()
    top = jnp.max(scores, axis=-1, keepdims=True)
    raised = jnp.exp(scores - top)
    total = jnp.sum(raised, axis=-1, keepdims=True)
    logsum = top + jnp.log(total)
    chances = (raised / total).astype(jnp.bfloat16)
    attended = (
        jnp.einsum("kgtm,mkd->tkgd", chances, near_values, preferred_element_type=jnp.float32)
        .reshape(rows, model)
        .astype(jnp.bfloat16)
    )
    head_out = product(attended, head_full)
    entered = product(normed, input_full)
    inner_rows = entered[:, :inner].astype(jnp.bfloat16)
    gate_input = entered[:, inner:]
    before = passed_along(inner_rows[rows - kernel + 1 :], "seq", 1)
    extended = jnp.concatenate([before, inner_rows], axis=0).astype(jnp.float32)
    edge_segment = lax.dynamic_slice_in_dim(
        padded_segment, start + WINDOW - kernel + 1, rows + kernel - 1
    )
    taps = []
    sames = []
    filtered = filter_bias + jnp.zeros((rows, inner), jnp.float32)
    for tap in range(kernel):
        begin = kernel - 1 - tap
        same = (edge_segment[begin : begin + rows] == segment).astype(jnp.float32)
        kept_rows = extended[begin : begin + rows] * same[:, None]
        taps.append(kept_rows)
        sames.append(same)
        filtered = filtered + filter_weight[tap] * kept_rows
    smoothed = (filtered * jax.nn.sigmoid(filtered)).astype(jnp.bfloat16)
    scan_input_rows = smoothed.astype(jnp.float32)
    projected = product(smoothed, select_full)
    step_low = projected[:, :rank].astype(jnp.bfloat16)
    entry = projected[:, rank : rank + states]
    read = projected[:, rank + states :]
    unsquashed_step = right_product(step_low, step_full) + step_offset
    step = jnp.log1p(jnp.exp(unsquashed_step))
    previous = lax.dynamic_slice_in_dim(padded_segment, start + WINDOW - 1, rows)
    hold = (previous == segment).astype(jnp.float32)
    decay = -jnp.exp(decay_log)
    part = math.gcd(rows, 16)
    count = rows // part

    def stretched(value_array):
        return value_array.reshape((count, part) + value_array.shape[1:]).swapaxes(0, 1)

    def whole_sequence_scan(value_array):
        return value_array.swapaxes(0, 1).reshape((rows,) + value_array.shape[2:])

    scan_items = (
        stretched(step),
        stretched(scan_input_rows),
        stretched(entry),
        stretched(read),
        stretched(hold),
    )
    zero_state = jnp.zeros((count, states, inner), jnp.float32)
    unit_state = jnp.ones((count, states, inner), jnp.float32)
    unit = (jnp.ones((states, inner), jnp.float32), jnp.zeros((states, inner), jnp.float32))

    def local_step(carry, item):
        factor, inject = factors(item[0], item[1], item[2], item[4], decay)
        return ((carry[0] * factor, factor * carry[1] + inject), None)

    (stretch_prod, stretch_state), _ = lax.scan(local_step, (unit_state, zero_state), scan_items)
    running = lax.associative_scan(link, (stretch_prod, stretch_state), axis=0)
    entering = carried_in((running[0][-1], running[1][-1]), "seq", link, unit, False)[1]
    stretch_start = (
        jnp.concatenate([zero_state[:1], running[1][:-1]], axis=0)
        + jnp.concatenate([unit_state[:1], running[0][:-1]], axis=0) * entering[None]
    )

    def run_step(state, item):
        factor, inject = factors(item[0], item[1], item[2], item[4], decay)
        state = factor * state + inject
        return (state, jnp.sum(item[3][:, :, None] * state, axis=1))

    _, scanned_rows = lax.scan(run_step, stretch_start, scan_items)
    scan_result_rows = whole_sequence_scan(scanned_rows) + direct_skip_weight * scan_input_rows
    sigma_input = jax.nn.sigmoid(gate_input)
    silu_input = gate_input * sigma_input
    gated = (scan_result_rows * silu_input).astype(jnp.bfloat16)
    branch = product(gated, mixer_full)
    head_scale = inverse_norm(head_out)
    branch_scale = inverse_norm(branch)
    hidden = inputs + 0.5 * (
        head_out * head_scale * attend_gain + branch * branch_scale * state_gain
    )
    second_scale = inverse_norm(hidden)
    second = (hidden * second_scale * feed_gain).astype(jnp.bfloat16)
    feed_back = cotangent[0]
    feed_full = fetch((gate_weight, up_weight, down_weight))
    feed_out, delta_second, feed_terms = feed_block(
        second, feed_back, feed_full[0], feed_full[1], feed_full[2]
    )
    gate_gradient, up_gradient, down_gradient = reduce_terms(feed_terms)
    result = (hidden + feed_out).astype(jnp.bfloat16)
    feed_sum = jnp.sum(delta_second * hidden * second_scale, axis=0)
    delta_hidden = upstream + norm_back(hidden, second_scale, delta_second * feed_gain)
    query_full, key_full, value_full, head_full, input_full, select_full, step_full, mixer_full = (
        fetch(mixer_shards)
    )
    half = 0.5 * delta_hidden
    attend_sum = jnp.sum(half * head_out * head_scale, axis=0)
    state_sum = jnp.sum(half * branch * branch_scale, axis=0)
    delta_head = norm_back(head_out, head_scale, half * attend_gain).astype(jnp.bfloat16)
    delta_branch = norm_back(branch, branch_scale, half * state_gain).astype(jnp.bfloat16)
    delta_attended = (
        right_product(delta_head, head_full)
        .astype(jnp.bfloat16)
        .reshape(rows, key_heads, groups, HEAD_SIZE)
    )
    weights = jnp.exp(score_table() - logsum)
    chances = weights.astype(jnp.bfloat16)
    delta_chance = jnp.einsum(
        "tkgd,mkd->kgtm", delta_attended, near_values, preferred_element_type=jnp.float32
    )
    value_near = jnp.einsum(
        "kgtm,tkgd->mkd", chances, delta_attended, preferred_element_type=jnp.float32
    )
    delta_scores = (
        weights * (delta_chance - jnp.sum(weights * delta_chance, axis=-1, keepdims=True))
    ).astype(jnp.bfloat16)
    delta_query = (
        (
            jnp.einsum(
                "kgtm,mkd->tkgd", delta_scores, near_keys, preferred_element_type=jnp.float32
            )
            * 0.125
        )
        .reshape(rows, model)
        .astype(jnp.bfloat16)
    )
    key_near = (
        jnp.einsum("kgtm,tkgd->mkd", delta_scores, grouped, preferred_element_type=jnp.float32)
        * 0.125
    )
    delta_near = jnp.stack([key_near, value_near]).reshape(2, span, key_heads * HEAD_SIZE)
    delta_pairs = delta_near[:, reach * rows :]
    for offset in range(reach, 0, -1):
        piece = delta_near[:, (reach - offset) * rows : (reach - offset + 1) * rows]
        delta_pairs = delta_pairs + passed_along(piece.astype(jnp.bfloat16), "seq", -offset).astype(
            piece.dtype
        )
    delta_pairs = delta_pairs.astype(jnp.bfloat16)
    delta_normed = (
        right_product(delta_query, query_full)
        + right_product(delta_pairs[0], key_full)
        + right_product(delta_pairs[1], value_full)
    )
    delta_gated = right_product(delta_branch, mixer_full)
    delta_scan_output = delta_gated * silu_input
    delta_gate = (delta_gated * scan_result_rows * silu_slope(gate_input)).astype(jnp.bfloat16)
    skip_sum = jnp.sum(delta_scan_output * scan_input_rows, axis=0)
    back_items = scan_items + (stretched(delta_scan_output),)

    def back_step(carry, item):
        factor, _ = factors(item[0], item[1], item[2], item[4], decay)
        adjoint = item[3][:, :, None] * item[5][:, None, :] + carry[0]
        return ((factor * adjoint, carry[1] * factor), None)

    (stretch_beta, stretch_alpha), _ = lax.scan(
        back_step, (zero_state, unit_state), back_items, reverse=True
    )
    backward_run = lax.associative_scan(link, (stretch_alpha, stretch_beta), axis=0, reverse=True)
    arriving = carried_in((backward_run[0][0], backward_run[1][0]), "seq", link, unit, True)[1]
    stretch_end = jnp.concatenate(
        [backward_run[1][1:] + backward_run[0][1:] * arriving[None], arriving[None]], axis=0
    )

    def store_step(state, item):
        factor, inject = factors(item[0], item[1], item[2], item[4], decay)
        return (factor * state + inject, state)

    _, priors = lax.scan(store_step, stretch_start, scan_items)

    def delta_step(carry, item):
        size, value, into, output, keep, incoming, prior = item
        factor, inject = factors(size, value, into, keep, decay)
        current = factor * prior + inject
        adjoint = output[:, :, None] * incoming[:, None, :] + carry[0]
        weighted = adjoint * prior * factor
        through = jnp.sum(adjoint * into[:, :, None], axis=1)
        delta_size = jnp.sum(weighted * decay[None], axis=1) + through * value
        delta_value = through * size
        delta_into = jnp.sum(adjoint * (size * value)[:, None, :], axis=2)
        delta_output = jnp.sum(incoming[:, None, :] * current, axis=2)
        decay_acc = carry[1] + jnp.sum(weighted * size[:, None, :], axis=0)
        return ((factor * adjoint, decay_acc), (delta_size, delta_value, delta_into, delta_output))

    (_, decay_acc), scan_gradient_tuple = lax.scan(
        delta_step,
        (stretch_end, jnp.zeros((states, inner), jnp.float32)),
        back_items + (priors,),
        reverse=True,
    )
    decay_sum = decay_acc * decay
    delta_scan_input = delta_scan_output * direct_skip_weight + whole_sequence_scan(
        scan_gradient_tuple[1]
    )
    delta_unsquashed_step = whole_sequence_scan(scan_gradient_tuple[0]) * jax.nn.sigmoid(
        unsquashed_step
    )
    offset_sum = jnp.sum(delta_unsquashed_step, axis=0)
    raw_low = delta_unsquashed_step.astype(jnp.bfloat16)
    delta_lowrank_step = product(raw_low, step_full)
    delta_projected = jnp.concatenate(
        [
            delta_lowrank_step,
            whole_sequence_scan(scan_gradient_tuple[2]),
            whole_sequence_scan(scan_gradient_tuple[3]),
        ],
        axis=1,
    ).astype(jnp.bfloat16)
    delta_scan_input = delta_scan_input + right_product(delta_projected, select_full)
    delta_filtered = delta_scan_input * silu_slope(filtered)
    bias_sum = jnp.sum(delta_filtered, axis=0)
    filter_sums = jnp.stack([jnp.sum(delta_filtered * kept_rows, axis=0) for kept_rows in taps])
    delta_extended = jnp.zeros((rows + kernel - 1, inner), jnp.float32)
    for tap in range(kernel):
        begin = kernel - 1 - tap
        delta_extended = delta_extended.at[begin : begin + rows].add(
            delta_filtered * filter_weight[tap] * sames[tap][:, None]
        )
    arrived = passed_along(delta_extended[: kernel - 1].astype(jnp.bfloat16), "seq", -1).astype(
        jnp.float32
    )
    delta_inner = delta_extended[kernel - 1 :] + jnp.pad(arrived, ((rows - kernel + 1, 0), (0, 0)))
    delta_entered = jnp.concatenate([delta_inner.astype(jnp.bfloat16), delta_gate], axis=1)
    delta_normed = delta_normed + right_product(delta_entered, input_full)
    norm_sum = jnp.sum(delta_normed * inputs * first_scale, axis=0)
    delta_tokens = delta_hidden + norm_back(inputs, first_scale, delta_normed * norm_gain)
    query_sums = left_product(normed, delta_query)
    key_sums = left_product(normed, delta_pairs[0])
    value_sums = left_product(normed, delta_pairs[1])
    head_sums = left_product(attended, delta_head)
    input_sums = left_product(normed, delta_entered)
    select_sums = left_product(smoothed, delta_projected)
    step_sums = left_product(raw_low, step_low)
    mixer_sums = left_product(gated, delta_branch)
    mixer_grads = reduce_terms(
        (
            query_sums,
            key_sums,
            value_sums,
            head_sums,
            input_sums,
            select_sums,
            step_sums,
            mixer_sums,
        )
    )
    smalls = lax.psum(
        (
            norm_sum,
            filter_sums,
            bias_sum,
            offset_sum,
            decay_sum,
            skip_sum,
            attend_sum,
            state_sum,
            feed_sum,
        ),
        ("seq", "wt"),
    )
    return (
        result[None],
        delta_tokens[None],
        smalls[0],
        mixer_grads[0],
        mixer_grads[1],
        mixer_grads[2],
        mixer_grads[3],
        mixer_grads[4],
        smalls[1],
        smalls[2],
        mixer_grads[5],
        mixer_grads[6],
        smalls[3],
        smalls[4],
        smalls[5],
        mixer_grads[7],
        smalls[6],
        smalls[7],
        smalls[8],
        gate_gradient,
        up_gradient,
        down_gradient,
    )


def solution(mesh):
    placed = (
        P("wt", "seq", None),
        P("wt", None),
        P("wt", "seq", None),
        P(),
        P(None, "wt"),
        P(None, "wt"),
        P(None, "wt"),
        P(None, "wt"),
        P(None, "wt"),
        P(),
        P(),
        P(None, "wt"),
        P(None, "wt"),
        P(),
        P(),
        P(),
        P(None, "wt"),
        P(),
        P(),
        P(),
        P(None, "wt"),
        P(None, "wt"),
        P(None, "wt"),
    )
    return jax.shard_map(
        per_device,
        mesh=mesh,
        in_specs=placed,
        out_specs=(
            P("wt", "seq", None),
            P("wt", "seq", None),
            P(),
            P("seq", "wt"),
            P("seq", "wt"),
            P("seq", "wt"),
            P("seq", "wt"),
            P("seq", "wt"),
            P(),
            P(),
            P("seq", "wt"),
            P("seq", "wt"),
            P(),
            P(),
            P(),
            P("seq", "wt"),
            P(),
            P(),
            P(),
            P("seq", "wt"),
            P("seq", "wt"),
            P("seq", "wt"),
        ),
        check_vma=False,
    )
```

profile of v0, /device:TPU:0, one launch (start us, length us, event | category | flops | bytes accessed | tf_op | source)
XLA Modules:
  0.0 4781.0 jit_solution(3331726522165622866)
XLA Ops:
  12.5 12.1 all-gather.1
  24.6 17.0 all-gather
  42.9 213.8 %all-gather.21.cloned.1.call-done = bf16[1600,6400]{1,0:T(8,128)(2,1)} async-done(((bf16[1600,3200]{1,0:T(8,128)(2,1)}), bf16[1600,6400]{1,0:T(8,128)(2,1)}) %all-gather.21.cloned.1.call-update) | async-done | bytes 20480016 | tf_op jit(solution)/shard_map/all_gather | solution.py:86
  256.7 11.9 fusion.130
  295.4 61.3 %while.113 = (s32[]{:T(128)}, f32[8,16,3200]{2,1,0:T(8,128)S(1)}, f32[8,16,3200]{2,1,0:T(8,128)S(1)}, f32[16,8,3200]{2,1,0:T(8,128)}, f32[16,3200]{1,0:T(8,128)S...) while((s32[]{:T(128)}, f32[8,16,3200]{2,1,0:T(8,128)S(1)}, ...), condition=%wide.region_5.6_spmd.clone, body=%wide.region_4.5_spmd.clone.sunk | while | flops 3302403 | bytes 7476967 | solution.py:260
  379.1 27.3 all_gather.53
  408.0 14.8 all_gather.54
  445.6 15.3 collective-permute-start.2
  480.2 7.4 fusion.131
  487.6 7.3 fusion.23
  495.6 8.7 fusion.38
  504.2 5.0 multiply_reduce_fusion.19
  509.8 119.7 %all-gather.37.cloned.1.call-done = bf16[2,2752,1600]{1,2,0:T(8,128)(2,1)} async-done(((bf16[1,2752,1600]{1,2,0:T(8,128)(2,1)}), bf16[2,2752,1600]{1,2,0:T(8,128)(2,1)}) %all-gather.37.cloned.1.call-update) | async-done | bytes 17612816 | tf_op jit(solution)/shard_map/all_gather | solution.py:86
  629.5 24.8 copy.102
  654.3 191.7 %all-gather.35.cloned.1.call-done = bf16[2,2752,1600]{1,2,0:T(8,128)(2,1)} async-done(((bf16[1,2752,1600]{1,2,0:T(8,128)(2,1)}), bf16[2,2752,1600]{1,2,0:T(8,128)(2,1)}) %all-gather.35.cloned.1.call-update) | async-done | bytes 17612816 | tf_op jit(solution)/shard_map/all_gather | solution.py:86
  845.9 24.8 copy.101
  870.7 191.7 %all-gather.33.cloned.1.call-done = bf16[2,2752,1600]{1,2,0:T(8,128)(2,1)} async-done(((bf16[1,2752,1600]{1,2,0:T(8,128)(2,1)}), bf16[2,2752,1600]{1,2,0:T(8,128)(2,1)}) %all-gather.33.cloned.1.call-update) | async-done | bytes 17612816 | tf_op jit(solution)/shard_map/all_gather | solution.py:86
  1062.4 23.5 copy.100
  1112.7 45.3 all-gather.23.cloned.1.call-done
  1164.1 81.1 %while.110 = (s32[]{:T(128)}, f32[8,16,3200]{2,1,0:T(8,128)S(1)}, f32[16,8,3200]{2,1,0:T(8,128)}, f32[16,8,3200]{2,1,0:T(8,128)}, f32[16,3200]{1,0:T(8,128)S(1)}...) while((s32[]{:T(128)}, f32[8,16,3200]{2,1,0:T(8,128)S(1)}, ...), condition=%wide.region_10.11_spmd, body=%wide.region_8.10_spmd.sunk | while | flops 2867202 | bytes 4508897 | solution.py:273
  1251.2 34.1 all-gather.27.cloned.1.call-done
  1285.3 5.8 multiply_reduce_fusion.18
  1293.4 13.3 fusion.134
  1306.8 13.2 fusion.133
  1320.0 12.1 multiply_convert_fusion.1
  1332.1 14.6 fusion.135
  1346.8 16.4 multiply_reduce_fusion.11
  1367.7 8.0 multiply_reduce_fusion.6
  1378.3 54.2 %while.114 = (s32[]{:T(128)}, f32[8,16,3200]{2,1,0:T(8,128)S(1)}, f32[8,16,3200]{2,1,0:T(8,128)S(1)}, f32[16,8,3200]{2,1,0:T(8,128)}, f32[16,3200]{1,0:T(8,128)S...) while((s32[]{:T(128)}, f32[8,16,3200]{2,1,0:T(8,128)S(1)}, ...), condition=%wide.region_18.19_spmd.clone, body=%wide.region_17.18_spmd.clone.sunk | while | flops 3276804 | bytes 7374583 | solution.py:357
  1460.6 13.9 multiply_reduce_fusion.5
  1475.3 7.6 multiply_convert_fusion
  1500.3 12.3 collective-permute-done.9
  1516.7 9.3 collective-permute-done.13
  1529.4 5.2 collective-permute-done.10
  1539.9 5.5 fusion.136
  1551.0 5.6 fusion.106
  1558.0 76.8 %while.112 = (s32[]{:T(128)}, f32[8,16,3200]{2,1,0:T(8,128)S(1)}, f32[16,8,16,3200]{3,2,1,0:T(8,128)}, f32[16,8,3200]{2,1,0:T(8,128)}, f32[16,3200]{1,0:T(8,128)...) while((s32[]{:T(128)}, f32[8,16,3200]{2,1,0:T(8,128)S(1)}, ...), condition=%wide.region_22.23_spmd, body=%wide.region_21.22_spmd.sunk | while | flops 2073602 | bytes 7476953 | solution.py:370
  1653.6 11.0 fusion.137
  1667.3 18.0 while.111
  1688.3 135.9 %while.115 = (s32[]{:T(128)}, f32[8,16,3200]{2,1,0:T(8,128)S(1)}, f32[16,3200]{1,0:T(8,128)S(1)}, f32[16,8,3200]{2,1,0:T(8,128)}, f32[16,8,3200]{2,1,0:T(8,128)}...) while((s32[]{:T(128)}, f32[8,16,3200]{2,1,0:T(8,128)S(1)}, ...), condition=%wide.region_29.30_spmd.clone, body=%wide.region_23.29_spmd.clone.sunk | while | flops 8294148 | bytes 7794499 | solution.py:386
  1829.2 76.8 %fusion.116 = (f32[3200,80]{0,1:T(8,128)}, f32[3200,64]{0,1:T(8,128)}) fusion(f32[3200,132]{0,1:T(8,128)S(1)} %fusion.98, f32[3200,100]{0,1:T(8,128)S(1)} %fusion.71), kind=kCustom, calls=%all-reduce-scatter.8 | all-reduce-scatter fusion | flops 921602 | bytes 4813312
  1923.3 230.7 %reduce-scatter.45.cloned.1.call-done = f32[3200,800]{0,1:T(8,128)} async-done(((f32[3200,1600]{0,1:T(8,128)}), f32[3200,800]{0,1:T(8,128)}) %reduce-scatter.45.cloned.1.call-update) | async-done | bytes 10240016 | tf_op jit(solution)/shard_map/reduce_scatter | solution.py:92
  2155.5 14.6 convolution_bitcast_fusion.2
  2170.1 34.6 copy.143
  2206.1 15.5 convolution_bitcast_fusion
  2223.3 14.8 convolution_bitcast_fusion.1
  2262.2 17.7 fusion.41
  2283.7 12.0 fusion.34
  2303.3 9.9 fusion.42
  2317.0 281.0 %all-reduce.61.cloned.1.call-done = (f32[1600,800]{0,1:T(8,128)}, f32[1600,160]{0,1:T(8,128)}, f32[1600,160]{0,1:T(8,128)}, f32[1600,800]{0,1:T(8,128)}, f32[320...) async-done(((f32[1600,800]{0,1:T(8,128)}, f32[1600,160]{0,1:T(8,128)}, f32[1600,160]{0,1:T(8,128)}, f32[1600,800]{0,1:T(8,128)}, f32[3200,66]{0,1:T(8,128)}, ...) | async-done | bytes 24012816
  2606.8 395.8 %reduce-scatter.51.cloned.1.call-done = f32[2752,1600]{1,0:T(8,128)} async-done(((f32[5504,1600]{1,0:T(8,128)}), f32[2752,1600]{1,0:T(8,128)}) %reduce-scatter.51.cloned.1.call-update) | async-done | bytes 17612816
  3002.6 19.8 copy.144
  3022.3 385.2 %reduce-scatter.49.cloned.1.call-done = f32[2752,1600]{1,0:T(8,128)} async-done(((f32[5504,1600]{1,0:T(8,128)}), f32[2752,1600]{1,0:T(8,128)}) %reduce-scatter.49.cloned.1.call-update) | async-done | bytes 17612816
  3407.6 19.8 copy.142
  3427.4 364.7 %fusion.115 = (f32[104,2752]{1,0:T(8,128)S(1)}, f32[104,2752]{1,0:T(8,128)S(1)}) fusion(f32[1600,2752]{1,0:T(8,128)} %copy.142, f32[1600,2752]{1,0:T(8,128)} %copy.144), kind=kCustom, calls=%all-reduce-scatter.7 | all-reduce-scatter fusion | flops 9158657 | bytes 37515776
  3793.1 29.2 collective-permute-start.24
  3827.0 19.9 copy.140
  3846.8 417.2 %reduce-scatter.43.cloned.1.call-done = f32[1600,3200]{1,0:T(8,128)} async-done(((f32[1600,6400]{1,0:T(8,128)}), f32[1600,3200]{1,0:T(8,128)}) %reduce-scatter.43.cloned.1.call-update) | async-done | bytes 20480016 | tf_op jit(solution)/shard_map/reduce_scatter | solution.py:92
  4264.0 409.4 %fusion.114 = (f32[112,3200]{1,0:T(8,128)S(1)}, f32[104,2752]{1,0:T(8,128)}) fusion(f32[1600,3200]{1,0:T(8,128)} %reduce-scatter.43.cloned.1.call-done, f32[1600,2752]{1,0:T(8,128)} %copy.140), kind=kCustom, calls=%all-reduce-scatter.6 | all-reduce-scatter fusion | flops 10313730 | bytes 40671744
  4673.3 32.5 collective-permute-start.18
  4710.7 7.3 concatenate.79
  4727.1 6.6 concatenate.78
  4736.2 6.6 concatenate.77
  4747.2 12.2 concatenate.74
  (1174 shorter events, 774.7 us)
Async XLA Ops:
  7.2 249.5 %all-gather.21.cloned.1.call-start = ((), (), s32[]{:S(2)}) async-start(), calls=%async_computation.11 | async-start | bytes 30720000 | tf_op jit(solution)/shard_map/all_gather | solution.py:86
  7.9 467.9 %all-gather.17.cloned.1.call-start = ((), (), s32[]{:S(2)}) async-start(), calls=%async_computation.9 | async-start | bytes 7987200 | tf_op jit(solution)/shard_map/all_gather | solution.py:86
  8.7 495.6 %all-gather.19.cloned.1.call-start = ((), (), s32[]{:S(2)}) async-start(), calls=%async_computation.10 | async-start | bytes 7987200 | tf_op jit(solution)/shard_map/all_gather | solution.py:86
  9.4 620.1 %all-gather.37.cloned.1.call-start = ((), (), s32[]{:S(2)}) async-start(), calls=%async_computation.26 | async-start | bytes 27033600 | tf_op jit(solution)/shard_map/all_gather | solution.py:86
  10.0 836.0 %all-gather.35.cloned.1.call-start = ((), (), s32[]{:S(2)}) async-start(), calls=%async_computation.25 | async-start | bytes 27033600 | tf_op jit(solution)/shard_map/all_gather | solution.py:86
  10.6 1051.8 %all-gather.33.cloned.1.call-start = ((), (), s32[]{:S(2)}) async-start(), calls=%async_computation.24 | async-start | bytes 27033600 | tf_op jit(solution)/shard_map/all_gather | solution.py:86
  11.2 1101.6 %all-gather.25.cloned.1.call-start = ((), (), s32[]{:S(2)}) async-start(), calls=%async_computation.13 | async-start | bytes 3481600 | tf_op jit(solution)/shard_map/all_gather | solution.py:30
  11.6 29.9 copy-start.135
  11.6 245.1 %copy-start.112 = (f32[1600]{0:T(1024)S(1)}, f32[1600]{0:T(1024)}, u32[]{:S(2)}) copy-start(f32[1600]{0:T(1024)} %param.48) | copy-start | bytes 19204
  12.4 256.2 %copy-start.146 = (f32[128]{0:T(128)}, f32[128]{0:T(128)S(1)}, u32[]{:S(2)}) copy-start(f32[128]{0:T(128)S(1)} %get-tuple-element.1369) | copy-start | bytes 1540
  42.2 214.5 %copy-start.167 = (s32[128]{0:T(128)}, s32[128]{0:T(128)S(1)}, u32[]{:S(2)}) copy-start(s32[128]{0:T(128)S(1)} %get-tuple-element.1292) | copy-start | bytes 1540
  270.4 11.0 collective-permute-start.8
  366.5 791.5 %all-gather.23.cloned.1.call-start = ((), (), s32[]{:S(2)}) async-start(), calls=%async_computation.12 | async-start | bytes 3481600 | tf_op jit(solution)/shard_map/all_gather | solution.py:30
  377.3 30.1 copy-start.10
  377.3 30.1 copy-start.147
  379.0 906.3 %all-gather.27.cloned.1.call-start = ((), (), s32[]{:S(2)}) async-start(), calls=%async_computation.14 | async-start | bytes 15360000 | tf_op jit(solution)/shard_map/all_gather | solution.py:86
  424.5 49.1 %collective-permute-start.7 = (bf16[2,128,320]{1,2,0:T(8,128)(2,1)}, bf16[2,128,320]{1,2,0:T(8,128)(2,1)}, u32[]{:S(2)}, u32[]{:S(2)}) collective-permute-start(bf16[2,128,320]{1,2,0:T(8,128)(2,1)} %pad_maximum_fusion.13), channel_id=1, source_target_pairs={{0,2},{2,4},{4,6},{6,8},{8,10},{10,12},{12,14},{14,16},{16,18},{18... | collective-permute-start | bytes 491528 | tf_op jit(solution)/shard_map/ppermute | solution.py:23
  426.6 46.0 collective-permute-start.6
  430.5 41.1 collective-permute-start.5
  434.8 27.0 collective-permute-start.1
  438.1 7.5 collective-permute-start
  440.9 1226.3 %all-gather.31.cloned.1.call-start = ((), (), s32[]{:S(2)}) async-start(), calls=%async_computation.16 | async-start | bytes 3481600 | tf_op jit(solution)/shard_map/all_gather | solution.py:30
  442.6 31.9 copy-start.124
  442.6 31.9 copy-start.126
  445.6 18.5 collective-permute-start.2
  461.9 6.1 collective-permute-start.3
  464.2 7.4 collective-permute-start.4
  1251.2 40.5 copy-start.11
  1251.2 40.5 copy-start.152
  1251.2 40.5 copy-start.154
  1251.2 40.5 copy-start.169
  1442.5 224.7 %all-gather.29.cloned.1.call-start = ((), (), s32[]{:S(2)}) async-start(), calls=%async_computation.15 | async-start | bytes 3481600 | tf_op jit(solution)/shard_map/all_gather | solution.py:30
  1455.4 467.9 %reduce-scatter.39.cloned.1.call-start = ((), (), s32[]{:S(2)}) async-start(), calls=%async_computation.19 | async-start | bytes 3194880 | tf_op jit(solution)/shard_map/reduce_scatter | solution.py:92
  1491.1 43.5 copy-start.24
  1493.3 41.3 copy-start.22
  1493.6 18.9 collective-permute-start.9
  1495.1 18.8 collective-permute-start.16
  1496.4 18.8 collective-permute-start.15
  1497.7 19.0 collective-permute-start.14
  1499.0 27.0 collective-permute-start.13
  1512.6 15.6 collective-permute-start.12
  1513.9 15.5 collective-permute-start.11
  1515.2 19.4 collective-permute-start.10
  1536.8 386.5 %reduce-scatter.37.cloned.1.call-start = ((), (), s32[]{:S(2)}) async-start(), calls=%async_computation.18 | async-start | bytes 3194880 | tf_op jit(solution)/shard_map/reduce_scatter | solution.py:92
  1538.8 384.6 %reduce-scatter.41.cloned.1.call-start = ((), (), s32[]{:S(2)}) async-start(), calls=%async_computation.20 | async-start | bytes 15974400 | tf_op jit(solution)/shard_map/reduce_scatter | solution.py:92
  1545.4 378.0 %reduce-scatter.35.cloned.1.call-start = ((), (), s32[]{:S(2)}) async-start(), calls=%async_computation.17 | async-start | bytes 15974400 | tf_op jit(solution)/shard_map/reduce_scatter | solution.py:92
  1556.6 597.5 %reduce-scatter.45.cloned.1.call-start = ((), (), s32[]{:S(2)}) async-start(), calls=%async_computation.23 | async-start | bytes 30720000 | tf_op jit(solution)/shard_map/reduce_scatter | solution.py:92
  1667.1 930.8 %all-reduce.61.cloned.1.call-start = ((), (), s32[]{:S(2)}) async-start(), calls=%async_computation.31 | async-start | bytes 49315840
  1829.1 82.4 %copy-start.176 = (u32[32]{0:T(128)S(1)}, u32[32]{0:T(128)}, u32[]{:S(2)}) copy-start(u32[32]{0:T(128)} %constant.441) | copy-start | bytes 388
  1907.0 5.8 collective-permute-start.21
  1910.2 6.3 collective-permute-start.20
  2154.1 848.5 %reduce-scatter.51.cloned.1.call-start = ((), (), s32[]{:S(2)}) async-start(), calls=%async_computation.29 | async-start | bytes 54951936
  2204.7 1202.9 %reduce-scatter.49.cloned.1.call-start = ((), (), s32[]{:S(2)}) async-start(), calls=%async_computation.28 | async-start | bytes 54951936
  2221.7 1605.3 %reduce-scatter.47.cloned.1.call-start = ((), (), s32[]{:S(2)}) async-start(), calls=%async_computation.27 | async-start | bytes 54951936
  2238.1 2025.9 %reduce-scatter.43.cloned.1.call-start = ((), (), s32[]{:S(2)}) async-start(), calls=%async_computation.21 | async-start | bytes 61440000 | tf_op jit(solution)/shard_map/reduce_scatter | solution.py:92
  2258.7 3.2 collective-permute-start.17
  2279.9 2482.0 %all-reduce.59.cloned.1.call-start = ((), (), s32[]{:S(2)}) async-start(), calls=%async_computation.30 | async-start | bytes 266240 | tf_op jit(solution)/shard_map/psum | solution.py:448
  2314.9 2447.0 %all-reduce.57.cloned.1.call-start = ((), (), s32[]{:S(2)}) async-start(), calls=%async_computation.22 | async-start | bytes 409600 | tf_op jit(solution)/shard_map/psum | solution.py:448
  3792.1 54.8 %copy-start.31 = (f32[104,2752]{1,0:T(8,128)}, f32[104,2752]{1,0:T(8,128)S(1)}, u32[]{:S(2)}) copy-start(f32[104,2752]{1,0:T(8,128)S(1)} %get-tuple-element.1275) | copy-start | bytes 3434500
  3793.1 917.6 %collective-permute-start.24 = (f32[60,2752]{1,0:T(8,128)S(1)}, f32[60,2752]{1,0:T(8,128)}, u32[]{:S(2)}, u32[]{:S(2)}) collective-permute-start(f32[60,2752]{1,0:T(8,128)S(1)} %slice.578), channel_id=1, source_target_pairs={{0,2},{2,4},{4,6},{6,8},{8,10},{10,12},{12,14},{14,16},{16,18},{18... | collective-permute-start | bytes 1981448
  3822.3 904.8 %collective-permute-start.23 = (f32[60,2752]{1,0:T(8,128)}, f32[60,2752]{1,0:T(8,128)}, u32[]{:S(2)}, u32[]{:S(2)}) collective-permute-start(f32[60,2752]{1,0:T(8,128)} %slice.577), channel_id=1, source_target_pairs={{0,2},{2,4},{4,6},{6,8},{8,10},{10,12},{12,14},{14,16},{16,18},{18... | collective-permute-start | bytes 1981448
  4673.3 73.8 %collective-permute-start.18 = (f32[112,3200]{1,0:T(8,128)S(1)}, f32[112,3200]{1,0:T(8,128)}, u32[]{:S(2)}, u32[]{:S(2)}) collective-permute-start(f32[112,3200]{1,0:T(8,128)S(1)} %get-tuple-element.1270), channel_id=1, source_target_pairs={{0,2},{2,4},{4,6},{6,8},{8,10},{10,12},{12,14},{14,16},{16,18},{18... | collective-permute-start | bytes 4300808
  4720.5 15.7 collective-permute-start.22
  4724.7 22.5 collective-permute-start.19
  (167 other events, 932.5 us)
Sparse Core Ops, SparseCore 0:
  9.6 247.0 all-gather.20
  258.2 70.6 all-gather.16
  330.5 80.8 all-gather.18
  412.8 216.6 all-gather.36
  630.9 215.0 all-gather.34
  847.4 215.0 all-gather.32
  1064.7 45.7 all-gather.24
  1113.4 44.6 all-gather.22
  1159.6 125.6 all-gather.26
  1442.6 45.7 all-gather.30
  1491.3 61.1 all-gather.28
  1554.6 33.2 reduce-scatter.38
  1590.1 32.1 reduce-scatter.36
  1624.5 123.6 reduce-scatter.40
  1750.3 154.0 reduce-scatter.34
  1906.6 247.4 reduce-scatter.44
  2160.9 436.9 all-reduce.60
  2600.2 402.3 reduce-scatter.50
  3005.0 402.5 reduce-scatter.48
  3409.8 402.5 reduce-scatter.46
  3814.9 449.0 reduce-scatter.42
  4273.3 179.0 all-reduce.58
  4459.4 144.6 all-reduce.56
where the time goes:
time: 4810 us; the launch traced here: 4780 us
  waiting for transfers between devices  2550 us (53%)
  blocking collectives  922 us (19%)
  local copies, waits for them, and re-layouts  574 us (12%)
  other arithmetic  307 us (6%)
  matrix products  277 us (6%)
  starting transfers between devices  126 us (3%)
    unnamed x34, waiting for transfers between devices  1070 us
    unnamed x3, blocking collectives  851 us
    all_gather x7, waiting for transfers between devices, fetch(): lax.all_gather(for_sending(shards), 'wt', axis=1, tiled=True)  751 us
    reduce_scatter x6, waiting for transfers between devices, reduce_terms(): terms = lax.psum_scatter(terms, 'wt', scatter_dimension=1, tiled=True)  648 us
    unnamed x424, local copies, waits for them, and re-layouts  229 us
    mul x128, local copies, waits for them, and re-layouts, factors(): factor = jnp.exp(size[:, None, :] * decay[None]) * keep[:, None, None]  99.3 us
  transfers between devices with their start and end apart: 48, of which 21 were waited for; matrix products, arithmetic and copies ran while one was open for 38% of the time, Pallas kernels for 0%

commit v1 on v0

v1 whole, which is shorter than its diff:
```python
import jax
import jax.numpy as jnp
from jax import lax
from jax.experimental import pallas as pl
from jax.experimental.pallas import tpu as pltpu
from jax.sharding import PartitionSpec as P

HEAD_SIZE = 64
WINDOW = 1024


epsilon = 1e-06
masked = -1e30
bf16 = jnp.bfloat16
f32 = jnp.float32
LANES = 128
LOG2E = 1.4426950408889634


def passed_along(block, axis, distance):
    devices = range(lax.axis_size(axis))
    route = [(i - distance, i) for i in devices if i - distance in devices]
    return lax.ppermute(block, axis, route)


def from_ahead(block, distance):
    count = lax.axis_size("wt")
    return lax.ppermute(block, "wt", [((i + distance) % count, i) for i in range(count)])


def picked(blocks, index):
    result = blocks[0]
    for place in range(1, len(blocks)):
        result = jnp.where(index == place, blocks[place], result)
    return result


def gather_tokens(rows, axis=0):
    count = lax.axis_size("wt")
    return jnp.concatenate([rows] + [from_ahead(rows, k) for k in range(1, count)], axis=axis)


def swapped(blocks):
    count = len(blocks)
    return [blocks[0]] + [from_ahead(blocks[count - k], k) for k in range(1, count)]


def in_order(received, axis):
    place = lax.axis_index("wt")
    count = len(received)
    return jnp.concatenate([picked(received, (a - place) % count) for a in range(count)], axis=axis)


def cut_evenly(value, axis):
    return jnp.split(value, lax.axis_size("wt"), axis=axis)


def to_own_tokens(value, tokens=0, columns=1):
    return in_order(swapped(cut_evenly(value, tokens)), columns)


def to_own_columns(value, tokens=0, columns=1):
    count = lax.axis_size("wt")
    place = lax.axis_index("wt")
    owners = cut_evenly(value, columns)
    blocks = [picked(owners, (place + k) % count) for k in range(count)]
    return jnp.concatenate(swapped(blocks), axis=tokens)


def summed_tokens(value, tokens=0):
    blocks = cut_evenly(value, tokens)
    received = swapped([blocks[0]] + [b.astype(bf16) for b in blocks[1:]])
    total = received[0]
    for block in received[1:]:
        total = total + block.astype(f32)
    return total


def own_columns_sum(value):
    count = lax.axis_size("wt")
    place = lax.axis_index("wt")
    owners = cut_evenly(value, 1)
    return sum(swapped([picked(owners, (place + k) % count) for k in range(count)]))


def seq_swap(block, bit):
    count = lax.axis_size("seq")
    return lax.ppermute(block, "seq", [(i, i ^ (1 << bit)) for i in range(count)])


def features_first(value):
    count = lax.axis_size("seq")
    return value.T.reshape(count, value.shape[1] // count, value.shape[0])


def reversed_bits(value, bits):
    return sum(((value >> bit) & 1) << (bits - 1 - bit) for bit in range(bits))


def arrange_kernel(place_ref, left_ref, own_ref, across_ref, beside_ref, taken_ref):
    count, group, _ = left_ref.shape
    bits = count.bit_length() - 1
    for r in range(count):
        taken_ref[r * group : (r + 1) * group, :] = left_ref[place_ref[0] ^ reversed_bits(r, bits)].astype(f32)
    quarter = own_ref.shape[0]
    own_ref[...] = taken_ref[:quarter].astype(bf16)
    across_ref[:quarter] = taken_ref[quarter : 2 * quarter].astype(bf16)
    across_ref[quarter:] = taken_ref[3 * quarter :].astype(bf16)
    beside_ref[...] = taken_ref[2 * quarter : 3 * quarter].astype(bf16)


def shared_features(left):
    count, group, tokens = left.shape
    quarter = count * group // 4
    place = lax.axis_index("seq").astype(jnp.int32).reshape(1)
    whole = lambda rows: pl.BlockSpec((rows, tokens), lambda i, place: (0, 0))
    sizes = [quarter, 2 * quarter, quarter]
    own, across, beside = pl.pallas_call(
        arrange_kernel,
        grid_spec=pltpu.PrefetchScalarGridSpec(
            num_scalar_prefetch=1,
            grid=(1,),
            in_specs=[pl.BlockSpec((count, group, tokens), lambda i, place: (0, 0, 0))],
            out_specs=[whole(size) for size in sizes],
            scratch_shapes=[pltpu.VMEM((count * group, tokens), f32)],
        ),
        out_shape=[jax.ShapeDtypeStruct((size, tokens), bf16) for size in sizes],
        compiler_params=pltpu.CompilerParams(vmem_limit_bytes=24 * 2**20),
        cost_estimate=pl.CostEstimate(flops=0, transcendentals=0, bytes_accessed=8 * quarter * tokens * 2),
        name="arrange",
    )(place, left)
    return own, beside, seq_swap(across, 1)


def quarter_kernel(
    own_ref, beside_ref, across_ref, right_ref, right_across_ref, keep_ref, send_ref, left_in, right_in, total, sent, got
):
    quarter, columns = total.shape
    place = lax.axis_index("seq")
    partner = {"seq": place + 1 - 2 * (place % 2)}
    barrier = pltpu.get_barrier_semaphore()
    pl.semaphore_signal(barrier, inc=1, device_id=partner, device_id_type=pl.DeviceIdType.MESH)
    pl.semaphore_wait(barrier, 1)
    moves = [
        (right_ref, right_in.at[0]),
        (right_across_ref, right_in.at[1]),
        (beside_ref, left_in.at[0]),
        (across_ref.at[pl.ds(quarter, quarter)], left_in.at[1]),
    ]
    copies = [
        pltpu.make_async_remote_copy(
            src_ref=source,
            dst_ref=target,
            send_sem=sent.at[i],
            recv_sem=got.at[i],
            device_id=partner,
            device_id_type=pl.DeviceIdType.MESH,
        )
        for i, (source, target) in enumerate(moves)
    ]
    for copy in copies:
        copy.start()
    chunks = [slice(at, min(at + 512, columns)) for at in range(0, columns, 512)]
    for chunk in chunks:
        total[:, chunk] = jnp.dot(
            own_ref[...], right_ref[:, chunk], preferred_element_type=f32
        ) + jnp.dot(across_ref[:quarter], right_across_ref[:, chunk], preferred_element_type=f32)
    for copy in copies:
        copy.wait()
    half = quarter // 2
    for chunk in chunks:
        result = (
            total[:, chunk]
            + jnp.dot(left_in[0], right_in[0, :, chunk], preferred_element_type=f32)
            + jnp.dot(left_in[1], right_in[1, :, chunk], preferred_element_type=f32)
        )
        keep_ref[:, chunk] = result[:half].astype(bf16)
        send_ref[:, chunk] = result[half:].astype(bf16)


def quarter_gradient(left, right, collective):
    rows, tokens = left[0].shape
    columns = right[0].shape[1]
    vmem = pl.BlockSpec(memory_space=pltpu.VMEM)
    return pl.pallas_call(
        quarter_kernel,
        in_specs=[vmem] * 5,
        out_specs=[vmem] * 2,
        out_shape=[jax.ShapeDtypeStruct((rows // 2, columns), bf16)] * 2,
        scratch_shapes=[
            pltpu.VMEM((2, rows, tokens), bf16),
            pltpu.VMEM((2, tokens, columns), bf16),
            pltpu.VMEM((rows, columns), f32),
            pltpu.SemaphoreType.DMA((4,)),
            pltpu.SemaphoreType.DMA((4,)),
        ],
        compiler_params=pltpu.CompilerParams(
            vmem_limit_bytes=40 * 2**20, collective_id=collective, has_side_effects=True
        ),
        cost_estimate=pl.CostEstimate(flops=0, transcendentals=0, bytes_accessed=1 << 20),
        name="gradient",
    )(*left, *right)


def added(keep, received):
    total = keep.astype(f32) + received.astype(f32)
    half = total.shape[0] // 2
    return total[:half].astype(bf16), total[half:].astype(bf16)


class Gradient:
    def __init__(self, left, right, collective):
        self.left, self.right, self.collective = left, (right, seq_swap(right, 1)), collective
        self.bits = lax.axis_size("seq").bit_length() - 1
        self.bit = 2
        self.total = None

    def start(self):
        self.received = seq_swap(self.send, self.bit)
        self.bit += 1

    def finish(self):
        if self.bit == 2:
            self.keep, self.send = quarter_gradient(self.left, self.right, self.collective)
        elif self.bit < self.bits:
            self.keep, self.send = added(self.keep, self.received)
        else:
            self.total = self.keep.astype(f32) + self.received.astype(f32)

    def state(self):
        return (self.keep, self.send) if self.total is None else self.total

    def set_state(self, state):
        if self.total is None:
            self.keep, self.send = state
        else:
            self.total = state


def advance(chain, gradients):
    for gradient in gradients:
        gradient.finish()
    chain, states = lax.optimization_barrier((chain, [g.state() for g in gradients]))
    for gradient, state in zip(gradients, states):
        gradient.set_state(state)
        if gradient.total is None:
            gradient.start()
    return chain


def completed_all(gradients):
    while any(gradient.total is None for gradient in gradients):
        for gradient in gradients:
            gradient.finish()
            if gradient.total is None:
                gradient.start()
    return [gradient.total for gradient in gradients]


def column_chunks(value, chunks):
    width = value.shape[1] // lax.axis_size("wt")
    piece = -(-width // chunks // LANES) * LANES
    owners = cut_evenly(value, 1)
    return [
        to_own_columns(jnp.concatenate([owner[:, at : at + piece] for owner in owners], axis=1))
        for at in range(0, width, piece)
    ]


def completed(gradient):
    while gradient.total is None:
        gradient.finish()
        if gradient.total is None:
            gradient.start()
    return gradient.total


def lane_blocks(inner):
    blocks = inner // LANES
    return next(n for n in (5, 4, 3, 2, 1) if blocks % n == 0)

def cut_lanes(value):
    return [value[:, i * LANES : (i + 1) * LANES] for i in range(value.shape[1] // LANES)]

def spread(ref, tile, row, states):
    values = ref[tile, row : row + 1, :]
    return [jnp.broadcast_to(part, (states, LANES)) for part in cut_lanes(values)]


def advanced(size_ref, inject_ref, entry_ref, decay, tile, row, state):
    states = entry_ref.shape[1]
    into = entry_ref[tile * 8 + row]
    return tuple(
        jnp.exp2(size * rate) * old + inject * into
        for size, inject, rate, old in zip(
            spread(size_ref, tile, row, states), spread(inject_ref, tile, row, states), decay, state
        )
    )


def no_state(decay_ref):
    return tuple(jnp.zeros_like(part) for part in cut_lanes(decay_ref[...]))


def state_kernel(size_ref, inject_ref, entry_ref, decay_ref, last_ref):
    decay = cut_lanes(decay_ref[...])

    def tokens(tile, state):
        for row in range(8):
            state = advanced(size_ref, inject_ref, entry_ref, decay, tile, row, state)
        return state

    state = lax.fori_loop(0, size_ref.shape[0], tokens, no_state(decay_ref))
    last_ref[...] = jnp.concatenate(state, axis=1)


def output_kernel(size_ref, inject_ref, entry_ref, read_ref, decay_ref, begin_ref, out_ref):
    decay = cut_lanes(decay_ref[...])

    def tokens(tile, state):
        for row in range(8):
            state = advanced(size_ref, inject_ref, entry_ref, decay, tile, row, state)
            output = read_ref[tile * 8 + row]
            for i, part in enumerate(state):
                out_ref[tile, row : row + 1, i * LANES : (i + 1) * LANES] = jnp.sum(
                    output * part, axis=0, keepdims=True
                )
        return state

    lax.fori_loop(0, size_ref.shape[0], tokens, tuple(cut_lanes(begin_ref[...])))


def adjoint_kernel(size_ref, back_ref, read_ref, decay_ref, first_ref):
    states = decay_ref.shape[0]
    decay = cut_lanes(decay_ref[...])
    tiles = size_ref.shape[0]

    def tokens(turn, carry):
        tile = tiles - 1 - turn
        for row in reversed(range(8)):
            output = read_ref[tile * 8 + row]
            carry = tuple(
                jnp.exp2(size * rate) * (output * back + old)
                for size, back, rate, old in zip(
                    spread(size_ref, tile, row, states), spread(back_ref, tile, row, states), decay, carry
                )
            )
        return carry

    carry = lax.fori_loop(0, tiles, tokens, no_state(decay_ref))
    first_ref[...] = jnp.concatenate(carry, axis=1)


def gradient_kernel(
    size_ref,
    inject_ref,
    back_ref,
    entry_ref,
    read_ref,
    decay_ref,
    rate_ref,
    begin_ref,
    end_ref,
    through_ref,
    sized_ref,
    entry_back_ref,
    read_back_ref,
    decay_back_ref,
    prior_ref,
):
    states = decay_ref.shape[0]
    decay = cut_lanes(decay_ref[...])
    tiles = size_ref.shape[0]

    @pl.when(pl.program_id(0) == 0)
    def _():
        entry_back_ref[...] = jnp.zeros_like(entry_back_ref)
        read_back_ref[...] = jnp.zeros_like(read_back_ref)

    def forward(tile, state):
        for row in range(8):
            for i, part in enumerate(state):
                prior_ref[tile * 8 + row, :, i * LANES : (i + 1) * LANES] = part
            state = advanced(size_ref, inject_ref, entry_ref, decay, tile, row, state)
        return state

    last = lax.fori_loop(0, tiles, forward, tuple(cut_lanes(begin_ref[...])))

    def backward(turn, carry):
        tile = tiles - 1 - turn
        arriving, current, total = carry
        for row in reversed(range(8)):
            t = tile * 8 + row
            into = entry_ref[t]
            output = read_ref[t]
            sizes = spread(size_ref, tile, row, states)
            injects = spread(inject_ref, tile, row, states)
            backs = spread(back_ref, tile, row, states)
            entry_back = entry_back_ref[t]
            read_back = read_back_ref[t]
            new_arriving, new_current, new_total = [], [], []
            for k in range(len(decay)):
                lanes = slice(k * LANES, (k + 1) * LANES)
                prior = prior_ref[t, :, lanes]
                adjoint = output * backs[k] + arriving[k]
                leaving = jnp.exp2(sizes[k] * decay[k]) * adjoint
                weighted = leaving * prior
                through_ref[tile, row : row + 1, lanes] = jnp.sum(adjoint * into, axis=0, keepdims=True)
                sized_ref[tile, row : row + 1, lanes] = jnp.sum(
                    weighted * rate_ref[:, lanes], axis=0, keepdims=True
                )
                entry_back = entry_back + adjoint * injects[k]
                read_back = read_back + current[k] * backs[k]
                new_total.append(total[k] + weighted * sizes[k])
                new_arriving.append(leaving)
                new_current.append(prior)
            entry_back_ref[t] = entry_back
            read_back_ref[t] = read_back
            arriving, current, total = new_arriving, new_current, new_total
        return tuple(arriving), tuple(current), tuple(total)

    arriving = tuple(cut_lanes(end_ref[...]))
    _, _, total = lax.fori_loop(0, tiles, backward, (arriving, last, no_state(decay_ref)))
    decay_back_ref[...] = jnp.concatenate(total, axis=1)


def scan_call(body, name, token_args, wide_args, state_args, outs, scratch=False, flops=0):
    rows, inner = token_args[0].shape
    states = state_args[0].shape[0]
    width = lane_blocks(inner) * LANES
    token = pl.BlockSpec((rows // 8, 8, width), lambda i: (0, 0, i))
    wide = pl.BlockSpec((rows, states, LANES), lambda i: (0, 0, 0))
    state = pl.BlockSpec((states, width), lambda i: (0, i))
    kinds = {
        "token": (token, jax.ShapeDtypeStruct((rows // 8, 8, inner), f32)),
        "wide": (wide, jax.ShapeDtypeStruct((rows, states, LANES), f32)),
        "state": (state, jax.ShapeDtypeStruct((states, inner), f32)),
    }
    size = rows * states * inner
    results = pl.pallas_call(
        body,
        grid=(inner // width,),
        in_specs=[token] * len(token_args) + [wide] * len(wide_args) + [state] * len(state_args),
        out_specs=[kinds[k][0] for k in outs],
        out_shape=[kinds[k][1] for k in outs],
        scratch_shapes=[pltpu.VMEM((rows, states, width), f32)] if scratch else [],
        compiler_params=pltpu.CompilerParams(vmem_limit_bytes=40 * 2**20),
        cost_estimate=pl.CostEstimate(flops=0, transcendentals=0, bytes_accessed=flops << 18),
        name=name,
    )(*[arg.reshape(rows // 8, 8, inner) for arg in token_args], *wide_args, *state_args)
    return [r.reshape(rows, inner) if k == "token" else r for k, r in zip(outs, results)]


def entering(total, part, rate, reverse):
    count = lax.axis_size("seq")
    sign = -1 if reverse else 1
    packed = jnp.concatenate([total[None], part], axis=0)
    near = passed_along(packed, "seq", sign)
    far = passed_along(packed, "seq", 2 * sign)
    total, part = near[0] + far[0], jnp.exp2(near[0] * rate) * far[1:] + near[1:]
    distance = 2
    while distance < count:
        received = passed_along(jnp.concatenate([total[None], part], axis=0), "seq", distance * sign)
        part = jnp.exp2(total * rate) * received[1:] + part
        total = total + received[0]
        distance *= 2
    return part


def summed_everywhere(parts):
    sizes = [part.size for part in parts]
    packed = jnp.concatenate([part.reshape(-1) for part in parts])
    packed = jnp.pad(packed, (0, -packed.size % 1024)).reshape(-1, 128)
    for axis in ("seq", "wt"):
        count = lax.axis_size(axis)
        bit = 1
        while bit < count:
            packed = packed + lax.ppermute(packed, axis, [(i, i ^ bit) for i in range(count)])
            bit *= 2
    packed = packed.reshape(-1)
    result, begin = [], 0
    for part, size in zip(parts, sizes):
        result.append(packed[begin : begin + size].reshape(part.shape))
        begin += size
    return result


def product(left, right):
    return jnp.dot(left, right, preferred_element_type=jnp.float32)


def left_product(left, right):
    return lax.dot_general(
        left, right, (((0,), (0,)), ((), ())), preferred_element_type=jnp.float32
    )


def right_product(left, right):
    return lax.dot_general(
        left, right, (((1,), (1,)), ((), ())), preferred_element_type=jnp.float32
    )


def transposed_dot(left, right):
    return lax.dot_general(left, right, (((0,), (0,)), ((), ())), preferred_element_type=f32)


def heads_beside(value):
    heads = value.shape[0] // HEAD_SIZE
    return jnp.concatenate(
        [value[h * HEAD_SIZE : (h + 1) * HEAD_SIZE] for h in range(heads)], axis=1
    )


def store_heads(ref, value):
    rows = ref.shape[1]
    for h in range(ref.shape[0] // HEAD_SIZE):
        ref[h * HEAD_SIZE : (h + 1) * HEAD_SIZE, :] = value[:, h * rows : (h + 1) * rows].astype(ref.dtype)


def chance_table(query, keys, bias):
    heads = query.shape[1] // bias.shape[1]
    scores = transposed_dot(keys, query) + jnp.concatenate([bias] * heads, axis=1)
    raised = jnp.exp(scores - jnp.max(scores, axis=0, keepdims=True))
    return raised * (1.0 / jnp.sum(raised, axis=0, keepdims=True))


def attend_kernel(query_ref, keys_ref, values_ref, bias_ref, out_ref):
    query = heads_beside(query_ref[...]) * bf16(0.125)
    chances = chance_table(query, keys_ref[...], bias_ref[...]).astype(bf16)
    store_heads(out_ref, jnp.dot(values_ref[...], chances, preferred_element_type=f32))


def attend_back_kernel(query_ref, keys_ref, values_ref, back_ref, bias_ref, query_back_ref, keys_back_ref, values_back_ref):
    query = heads_beside(query_ref[...]) * bf16(0.125)
    back = heads_beside(back_ref[...])
    weights = chance_table(query, keys_ref[...], bias_ref[...])
    values_back_ref[...] = right_product(back, weights.astype(bf16))
    delta = transposed_dot(values_ref[...], back)
    weighted = weights * delta
    scores_back = (weighted - weights * jnp.sum(weighted, axis=0, keepdims=True)).astype(bf16)
    store_heads(query_back_ref, jnp.dot(keys_ref[...], scores_back, preferred_element_type=f32) * 0.125)
    keys_back_ref[...] = right_product(query, scores_back)


def attention_call(body, name, wide, near, bias, outs, flops):
    span, rows = bias.shape
    key_heads = near[0].shape[0] // HEAD_SIZE
    width = wide[0].shape[0] // key_heads
    wide_spec = pl.BlockSpec((width, rows), lambda k: (k, 0))
    near_spec = pl.BlockSpec((HEAD_SIZE, span), lambda k: (k, 0))
    kinds = {
        "wide": (wide_spec, jax.ShapeDtypeStruct(wide[0].shape, bf16)),
        "near": (near_spec, jax.ShapeDtypeStruct(near[0].shape, f32)),
    }
    size = key_heads * span * rows * (width // HEAD_SIZE)
    return pl.pallas_call(
        body,
        grid=(key_heads,),
        in_specs=[wide_spec] + [near_spec] * 2 + [wide_spec] * (len(wide) - 1)
        + [pl.BlockSpec((span, rows), lambda k: (0, 0))],
        out_specs=[kinds[k][0] for k in outs],
        out_shape=[kinds[k][1] for k in outs],
        compiler_params=pltpu.CompilerParams(vmem_limit_bytes=56 * 2**20),
        cost_estimate=pl.CostEstimate(flops=0, transcendentals=0, bytes_accessed=flops << 19),
        name=name,
    )(wide[0], *near, *wide[1:], bias)


def outer_product(left, right):
    return lax.dot_general(left, right, (((0,), (1,)), ((), ())), preferred_element_type=f32)


def inverse_norm(value):
    return lax.rsqrt(jnp.mean(value * value, axis=-1, keepdims=True) + epsilon)


def norm_back(value, scale, incoming):
    return scale * incoming - scale * scale * scale * value * jnp.mean(
        incoming * value, axis=-1, keepdims=True
    )


def silu_slope(value):
    sigma = jax.nn.sigmoid(value)
    return sigma * (1.0 + value * (1.0 - sigma))


def gather_columns(own):
    count = lax.axis_size("wt")
    turned = own.T
    return in_order([turned] + [from_ahead(turned, k) for k in range(1, count)], 0)


def feed_block(second_rows, back_rows, gate_cols, up_cols, down_cols):
    gate_raw = product(second_rows, gate_cols)
    up_raw = product(second_rows, up_cols)
    sigma_gate = jax.nn.sigmoid(gate_raw)
    activated = (gate_raw * sigma_gate * up_raw).astype(jnp.bfloat16)
    feed_out = right_product(activated, down_cols)
    delta_act = product(back_rows, down_cols)
    delta_gate = (delta_act * up_raw * silu_slope(gate_raw)).astype(jnp.bfloat16)
    delta_up = (delta_act * gate_raw * sigma_gate).astype(jnp.bfloat16)
    delta_second = right_product(delta_gate, gate_cols) + right_product(delta_up, up_cols)
    return (feed_out, delta_second, activated, delta_gate, delta_up)


def per_device(
    tokens,
    segment_ids,
    cotangent,
    norm_gain,
    query_weight,
    key_weight,
    value_weight,
    head_weight,
    input_weight,
    filter_weight,
    filter_bias,
    select_weight,
    step_weight,
    step_offset,
    decay_log,
    direct_skip_weight,
    mixer_weight,
    attend_gain,
    state_gain,
    feed_gain,
    gate_weight,
    up_weight,
    down_weight,
):
    rows = tokens.shape[1]
    model = tokens.shape[2]
    inner = filter_weight.shape[1]
    kernel = filter_weight.shape[0]
    states = decay_log.shape[0]
    start = lax.axis_index("seq") * rows
    whole_segment = segment_ids[0]
    padded_segment = jnp.concatenate([jnp.full((WINDOW,), -1, jnp.int32), whole_segment])
    segment = lax.dynamic_slice_in_dim(whole_segment, start, rows)
    inputs = tokens[0].astype(jnp.float32)
    upstream = cotangent[0].astype(jnp.float32)
    both_tokens = gather_tokens(tokens[0])
    select_full = gather_columns(select_weight)
    step_full = gather_columns(step_weight)
    both_back = gather_tokens(cotangent[0])
    rank = step_full.shape[0]
    first_scale = inverse_norm(inputs)
    both_inputs = both_tokens.astype(jnp.float32)
    both_normed = (both_inputs * inverse_norm(both_inputs) * norm_gain).astype(jnp.bfloat16)
    normed_shared = shared_features(features_first(both_normed))
    back_shared = shared_features(features_first(both_back))
    pairs = jnp.stack(
        [outer_product(weight, both_normed).astype(bf16) for weight in (key_weight, value_weight)]
    )
    pairs = to_own_tokens(pairs, 2, 1)
    entered = to_own_tokens(product(both_normed, input_weight).astype(jnp.bfloat16))
    query = to_own_tokens(outer_product(query_weight, both_normed).astype(jnp.bfloat16), 1, 0)
    hops = -(-WINDOW // (4 * rows))
    near = jnp.concatenate(
        [pairs] + [passed_along(pairs, "seq", 4 * hop) for hop in range(1, hops + 1)], axis=2
    )
    for bit in (1, 0):
        near = jnp.concatenate([near, seq_swap(near, bit)], axis=2)
    seq_place = lax.axis_index("seq")
    block_places = jnp.stack(
        [(seq_place ^ other) - 4 * hop for other in (0, 2, 1, 3) for hop in range(hops + 1)]
    )
    near_place = (block_places[:, None] * rows + jnp.arange(rows, dtype=jnp.int32)[None, :]).reshape(-1)
    near_segment = jnp.where(
        block_places[:, None] >= 0,
        jnp.take(whole_segment.reshape(-1, rows), jnp.maximum(block_places, 0), axis=0),
        -1,
    ).reshape(-1)
    distance = start + jnp.arange(rows, dtype=jnp.int32)[None, :] - near_place[:, None]
    allowed = (distance >= 0) & (distance < WINDOW) & (segment[None, :] == near_segment[:, None])
    bias = jnp.where(allowed, 0.0, masked)
    (attended,) = attention_call(attend_kernel, "attend", [query], [near[0], near[1]], bias, ["wide"], 2)
    both_attended = gather_tokens(attended, 1)
    attended_shared = shared_features(
        both_attended.reshape(lax.axis_size("seq"), -1, both_attended.shape[1])
    )
    head_out = to_own_tokens(left_product(both_attended, head_weight).astype(bf16)).astype(f32)
    inner_rows = entered[:, :inner]
    gate_input = entered[:, inner:].astype(jnp.float32)
    before = passed_along(inner_rows[rows - kernel + 1 :], "seq", 1)
    extended = jnp.concatenate([before, inner_rows], axis=0).astype(jnp.float32)
    edge_segment = lax.dynamic_slice_in_dim(
        padded_segment, start + WINDOW - kernel + 1, rows + kernel - 1
    )
    taps = []
    sames = []
    filtered = filter_bias + jnp.zeros((rows, inner), jnp.float32)
    for tap in range(kernel):
        begin = kernel - 1 - tap
        same = (edge_segment[begin : begin + rows] == segment).astype(jnp.float32)
        kept_rows = extended[begin : begin + rows] * same[:, None]
        taps.append(kept_rows)
        sames.append(same)
        filtered = filtered + filter_weight[tap] * kept_rows
    smoothed = (filtered * jax.nn.sigmoid(filtered)).astype(jnp.bfloat16)
    scan_input_rows = smoothed.astype(jnp.float32)
    smoothed_shared = shared_features(features_first(smoothed))
    projected = right_product(smoothed, select_full)
    step_low = projected[:, :rank].astype(jnp.bfloat16)
    entry = projected[:, rank : rank + states]
    read = projected[:, rank + states :]
    unsquashed_step = product(step_low, step_full) + step_offset
    step = jnp.log1p(jnp.exp(unsquashed_step))
    previous = lax.dynamic_slice_in_dim(padded_segment, start + WINDOW - 1, rows)
    hold = (previous == segment).astype(jnp.float32)
    decay = -jnp.exp(decay_log)
    rate = decay * LOG2E
    size = jnp.where(hold[:, None] == 0.0, 1e30, step)
    inject = step * scan_input_rows
    entry_wide = jnp.broadcast_to(entry[:, :, None], (rows, states, LANES))
    read_wide = jnp.broadcast_to(read[:, :, None], (rows, states, LANES))
    total = jnp.sum(size, axis=0)
    (last,) = scan_call(state_kernel, "scan_state", [size, inject], [entry_wide], [rate], ["state"], flops=4)
    begin_state = entering(total, last, rate, False)
    (scanned,) = scan_call(
        output_kernel, "scan_output", [size, inject], [entry_wide, read_wide], [rate, begin_state], ["token"], flops=6
    )
    scan_result_rows = scanned + direct_skip_weight * scan_input_rows
    sigma_input = jax.nn.sigmoid(gate_input)
    silu_input = gate_input * sigma_input
    gated = (scan_result_rows * silu_input).astype(jnp.bfloat16)
    both_gated = gather_tokens(gated)
    gated_shared = shared_features(features_first(both_gated))
    branch = to_own_tokens(product(both_gated, mixer_weight).astype(jnp.bfloat16)).astype(f32)
    head_scale = inverse_norm(head_out)
    branch_scale = inverse_norm(branch)
    hidden = inputs + 0.5 * (
        head_out * head_scale * attend_gain + branch * branch_scale * state_gain
    )
    second_scale = inverse_norm(hidden)
    second = (hidden * second_scale * feed_gain).astype(jnp.bfloat16)
    both_second = gather_tokens(second)
    feed_part, second_part, activated, feed_gate, feed_up = feed_block(
        both_second, both_back, gate_weight, up_weight, down_weight
    )
    second_shared = shared_features(features_first(both_second))
    down = Gradient(back_shared, activated, 1)
    gate = Gradient(second_shared, feed_gate, 1)
    up = Gradient(second_shared, feed_up, 1)
    delta_second = summed_tokens(second_part)
    feed_out = summed_tokens(feed_part)
    result = (hidden + feed_out).astype(jnp.bfloat16)
    feed_sum = jnp.sum(delta_second * hidden * second_scale, axis=0)
    delta_hidden = upstream + norm_back(hidden, second_scale, delta_second * feed_gain)
    half = 0.5 * delta_hidden
    attend_sum = jnp.sum(half * head_out * head_scale, axis=0)
    state_sum = jnp.sum(half * branch * branch_scale, axis=0)
    delta_head = norm_back(head_out, head_scale, half * attend_gain).astype(jnp.bfloat16)
    delta_branch = norm_back(branch, branch_scale, half * state_gain).astype(jnp.bfloat16)
    delta_head, delta_branch = advance((delta_head, delta_branch), [down])
    both_delta_head = to_own_columns(delta_head)
    both_delta_branch = to_own_columns(delta_branch)
    head = Gradient(attended_shared, both_delta_head, 2)
    mixer = Gradient(gated_shared, both_delta_branch, 3)
    delta_gated = summed_tokens(right_product(both_delta_branch, mixer_weight))
    delta_attended = summed_tokens(right_product(head_weight, both_delta_head), 1).astype(bf16)
    delta_query, key_near, value_near = attention_call(
        attend_back_kernel, "attend_back", [query, delta_attended], [near[0], near[1]], bias, ["wide", "near", "near"], 5
    )
    delta_near = jnp.stack([key_near, value_near])
    for bit in (0, 1):
        half = delta_near.shape[2] // 2
        received = seq_swap(delta_near[:, :, half:].astype(bf16), bit)
        delta_near = delta_near[:, :, :half] + received.astype(f32)
    delta_pairs = delta_near[:, :, :rows]
    for hop in range(1, hops + 1):
        piece = delta_near[:, :, hop * rows : (hop + 1) * rows].astype(bf16)
        delta_pairs = delta_pairs + passed_along(piece, "seq", -4 * hop).astype(f32)
    delta_pairs = delta_pairs.astype(jnp.bfloat16)
    both_qkv = jnp.concatenate(
        [
            to_own_columns(delta_query, 1, 0),
            to_own_columns(delta_pairs[0], 1, 0),
            to_own_columns(delta_pairs[1], 1, 0),
        ],
        axis=0,
    ).T
    qkv_sums = Gradient(normed_shared, both_qkv, 4)
    delta_scan_output = delta_gated * silu_input
    delta_gate = (delta_gated * scan_result_rows * silu_slope(gate_input)).astype(jnp.bfloat16)
    skip_sum = jnp.sum(delta_scan_output * scan_input_rows, axis=0)
    (first,) = scan_call(adjoint_kernel, "scan_adjoint", [size, delta_scan_output], [read_wide], [rate], ["state"], flops=4)
    end_state = entering(total, first, rate, True)
    end_state = advance(end_state, [down, gate, up, head, mixer])
    through, sized, entry_back, read_back, decay_acc = scan_call(
        gradient_kernel,
        "scan_gradient",
        [size, inject, delta_scan_output],
        [entry_wide, read_wide],
        [rate, decay, begin_state, end_state],
        ["token", "token", "wide", "wide", "state"],
        scratch=True,
        flops=20,
    )
    through, sized, decay_acc = advance((through, sized, decay_acc), [down, gate, up, head, mixer])
    decay_sum = decay_acc * decay
    delta_scan_input = delta_scan_output * direct_skip_weight + through * step
    delta_unsquashed_step = (sized + through * scan_input_rows) * jax.nn.sigmoid(unsquashed_step)
    offset_sum = jnp.sum(delta_unsquashed_step, axis=0)
    raw_low = delta_unsquashed_step.astype(jnp.bfloat16)
    delta_lowrank_step = right_product(raw_low, step_full)
    delta_projected = jnp.concatenate(
        [
            delta_lowrank_step,
            jnp.sum(entry_back, axis=-1),
            jnp.sum(read_back, axis=-1),
        ],
        axis=1,
    ).astype(jnp.bfloat16)
    delta_scan_input = delta_scan_input + product(delta_projected, select_full)
    delta_filtered = delta_scan_input * silu_slope(filtered)
    bias_sum = jnp.sum(delta_filtered, axis=0)
    filter_sums = jnp.stack([jnp.sum(delta_filtered * kept_rows, axis=0) for kept_rows in taps])
    shares = [delta_filtered * filter_weight[tap] * sames[tap][:, None] for tap in range(kernel)]
    leaving = jnp.stack(
        [
            sum(shares[tap][tap - back] for tap in range(back, kernel))
            for back in range(kernel - 1, 0, -1)
        ]
    )
    arrived = passed_along(leaving.astype(jnp.bfloat16), "seq", -1).astype(jnp.float32)
    delta_inner = sum(jnp.pad(share[tap:], ((0, tap), (0, 0))) for tap, share in enumerate(shares))
    delta_inner = delta_inner + jnp.pad(arrived, ((rows - kernel + 1, 0), (0, 0)))
    delta_entered = jnp.concatenate([delta_inner.astype(jnp.bfloat16), delta_gate], axis=1)
    delta_entered = advance(delta_entered, [up, head, mixer])
    both_entered = column_chunks(delta_entered, 4)
    widths = (query_weight.shape[1], key_weight.shape[1], value_weight.shape[1])
    cuts = (0, widths[0], widths[0] + widths[1], sum(widths))
    delta_normed = right_product(jnp.concatenate(both_entered, axis=1), input_weight)
    for place, weight in enumerate((query_weight, key_weight, value_weight)):
        delta_normed = delta_normed + right_product(both_qkv[:, cuts[place] : cuts[place + 1]], weight)
    delta_normed = summed_tokens(delta_normed)
    norm_sum = jnp.sum(delta_normed * inputs * first_scale, axis=0)
    delta_tokens = delta_hidden + norm_back(inputs, first_scale, delta_normed * norm_gain)
    select_sums = Gradient(smoothed_shared, delta_projected, 5)
    step_sums = Gradient(shared_features(features_first(raw_low)), step_low, 6)
    input_sums = [
        Gradient(normed_shared, part, 7 if part.shape == both_entered[0].shape else 8) for part in both_entered
    ]
    qkv_gradient = completed(qkv_sums)
    query_gradient, key_gradient, value_gradient = (
        qkv_gradient[:, cuts[place] : cuts[place + 1]] for place in range(3)
    )
    select_gradient = own_columns_sum(completed(select_sums))
    step_gradient = own_columns_sum(completed(step_sums))
    input_gradient = jnp.concatenate(completed_all(input_sums), axis=1)
    down_gradient, gate_gradient, up_gradient, head_gradient, mixer_gradient = (
        completed(gradient) for gradient in (down, gate, up, head, mixer)
    )
    feed_total, attend_total, state_total, skip_total, decay_total, offset_total = lax.psum(
        (feed_sum, attend_sum, state_sum, skip_sum, decay_sum, offset_sum), ("seq", "wt")
    )
    norm_total, filter_total, bias_total = summed_everywhere((norm_sum, filter_sums, bias_sum))
    return (
        result[None],
        delta_tokens[None],
        norm_total,
        query_gradient,
        key_gradient,
        value_gradient,
        head_gradient,
        input_gradient,
        filter_total,
        bias_total,
        select_gradient,
        step_gradient,
        offset_total,
        decay_total,
        skip_total,
        mixer_gradient,
        attend_total,
        state_total,
        feed_total,
        gate_gradient,
        up_gradient,
        down_gradient,
    )


def solution(mesh):
    placed = (
        P("wt", "seq", None),
        P("wt", None),
        P("wt", "seq", None),
        P(),
        P(None, "wt"),
        P(None, "wt"),
        P(None, "wt"),
        P(None, "wt"),
        P(None, "wt"),
        P(),
        P(),
        P(None, "wt"),
        P(None, "wt"),
        P(),
        P(),
        P(),
        P(None, "wt"),
        P(),
        P(),
        P(),
        P(None, "wt"),
        P(None, "wt"),
        P(None, "wt"),
    )
    return jax.shard_map(
        per_device,
        mesh=mesh,
        in_specs=placed,
        out_specs=(
            P("wt", "seq", None),
            P("wt", "seq", None),
            P(),
            P("seq", "wt"),
            P("seq", "wt"),
            P("seq", "wt"),
            P("seq", "wt"),
            P("seq", "wt"),
            P(),
            P(),
            P("seq", "wt"),
            P("seq", "wt"),
            P(),
            P(),
            P(),
            P("seq", "wt"),
            P(),
            P(),
            P(),
            P("seq", "wt"),
            P("seq", "wt"),
            P("seq", "wt"),
        ),
        check_vma=False,
    )
```

time: 4810 us -> 1070 us (0.22)
  waiting for transfers between devices: 2550 us -> 332 us
  blocking collectives: 922 us -> 40.9 us
  local copies, waits for them, and re-layouts: 574 us -> 160 us
  matrix products: 277 us -> 85.8 us
  other arithmetic: 307 us -> 116 us
  Pallas kernels: 0 us -> 158 us
    unnamed x34 -> x1, waiting for transfers between devices: 1070 us -> 0.02 us
    unnamed x3 -> x0, blocking collectives: 851 us -> none
    all_gather x11 -> x0, waiting for transfers between devices: 796 us -> none  [the longest x7 751 us: fetch(): lax.all_gather(for_sending(shards), 'wt', axis=1, tiled=True)]
    reduce_scatter x6 -> x0, waiting for transfers between devices: 648 us -> none  [reduce_terms(): terms = lax.psum_scatter(terms, 'wt', scatter_dimension=1, tiled=True)]
    ppermute x0 -> x80, waiting for transfers between devices: none -> 291 us  [the longest x47 197 us: seq_swap(): return lax.ppermute(block, 'seq', [(i, i ^ 1 << bit) for i in range(count)])]
    mul x240 -> x0, local copies, waits for them, and re-layouts: 163 us -> none  [the longest x128 99.3 us: factors(): factor = jnp.exp(size[:, None, :] * decay[None]) * keep[:, None, None]]
    unnamed x424 -> x466, local copies, waits for them, and re-layouts: 229 us -> 68.2 us
    pallas_call x0 -> x25, Pallas kernels: none -> 158 us  [the longest x12 70 us: quarter_gradient(): pl.pallas_call(quarter_kernel, in_specs=[vmem] * 5, out_specs=[vmem] * 2,...]
  transfers between devices with their start and end apart: 48 -> 97, of which waited for: 21 -> 39; matrix products, arithmetic and copies ran while one was open for 38% -> 30% of each run, Pallas kernels for 0% -> 15%
where the time goes in v1:
time: 1070 us; the launch traced here: 1060 us
  waiting for transfers between devices  332 us (31%)
  local copies, waits for them, and re-layouts  160 us (15%)
  Pallas kernels  158 us (15%)
  starting transfers between devices  146 us (14%)
  other arithmetic  116 us (11%)
  matrix products  85.8 us (8%)
  blocking collectives  40.9 us (4%)
  between operations  17.4 us (2%)
    ppermute x47, waiting for transfers between devices, seq_swap(): return lax.ppermute(block, 'seq', [(i, i ^ 1 << bit) for i in range(count)])  197 us
    ppermute x28, waiting for transfers between devices, from_ahead(): lax.ppermute(block, 'wt', [((i + distance) % count, i) for i in range(cou...  74.6 us
    pallas_call x12, Pallas kernels, quarter_gradient(): pl.pallas_call(quarter_kernel, in_specs=[vmem] * 5, out_specs=[vmem] * 2,...  70 us
    ppermute x47, starting transfers between devices, seq_swap(): return lax.ppermute(block, 'seq', [(i, i ^ 1 << bit) for i in range(count)])  69 us
    unnamed x466, local copies, waits for them, and re-layouts  68.2 us
    pallas_call x4, Pallas kernels, scan_call(): pl.pallas_call(body, grid=(inner // width,), in_specs=[token] * len(token...  51.2 us
    dot_general x7, matrix products, product(): return jnp.dot(left, right, preferred_element_type=jnp.float32)  44 us
    psum x1, blocking collectives, per_device(): lax.psum((feed_sum, attend_sum, state_sum, skip_sum, decay_sum, offset_su...  40.9 us
  transfers between devices with their start and end apart: 97, of which 39 were waited for; matrix products, arithmetic and copies ran while one was open for 30% of the time, Pallas kernels for 15%

profile of v1, /device:TPU:0, one launch (start us, length us, event | category | flops | bytes accessed | tf_op | source)
XLA Modules:
  0.0 1056.7 jit_solution(17488157355098548869)
XLA Ops:
  20.7 20.2 %collective-permute-done.12 = bf16[50,3200]{1,0:T(8,128)(2,1)} collective-permute-done((bf16[50,3200]{1,0:T(8,128)(2,1)}, bf16[50,3200]{1,0:T(8,128)(2,1)}, u32[]{:S(2)}, u32[]{:S(2)}) %collective-permute-start.12) | collective-permute-done | bytes 320032 | tf_op jit(solution)/shard_map/ppermute | solution.py:28
  53.2 7.6 convolution_convert_fusion
  88.8 4.1 collective-permute-start.3
  92.9 5.3 collective-permute-start.4
  106.4 6.2 scan_state.1
  118.9 6.7 collective-permute-done.14
  125.9 4.4 collective-permute-start.15
  133.1 4.8 collective-permute-done.15
  138.0 4.4 collective-permute-start.16
  150.2 5.0 collective-permute-start.17
  167.3 10.4 scan_output.1
  183.5 11.1 %attend.1 = bf16[1600,128]{1,0:T(8,128)(2,1)} custom-call(bf16[1600,128]{1,0:T(8,128)(2,1)} %pad_maximum_fusion.28.query_ref, bf16[320,1536]{1,0:T(8,128)(2,1)} %get-tuple-element.336.keys_ref, bf16[320,1536]{1,0:T(8,128)(2,1)} %get-tuple-element.335.values_ref, f32[1536,128]{1,0:T(8,128)} %fusion.67.bias_ref), custom_call_target="tpu_custom_call" | custom-call | bytes 1048576 | tf_op jit(solution)/shard_map/attend/pallas_call | solution.py:557
  199.4 7.8 collective-permute-done.7
  216.6 12.8 %collective-permute-done.8 = bf16[128,800]{1,0:T(8,128)(2,1)} collective-permute-done((bf16[128,800]{1,0:T(8,128)(2,1)}, bf16[128,800]{1,0:T(8,128)(2,1)}, u32[]{:S(2)}, u32[]{:S(2)}) %collective-permute-start.8) | collective-permute-done | bytes 204832 | tf_op jit(solution)/shard_map/ppermute | solution.py:28
  230.7 4.9 convolution_convert_fusion.2
  237.9 5.1 collective-permute-done.19
  252.2 4.1 copy.208
  258.8 7.6 fusion.79
  270.5 8.7 multiply_convert_fusion
  288.3 7.7 fusion.123
  328.1 4.3 fusion.63
  334.9 6.2 collective-permute-done.25
  348.3 8.5 gradient.12
  365.2 14.9 %collective-permute-done.36 = bf16[256,2752]{0,1:T(8,128)(2,1)} collective-permute-done((bf16[256,2752]{0,1:T(8,128)(2,1)}, bf16[256,2752]{0,1:T(8,128)(2,1)}, u32[]{:S(2)}, u32[]{:S(2)}) %collective-permute-start.36) | collective-permute-done | bytes 1409056 | tf_op jit(solution)/shard_map/ppermute | solution.py:88
  382.6 27.7 %collective-permute-done.35 = bf16[256,2752]{0,1:T(8,128)(2,1)} collective-permute-done((bf16[256,2752]{0,1:T(8,128)(2,1)}, bf16[256,2752]{0,1:T(8,128)(2,1)}, u32[]{:S(2)}, u32[]{:S(2)}) %collective-permute-start.35) | collective-permute-done | bytes 1409056 | tf_op jit(solution)/shard_map/ppermute | solution.py:88
  416.7 8.5 gradient.14
  425.3 8.5 gradient.13
  441.0 4.5 fusion.103
  453.5 21.7 %attend_back.1 = (bf16[1600,128]{1,0:T(8,128)(2,1)}, f32[320,1536]{1,0:T(8,128)}, f32[320,1536]{1,0:T(8,128)}) custom-call(bf16[1600,128]{1,0:T(8,128)(2,1)} %pad_maximum_fusion.28.query_ref, bf16[320,1536]{1,0:T(8,128)(2,1)} %get-tuple-element.336.keys_ref, bf16[320,1536]{1,0:T(8,128)(2,1)} %get-tuple-element.335.values_ref, ...), custom_call_target="tpu_custom_call" | custom-call | bytes 2621440 | tf_op jit(solution)/shard_map/attend_back/pallas_call | solution.py:557
  483.7 4.9 fusion.17
  488.7 6.3 scan_adjoint.1
  502.0 7.0 gradient.16
  511.9 5.1 gradient.15
  525.7 20.3 %collective-permute-done.33 = bf16[200,2752]{1,0:T(8,128)(2,1)S(1)} collective-permute-done((bf16[200,2752]{1,0:T(8,128)(2,1)S(1)}, bf16[200,2752]{1,0:T(8,128)(2,1)S(1)}, u32[]{:S(2)}, u32[]{:S(2)}) %collective-permute-start.33) | collective-permute-done | bytes 1100832 | tf_op jit(solution)/shard_map/ppermute | solution.py:88
  551.3 9.4 collective-permute-done.31
  573.6 6.6 collective-permute-done.32
  587.1 28.3 %scan_gradient.1 = (f32[16,8,3200]{2,1,0:T(8,128)S(1)}, f32[16,8,3200]{2,1,0:T(8,128)S(1)}, f32[128,16,128]{2,1,0:T(8,128)S(1)}, f32[128,16,128]{2,1,0:T(8,128)S(1)}, f32[16,3200]{1,0:T(8,128)S(1)}) custom-call(f32[16,8,3200]{2,1,0:T(8,128)S(1)} %copy-done.4, f32[16,8,3200]{2,1,0:T(8,128)S(1)} %copy-done.7, f32[16,8,3200]{2,1,0:T(8,128)S(1)} %bitcast.143, ...), custom_call_target="tpu_custom_call" | custom-call | bytes 5242880 | tf_op jit(solution)/shard_map/scan_gradient/pallas_call | solution.py:440
  630.5 4.7 collective-permute-done.59
  635.2 10.6 collective-permute-start.42
  645.7 4.7 collective-permute-done.60
  660.0 4.3 fusion.72
  675.2 9.5 collective-permute-done.70
  685.0 6.1 gradient.17
  696.2 19.7 %collective-permute-done.43 = bf16[200,2752]{1,0:T(8,128)(2,1)} collective-permute-done((bf16[200,2752]{1,0:T(8,128)(2,1)}, bf16[200,2752]{1,0:T(8,128)(2,1)}, u32[]{:S(2)}, u32[]{:S(2)}) %collective-permute-start.43) | collective-permute-done | bytes 1100832 | tf_op jit(solution)/shard_map/ppermute | solution.py:88
  728.8 9.7 multiply_reduce_fusion.3
  754.3 40.9 %all-reduce.6 = (f32[3200]{0:T(1024)}, f32[3200]{0:T(1024)}, f32[1600]{0:T(1024)}, f32[1600]{0:T(1024)}, f32[1600]{0:T(1024)}) all-reduce(f32[3200]{0:T(1024)} %get-tuple-element.304, f32[3200]{0:T(1024)} %get-tuple-element.302, f32[1600]{0:T(1024)} %get-tuple-element.292, ...), channel_id=1, replica_groups=mesh['seq'=16,'wt'=2] {'seq','wt'}, use_global_device_ids=true, to_apply=%region_19.20 | all-reduce | flops 11200 | bytes 89600 | tf_op jit(solution)/shard_map/psum | solution.py:857
  806.6 7.6 collective-permute-done.87
  818.9 9.4 collective-permute-done.88
  828.4 9.6 collective-permute-done.49
  854.1 13.0 %collective-permute-done.92 = bf16[400,100]{1,0:T(8,128)(2,1)S(1)} collective-permute-done((bf16[400,100]{1,0:T(8,128)(2,1)S(1)}, bf16[400,100]{1,0:T(8,128)(2,1)S(1)}, u32[]{:S(2)}, u32[]{:S(2)}) %collective-permute-start.92) | collective-permute-done | bytes 80032 | tf_op jit(solution)/shard_map/ppermute | solution.py:88
  870.5 10.1 collective-permute-done.50
  882.5 17.7 %collective-permute-done.93 = bf16[200,100]{1,0:T(8,128)(2,1)S(1)} collective-permute-done((bf16[200,100]{1,0:T(8,128)(2,1)S(1)}, bf16[200,100]{1,0:T(8,128)(2,1)S(1)}, u32[]{:S(2)}, u32[]{:S(2)}) %collective-permute-start.93) | collective-permute-done | bytes 40032 | tf_op jit(solution)/shard_map/ppermute | solution.py:88
  913.6 13.5 %collective-permute-done.54 = bf16[128,512]{1,0:T(8,128)(2,1)S(1)} collective-permute-done((bf16[128,512]{1,0:T(8,128)(2,1)S(1)}, bf16[128,512]{1,0:T(8,128)(2,1)S(1)}, u32[]{:S(2)}, u32[]{:S(2)}) %collective-permute-start.54) | collective-permute-done | bytes 131104 | tf_op jit(solution)/shard_map/ppermute | solution.py:28
  928.0 7.0 convolution_add_fusion.3
  947.6 4.7 collective-permute-done.63
  955.9 4.2 gradient.21
  961.9 5.5 collective-permute-done.83
  968.5 13.3 %collective-permute-done.65 = f32[144,128]{1,0:T(8,128)S(1)} collective-permute-done((f32[144,128]{1,0:T(8,128)S(1)}, f32[144,128]{1,0:T(8,128)S(1)}, u32[]{:S(2)}, u32[]{:S(2)}) %collective-permute-start.65) | collective-permute-done | bytes 73760 | tf_op jit(solution)/shard_map/ppermute | solution.py:478
  981.9 4.3 collective-permute-done.66
  991.5 5.5 gradient.18
  999.1 5.5 gradient.19
  1004.7 4.7 gradient.20
  1027.0 13.6 %collective-permute-done.75 = bf16[100,896]{1,0:T(8,128)(2,1)S(1)} collective-permute-done((bf16[100,896]{1,0:T(8,128)(2,1)S(1)}, bf16[100,896]{1,0:T(8,128)(2,1)S(1)}, u32[]{:S(2)}, u32[]{:S(2)}) %collective-permute-start.75) | collective-permute-done | bytes 179232 | tf_op jit(solution)/shard_map/ppermute | solution.py:88
  1040.7 3.9 collective-permute-done.78
  (869 shorter events, 434.7 us)
Async XLA Ops:
  7.3 1040.6 %all-reduce.9.cloned.1.call-start = ((), (), s32[]{:S(2)}) async-start(), calls=%async_computation | async-start | bytes 409600 | tf_op jit(solution)/shard_map/psum | solution.py:857
  9.4 33.5 %collective-permute-start = (bf16[128,1600]{1,0:T(8,128)(2,1)}, bf16[128,1600]{1,0:T(8,128)(2,1)}, u32[]{:S(2)}, u32[]{:S(2)}) collective-permute-start(bf16[128,1600]{1,0:T(8,128)(2,1)} %bitcast), channel_id=1, source_target_pairs={{1,0},{0,1},{3,2},{2,3},{5,4},{4,5},{7,6},{6,7},{9,8},{8,9},{11,10... | collective-permute-start | bytes 1228808 | tf_op jit(solution)/shard_map/ppermute | solution.py:28
  12.4 71.6 %collective-permute-start.11 = (bf16[66,3200]{1,0:T(8,128)(2,1)}, bf16[66,3200]{1,0:T(8,128)(2,1)}, u32[]{:S(2)}, u32[]{:S(2)}) collective-permute-start(bf16[66,3200]{1,0:T(8,128)(2,1)} %bitcast.164), channel_id=1, source_target_pairs={{1,0},{0,1},{3,2},{2,3},{5,4},{4,5},{7,6},{6,7},{9,8},{8,9},{11,10... | collective-permute-start | bytes 1267208 | tf_op jit(solution)/shard_map/ppermute | solution.py:28
  12.4 28.5 %collective-permute-start.12 = (bf16[50,3200]{1,0:T(8,128)(2,1)}, bf16[50,3200]{1,0:T(8,128)(2,1)}, u32[]{:S(2)}, u32[]{:S(2)}) collective-permute-start(bf16[50,3200]{1,0:T(8,128)(2,1)} %bitcast.165), channel_id=1, source_target_pairs={{1,0},{0,1},{3,2},{2,3},{5,4},{4,5},{7,6},{6,7},{9,8},{8,9},{11,10... | collective-permute-start | bytes 960008 | tf_op jit(solution)/shard_map/ppermute | solution.py:28
  16.4 48.4 %collective-permute-start.22 = (bf16[128,1600]{1,0:T(8,128)(2,1)}, bf16[128,1600]{1,0:T(8,128)(2,1)}, u32[]{:S(2)}, u32[]{:S(2)}) collective-permute-start(bf16[128,1600]{1,0:T(8,128)(2,1)} %bitcast.44), channel_id=1, source_target_pairs={{1,0},{0,1},{3,2},{2,3},{5,4},{4,5},{7,6},{6,7},{9,8},{8,9},{11,10... | collective-permute-start | bytes 1228808 | tf_op jit(solution)/shard_map/ppermute | solution.py:28
  47.9 37.5 %collective-permute-start.2 = (bf16[2,160,128]{2,1,0:T(8,128)(2,1)S(1)}, bf16[2,160,128]{2,1,0:T(8,128)(2,1)}, u32[]{:S(2)}, u32[]{:S(2)}) collective-permute-start(bf16[2,160,128]{2,1,0:T(8,128)(2,1)S(1)} %fusion.89), channel_id=1, source_target_pairs={{1,0},{0,1},{3,2},{2,3},{5,4},{4,5},{7,6},{6,7},{9,8},{8,9},{11,10... | collective-permute-start | bytes 245768 | tf_op jit(solution)/shard_map/ppermute | solution.py:28
  53.0 61.7 %collective-permute-start.1 = (bf16[800,128]{1,0:T(8,128)(2,1)}, bf16[800,128]{1,0:T(8,128)(2,1)}, u32[]{:S(2)}, u32[]{:S(2)}) collective-permute-start(bf16[800,128]{1,0:T(8,128)(2,1)} %split.143), channel_id=1, source_target_pairs={{1,0},{0,1},{3,2},{2,3},{5,4},{4,5},{7,6},{6,7},{9,8},{8,9},{11,10... | collective-permute-start | bytes 614408 | tf_op jit(solution)/shard_map/ppermute | solution.py:28
  62.9 23.6 %collective-permute-start.9 = (bf16[128,3200]{1,0:T(8,128)(2,1)}, bf16[128,3200]{1,0:T(8,128)(2,1)}, u32[]{:S(2)}, u32[]{:S(2)}) collective-permute-start(bf16[128,3200]{1,0:T(8,128)(2,1)} %split.149), channel_id=1, source_target_pairs={{1,0},{0,1},{3,2},{2,3},{5,4},{4,5},{7,6},{6,7},{9,8},{8,9},{11,10... | collective-permute-start | bytes 2457608 | tf_op jit(solution)/shard_map/ppermute | solution.py:28
  73.9 269.8 %collective-permute-start.24 = (bf16[800,256]{1,0:T(8,128)(2,1)}, bf16[800,256]{1,0:T(8,128)(2,1)}, u32[]{:S(2)}, u32[]{:S(2)}) collective-permute-start(bf16[800,256]{1,0:T(8,128)(2,1)} %get-tuple-element.108), channel_id=1, source_target_pairs={{0,4},{2,6},{4,0},{6,2},{8,12},{10,14},{12,8},{14,10},{16,20},{18,... | collective-permute-start | bytes 1228808 | tf_op jit(solution)/shard_map/ppermute | solution.py:88
  88.8 42.2 %collective-permute-start.3 = (bf16[2,320,128]{2,1,0:T(8,128)(2,1)}, bf16[2,320,128]{2,1,0:T(8,128)(2,1)S(1)}, u32[]{:S(2)}, u32[]{:S(2)}) collective-permute-start(bf16[2,320,128]{2,1,0:T(8,128)(2,1)} %get-tuple-element.395), channel_id=1, source_target_pairs={{0,8},{2,10},{4,12},{6,14},{8,16},{10,18},{12,20},{14,22},{16,24},... | collective-permute-start | bytes 491528 | tf_op jit(solution)/shard_map/ppermute | solution.py:23
  92.9 38.1 %collective-permute-start.4 = (bf16[2,320,128]{2,1,0:T(8,128)(2,1)}, bf16[2,320,128]{2,1,0:T(8,128)(2,1)}, u32[]{:S(2)}, u32[]{:S(2)}) collective-permute-start(bf16[2,320,128]{2,1,0:T(8,128)(2,1)} %get-tuple-element.395), channel_id=1, source_target_pairs={{0,16},{2,18},{4,20},{6,22},{8,24},{10,26},{12,28},{14,30},{1,17},... | collective-permute-start | bytes 491528 | tf_op jit(solution)/shard_map/ppermute | solution.py:23
  132.1 23.1 %collective-permute-start.5 = (bf16[2,320,384]{2,1,0:T(8,128)(2,1)S(1)}, bf16[2,320,384]{2,1,0:T(8,128)(2,1)S(1)}, u32[]{:S(2)}, u32[]{:S(2)}) collective-permute-start(bf16[2,320,384]{2,1,0:T(8,128)(2,1)S(1)} %pad_maximum_fusion.17), channel_id=1, source_target_pairs={{0,4},{2,6},{4,0},{6,2},{8,12},{10,14},{12,8},{14,10},{16,20},{18,... | collective-permute-start | bytes 1474568 | tf_op jit(solution)/shard_map/ppermute | solution.py:88
  157.3 20.5 %collective-permute-start.6 = (bf16[2,320,768]{2,1,0:T(8,128)(2,1)}, bf16[2,320,768]{2,1,0:T(8,128)(2,1)}, u32[]{:S(2)}, u32[]{:S(2)}) collective-permute-start(bf16[2,320,768]{2,1,0:T(8,128)(2,1)} %pad_maximum_fusion.5), channel_id=1, source_target_pairs={{0,2},{2,0},{4,6},{6,4},{8,10},{10,8},{12,14},{14,12},{16,18},{18,... | collective-permute-start | bytes 2949128 | tf_op jit(solution)/shard_map/ppermute | solution.py:88
  199.3 31.3 %collective-permute-start.18 = (bf16[128,3200]{1,0:T(8,128)(2,1)}, bf16[128,3200]{1,0:T(8,128)(2,1)}, u32[]{:S(2)}, u32[]{:S(2)}) collective-permute-start(bf16[128,3200]{1,0:T(8,128)(2,1)} %get-tuple-element.317), channel_id=1, source_target_pairs={{1,0},{0,1},{3,2},{2,3},{5,4},{4,5},{7,6},{6,7},{9,8},{8,9},{11,10... | collective-permute-start | bytes 2457608 | tf_op jit(solution)/shard_map/ppermute | solution.py:28
  209.8 19.6 %collective-permute-start.8 = (bf16[128,800]{1,0:T(8,128)(2,1)}, bf16[128,800]{1,0:T(8,128)(2,1)}, u32[]{:S(2)}, u32[]{:S(2)}) collective-permute-start(bf16[128,800]{1,0:T(8,128)(2,1)} %split.147), channel_id=1, source_target_pairs={{1,0},{0,1},{3,2},{2,3},{5,4},{4,5},{7,6},{6,7},{9,8},{8,9},{11,10... | collective-permute-start | bytes 614408 | tf_op jit(solution)/shard_map/ppermute | solution.py:28
  287.0 37.0 %collective-permute-start.23 = (bf16[128,1600]{1,0:T(8,128)(2,1)}, bf16[128,1600]{1,0:T(8,128)(2,1)}, u32[]{:S(2)}, u32[]{:S(2)}) collective-permute-start(bf16[128,1600]{1,0:T(8,128)(2,1)} %copy.243), channel_id=1, source_target_pairs={{1,0},{0,1},{3,2},{2,3},{5,4},{4,5},{7,6},{6,7},{9,8},{8,9},{11,10... | collective-permute-start | bytes 1228808 | tf_op jit(solution)/shard_map/ppermute | solution.py:28
  307.0 34.1 %collective-permute-start.25 = (bf16[256,2752]{0,1:T(8,128)(2,1)}, bf16[256,2752]{0,1:T(8,128)(2,1)}, u32[]{:S(2)}, u32[]{:S(2)}) collective-permute-start(bf16[256,2752]{0,1:T(8,128)(2,1)} %copy.201), channel_id=1, source_target_pairs={{0,4},{2,6},{4,0},{6,2},{8,12},{10,14},{12,8},{14,10},{16,20},{18,... | collective-permute-start | bytes 4227080 | tf_op jit(solution)/shard_map/ppermute | solution.py:88
  322.0 91.1 %collective-permute-start.34 = (bf16[800,256]{1,0:T(8,128)(2,1)}, bf16[800,256]{1,0:T(8,128)(2,1)S(1)}, u32[]{:S(2)}, u32[]{:S(2)}) collective-permute-start(bf16[800,256]{1,0:T(8,128)(2,1)} %get-tuple-element.116), channel_id=1, source_target_pairs={{0,4},{2,6},{4,0},{6,2},{8,12},{10,14},{12,8},{14,10},{16,20},{18,... | collective-permute-start | bytes 1228808 | tf_op jit(solution)/shard_map/ppermute | solution.py:88
  324.0 56.1 %collective-permute-start.36 = (bf16[256,2752]{0,1:T(8,128)(2,1)}, bf16[256,2752]{0,1:T(8,128)(2,1)}, u32[]{:S(2)}, u32[]{:S(2)}) collective-permute-start(bf16[256,2752]{0,1:T(8,128)(2,1)} %copy.206), channel_id=1, source_target_pairs={{0,4},{2,6},{4,0},{6,2},{8,12},{10,14},{12,8},{14,10},{16,20},{18,... | collective-permute-start | bytes 4227080 | tf_op jit(solution)/shard_map/ppermute | solution.py:88
  325.9 84.4 %collective-permute-start.35 = (bf16[256,2752]{0,1:T(8,128)(2,1)}, bf16[256,2752]{0,1:T(8,128)(2,1)}, u32[]{:S(2)}, u32[]{:S(2)}) collective-permute-start(bf16[256,2752]{0,1:T(8,128)(2,1)} %copy.204), channel_id=1, source_target_pairs={{0,4},{2,6},{4,0},{6,2},{8,12},{10,14},{12,8},{14,10},{16,20},{18,... | collective-permute-start | bytes 4227080 | tf_op jit(solution)/shard_map/ppermute | solution.py:88
  359.7 74.1 %collective-permute-start.26 = (bf16[128,800]{1,0:T(8,128)(2,1)}, bf16[128,800]{1,0:T(8,128)(2,1)}, u32[]{:S(2)}, u32[]{:S(2)}) collective-permute-start(bf16[128,800]{1,0:T(8,128)(2,1)} %get-tuple-element.377), channel_id=1, source_target_pairs={{1,0},{0,1},{3,2},{2,3},{5,4},{4,5},{7,6},{6,7},{9,8},{8,9},{11,10... | collective-permute-start | bytes 614408 | tf_op jit(solution)/shard_map/ppermute | solution.py:28
  361.3 76.5 %collective-permute-start.38 = (bf16[128,800]{1,0:T(8,128)(2,1)}, bf16[128,800]{1,0:T(8,128)(2,1)}, u32[]{:S(2)}, u32[]{:S(2)}) collective-permute-start(bf16[128,800]{1,0:T(8,128)(2,1)} %get-tuple-element.381), channel_id=1, source_target_pairs={{1,0},{0,1},{3,2},{2,3},{5,4},{4,5},{7,6},{6,7},{9,8},{8,9},{11,10... | collective-permute-start | bytes 614408 | tf_op jit(solution)/shard_map/ppermute | solution.py:28
  380.1 129.0 %collective-permute-start.37 = (bf16[800,256]{1,0:T(8,128)(2,1)}, bf16[800,256]{1,0:T(8,128)(2,1)}, u32[]{:S(2)}, u32[]{:S(2)}) collective-permute-start(bf16[800,256]{1,0:T(8,128)(2,1)} %copy-done.80), channel_id=1, source_target_pairs={{0,4},{2,6},{4,0},{6,2},{8,12},{10,14},{12,8},{14,10},{16,20},{18,... | collective-permute-start | bytes 1228808 | tf_op jit(solution)/shard_map/ppermute | solution.py:88
  410.3 85.5 %collective-permute-start.40 = (bf16[1600,256]{1,0:T(8,128)(2,1)}, bf16[1600,256]{1,0:T(8,128)(2,1)}, u32[]{:S(2)}, u32[]{:S(2)}) collective-permute-start(bf16[1600,256]{1,0:T(8,128)(2,1)} %copy-done.78), channel_id=1, source_target_pairs={{0,4},{2,6},{4,0},{6,2},{8,12},{10,14},{12,8},{14,10},{16,20},{18,... | collective-permute-start | bytes 2457608 | tf_op jit(solution)/shard_map/ppermute | solution.py:88
  435.8 61.2 %collective-permute-start.41 = (bf16[256,800]{1,0:T(8,128)(2,1)}, bf16[256,800]{1,0:T(8,128)(2,1)}, u32[]{:S(2)}, u32[]{:S(2)}) collective-permute-start(bf16[256,800]{1,0:T(8,128)(2,1)} %pad_maximum_fusion.18.right_ref), channel_id=1, source_target_pairs={{0,4},{2,6},{4,0},{6,2},{8,12},{10,14},{12,8},{14,10},{16,20},{18,... | collective-permute-start | bytes 1228808 | tf_op jit(solution)/shard_map/ppermute | solution.py:88
  446.6 36.4 %collective-permute-start.27 = (bf16[128,3200]{1,0:T(8,128)(2,1)}, bf16[128,3200]{1,0:T(8,128)(2,1)}, u32[]{:S(2)}, u32[]{:S(2)}) collective-permute-start(bf16[128,3200]{1,0:T(8,128)(2,1)} %split.234), channel_id=1, source_target_pairs={{1,0},{0,1},{3,2},{2,3},{5,4},{4,5},{7,6},{6,7},{9,8},{8,9},{11,10... | collective-permute-start | bytes 2457608 | tf_op jit(solution)/shard_map/ppermute | solution.py:28
  452.6 59.2 %collective-permute-start.39 = (bf16[256,800]{1,0:T(8,128)(2,1)}, bf16[256,800]{1,0:T(8,128)(2,1)}, u32[]{:S(2)}, u32[]{:S(2)}) collective-permute-start(bf16[256,800]{1,0:T(8,128)(2,1)} %pad_maximum_fusion.19.right_ref), channel_id=1, source_target_pairs={{0,4},{2,6},{4,0},{6,2},{8,12},{10,14},{12,8},{14,10},{16,20},{18,... | collective-permute-start | bytes 1228808 | tf_op jit(solution)/shard_map/ppermute | solution.py:88
  483.0 34.0 %collective-permute-start.56 = (bf16[800,128]{0,1:T(8,128)(2,1)}, bf16[800,128]{0,1:T(8,128)(2,1)}, u32[]{:S(2)}, u32[]{:S(2)}) collective-permute-start(bf16[800,128]{0,1:T(8,128)(2,1)} %get-tuple-element.379), channel_id=1, source_target_pairs={{1,0},{0,1},{3,2},{2,3},{5,4},{4,5},{7,6},{6,7},{9,8},{8,9},{11,10... | collective-permute-start | bytes 614408 | tf_op jit(solution)/shard_map/ppermute | solution.py:28
  495.7 26.4 %collective-permute-start.28 = (f32[17,3200]{1,0:T(8,128)}, f32[17,3200]{1,0:T(8,128)}, u32[]{:S(2)}, u32[]{:S(2)}) collective-permute-start(f32[17,3200]{1,0:T(8,128)} %pad_maximum_fusion.24), channel_id=1, source_target_pairs={{2,0},{4,2},{6,4},{8,6},{10,8},{12,10},{14,12},{16,14},{18,16},{20... | collective-permute-start | bytes 652808 | tf_op jit(solution)/shard_map/ppermute | solution.py:23
  497.0 25.1 %collective-permute-start.29 = (f32[17,3200]{1,0:T(8,128)}, f32[17,3200]{1,0:T(8,128)}, u32[]{:S(2)}, u32[]{:S(2)}) collective-permute-start(f32[17,3200]{1,0:T(8,128)} %pad_maximum_fusion.24), channel_id=1, source_target_pairs={{4,0},{6,2},{8,4},{10,6},{12,8},{14,10},{16,12},{18,14},{20,16},{2... | collective-permute-start | bytes 652808 | tf_op jit(solution)/shard_map/ppermute | solution.py:23
  509.1 175.9 %collective-permute-start.69 = (bf16[800,256]{1,0:T(8,128)(2,1)}, bf16[800,256]{1,0:T(8,128)(2,1)}, u32[]{:S(2)}, u32[]{:S(2)}) collective-permute-start(bf16[800,256]{1,0:T(8,128)(2,1)} %get-tuple-element.162), channel_id=1, source_target_pairs={{0,4},{2,6},{4,0},{6,2},{8,12},{10,14},{12,8},{14,10},{16,20},{18,... | collective-permute-start | bytes 1228808 | tf_op jit(solution)/shard_map/ppermute | solution.py:88
  511.8 332.3 %collective-permute-start.91 = (bf16[128,100]{1,0:T(8,128)(2,1)S(1)}, bf16[128,100]{1,0:T(8,128)(2,1)}, u32[]{:S(2)}, u32[]{:S(2)}) collective-permute-start(bf16[128,100]{1,0:T(8,128)(2,1)S(1)} %copy.239.right_ref), channel_id=1, source_target_pairs={{0,4},{2,6},{4,0},{6,2},{8,12},{10,14},{12,8},{14,10},{16,20},{18,... | collective-permute-start | bytes 76808 | tf_op jit(solution)/shard_map/ppermute | solution.py:88
  517.0 28.9 %collective-permute-start.33 = (bf16[200,2752]{1,0:T(8,128)(2,1)S(1)}, bf16[200,2752]{1,0:T(8,128)(2,1)S(1)}, u32[]{:S(2)}, u32[]{:S(2)}) collective-permute-start(bf16[200,2752]{1,0:T(8,128)(2,1)S(1)} %copy-done.77), channel_id=1, source_target_pairs={{0,8},{2,10},{4,12},{6,14},{8,0},{10,2},{12,4},{14,6},{16,24},{18,... | collective-permute-start | bytes 3302408 | tf_op jit(solution)/shard_map/ppermute | solution.py:88
  522.1 26.9 %collective-permute-start.57 = (bf16[2,320,768]{2,1,0:T(8,128)(2,1)S(1)}, bf16[2,320,768]{2,1,0:T(8,128)(2,1)}, u32[]{:S(2)}, u32[]{:S(2)}) collective-permute-start(bf16[2,320,768]{2,1,0:T(8,128)(2,1)S(1)} %copy-done.147), channel_id=1, source_target_pairs={{0,2},{2,0},{4,6},{6,4},{8,10},{10,8},{12,14},{14,12},{16,18},{18,... | collective-permute-start | bytes 2949128 | tf_op jit(solution)/shard_map/ppermute | solution.py:88
  524.4 21.9 %collective-permute-start.30 = (f32[17,3200]{1,0:T(8,128)S(1)}, f32[17,3200]{1,0:T(8,128)S(1)}, u32[]{:S(2)}, u32[]{:S(2)}) collective-permute-start(f32[17,3200]{1,0:T(8,128)S(1)} %pad_maximum_fusion.34), channel_id=1, source_target_pairs={{4,0},{6,2},{8,4},{10,6},{12,8},{14,10},{16,12},{18,14},{20,16},{2... | collective-permute-start | bytes 652808 | tf_op jit(solution)/shard_map/ppermute | solution.py:23
  569.9 53.9 %collective-permute-start.58 = (bf16[2,320,384]{2,1,0:T(8,128)(2,1)}, bf16[2,320,384]{2,1,0:T(8,128)(2,1)}, u32[]{:S(2)}, u32[]{:S(2)}) collective-permute-start(bf16[2,320,384]{2,1,0:T(8,128)(2,1)} %copy.216), channel_id=1, source_target_pairs={{0,4},{2,6},{4,0},{6,2},{8,12},{10,14},{12,8},{14,10},{16,20},{18,... | collective-permute-start | bytes 1474568 | tf_op jit(solution)/shard_map/ppermute | solution.py:88
  581.4 91.6 %collective-permute-start.46 = (bf16[400,800]{1,0:T(8,128)(2,1)}, bf16[400,800]{1,0:T(8,128)(2,1)}, u32[]{:S(2)}, u32[]{:S(2)}) collective-permute-start(bf16[400,800]{1,0:T(8,128)(2,1)} %copy-done.79), channel_id=1, source_target_pairs={{0,8},{2,10},{4,12},{6,14},{8,0},{10,2},{12,4},{14,6},{16,24},{18,... | collective-permute-start | bytes 1920008 | tf_op jit(solution)/shard_map/ppermute | solution.py:88
  581.5 46.6 %collective-permute-start.45 = (bf16[200,800]{1,0:T(8,128)(2,1)}, bf16[200,800]{1,0:T(8,128)(2,1)}, u32[]{:S(2)}, u32[]{:S(2)}) collective-permute-start(bf16[200,800]{1,0:T(8,128)(2,1)} %copy-done.82), channel_id=1, source_target_pairs={{0,8},{2,10},{4,12},{6,14},{8,0},{10,2},{12,4},{14,6},{16,24},{18,... | collective-permute-start | bytes 960008 | tf_op jit(solution)/shard_map/ppermute | solution.py:88
  628.1 22.3 %collective-permute-start.60 = (bf16[2,320,128]{1,2,0:T(8,128)(2,1)S(1)}, bf16[2,320,128]{1,2,0:T(8,128)(2,1)S(1)}, u32[]{:S(2)}, u32[]{:S(2)}) collective-permute-start(bf16[2,320,128]{1,2,0:T(8,128)(2,1)S(1)} %get-tuple-element.373), channel_id=1, source_target_pairs={{16,0},{18,2},{20,4},{22,6},{24,8},{26,10},{28,12},{30,14},{17,1},... | collective-permute-start | bytes 491528 | tf_op jit(solution)/shard_map/ppermute | solution.py:23
  635.2 32.4 %collective-permute-start.42 = (bf16[100,2752]{1,0:T(8,128)(2,1)S(1)}, bf16[100,2752]{1,0:T(8,128)(2,1)}, u32[]{:S(2)}, u32[]{:S(2)}) collective-permute-start(bf16[100,2752]{1,0:T(8,128)(2,1)S(1)} %copy-done.154), channel_id=1, source_target_pairs={{0,16},{2,18},{4,20},{6,22},{8,24},{10,26},{12,28},{14,30},{16,0},... | collective-permute-start | bytes 1651208 | tf_op jit(solution)/shard_map/ppermute | solution.py:88
  659.2 34.0 %collective-permute-start.44 = (bf16[200,2752]{1,0:T(8,128)(2,1)}, bf16[200,2752]{1,0:T(8,128)(2,1)}, u32[]{:S(2)}, u32[]{:S(2)}) collective-permute-start(bf16[200,2752]{1,0:T(8,128)(2,1)} %get-tuple-element.141), channel_id=1, source_target_pairs={{0,8},{2,10},{4,12},{6,14},{8,0},{10,2},{12,4},{14,6},{16,24},{18,... | collective-permute-start | bytes 3302408 | tf_op jit(solution)/shard_map/ppermute | solution.py:88
  673.0 122.3 %collective-permute-start.85 = (bf16[1600,128]{1,0:T(8,128)(2,1)}, bf16[1600,128]{1,0:T(8,128)(2,1)S(1)}, u32[]{:S(2)}, u32[]{:S(2)}) collective-permute-start(bf16[1600,128]{1,0:T(8,128)(2,1)} %get-tuple-element.176), channel_id=1, source_target_pairs={{0,4},{2,6},{4,0},{6,2},{8,12},{10,14},{12,8},{14,10},{16,20},{18,... | collective-permute-start | bytes 1228808 | tf_op jit(solution)/shard_map/ppermute | solution.py:88
  684.7 31.3 %collective-permute-start.43 = (bf16[200,2752]{1,0:T(8,128)(2,1)}, bf16[200,2752]{1,0:T(8,128)(2,1)}, u32[]{:S(2)}, u32[]{:S(2)}) collective-permute-start(bf16[200,2752]{1,0:T(8,128)(2,1)} %get-tuple-element.139), channel_id=1, source_target_pairs={{0,8},{2,10},{4,12},{6,14},{8,0},{10,2},{12,4},{14,6},{16,24},{18,... | collective-permute-start | bytes 3302408 | tf_op jit(solution)/shard_map/ppermute | solution.py:88
  691.1 159.1 %collective-permute-start.71 = (bf16[200,1120]{1,0:T(8,128)(2,1)}, bf16[200,1120]{1,0:T(8,128)(2,1)}, u32[]{:S(2)}, u32[]{:S(2)}) collective-permute-start(bf16[200,1120]{1,0:T(8,128)(2,1)} %get-tuple-element.164), channel_id=1, source_target_pairs={{0,8},{2,10},{4,12},{6,14},{8,0},{10,2},{12,4},{14,6},{16,24},{18,... | collective-permute-start | bytes 1344008 | tf_op jit(solution)/shard_map/ppermute | solution.py:88
  725.7 71.2 %collective-permute-start.86 = (bf16[128,132]{1,0:T(8,128)(2,1)}, bf16[128,132]{1,0:T(8,128)(2,1)}, u32[]{:S(2)}, u32[]{:S(2)}) collective-permute-start(bf16[128,132]{1,0:T(8,128)(2,1)} %pad_maximum_fusion.44.right_ref), channel_id=1, source_target_pairs={{0,4},{2,6},{4,0},{6,2},{8,12},{10,14},{12,8},{14,10},{16,20},{18,... | collective-permute-start | bytes 101384 | tf_op jit(solution)/shard_map/ppermute | solution.py:88
  741.4 61.2 %collective-permute-start.47 = (bf16[3,3200]{1,0:T(4,128)(2,1)}, bf16[3,3200]{1,0:T(4,128)(2,1)}, u32[]{:S(2)}, u32[]{:S(2)}) collective-permute-start(bf16[3,3200]{1,0:T(4,128)(2,1)} %pad_maximum_fusion.46), channel_id=1, source_target_pairs={{2,0},{4,2},{6,4},{8,6},{10,8},{12,10},{14,12},{16,14},{18,16},{20... | collective-permute-start | bytes 57608 | tf_op jit(solution)/shard_map/ppermute | solution.py:23
  795.3 114.6 %collective-permute-start.95 = (bf16[100,2752]{1,0:T(8,128)(2,1)}, bf16[100,2752]{1,0:T(8,128)(2,1)}, u32[]{:S(2)}, u32[]{:S(2)}) collective-permute-start(bf16[100,2752]{1,0:T(8,128)(2,1)} %get-tuple-element.187), channel_id=1, source_target_pairs={{0,16},{2,18},{4,20},{6,22},{8,24},{10,26},{12,28},{14,30},{16,0},... | collective-permute-start | bytes 1651208 | tf_op jit(solution)/shard_map/ppermute | solution.py:88
  796.9 50.2 %collective-permute-start.90 = (bf16[1600,128]{1,0:T(8,128)(2,1)}, bf16[1600,128]{1,0:T(8,128)(2,1)S(1)}, u32[]{:S(2)}, u32[]{:S(2)}) collective-permute-start(bf16[1600,128]{1,0:T(8,128)(2,1)} %copy-done.81), channel_id=1, source_target_pairs={{0,4},{2,6},{4,0},{6,2},{8,12},{10,14},{12,8},{14,10},{16,20},{18,... | collective-permute-start | bytes 1228808 | tf_op jit(solution)/shard_map/ppermute | solution.py:88
  843.3 37.3 %collective-permute-start.50 = (bf16[200,800]{1,0:T(8,128)(2,1)S(1)}, bf16[200,800]{1,0:T(8,128)(2,1)}, u32[]{:S(2)}, u32[]{:S(2)}) collective-permute-start(bf16[200,800]{1,0:T(8,128)(2,1)S(1)} %copy-done.165), channel_id=1, source_target_pairs={{0,16},{2,18},{4,20},{6,22},{8,24},{10,26},{12,28},{14,30},{16,0},... | collective-permute-start | bytes 960008 | tf_op jit(solution)/shard_map/ppermute | solution.py:88
  844.1 60.7 %collective-permute-start.48 = (bf16[100,2752]{1,0:T(8,128)(2,1)}, bf16[100,2752]{1,0:T(8,128)(2,1)}, u32[]{:S(2)}, u32[]{:S(2)}) collective-permute-start(bf16[100,2752]{1,0:T(8,128)(2,1)} %get-tuple-element.151), channel_id=1, source_target_pairs={{0,16},{2,18},{4,20},{6,22},{8,24},{10,26},{12,28},{14,30},{16,0},... | collective-permute-start | bytes 1651208 | tf_op jit(solution)/shard_map/ppermute | solution.py:88
  851.4 51.0 %collective-permute-start.72 = (bf16[100,1120]{1,0:T(8,128)(2,1)S(1)}, bf16[100,1120]{1,0:T(8,128)(2,1)S(1)}, u32[]{:S(2)}, u32[]{:S(2)}) collective-permute-start(bf16[100,1120]{1,0:T(8,128)(2,1)S(1)} %slice.489), channel_id=1, source_target_pairs={{0,16},{2,18},{4,20},{6,22},{8,24},{10,26},{12,28},{14,30},{16,0},... | collective-permute-start | bytes 672008 | tf_op jit(solution)/shard_map/ppermute | solution.py:88
  867.1 33.0 %collective-permute-start.93 = (bf16[200,100]{1,0:T(8,128)(2,1)S(1)}, bf16[200,100]{1,0:T(8,128)(2,1)S(1)}, u32[]{:S(2)}, u32[]{:S(2)}) collective-permute-start(bf16[200,100]{1,0:T(8,128)(2,1)S(1)} %slice.506), channel_id=1, source_target_pairs={{0,16},{2,18},{4,20},{6,22},{8,24},{10,26},{12,28},{14,30},{16,0},... | collective-permute-start | bytes 120008 | tf_op jit(solution)/shard_map/ppermute | solution.py:88
  900.9 41.2 %collective-permute-start.94 = (f32[200,50]{1,0:T(8,128)}, f32[200,50]{1,0:T(8,128)}, u32[]{:S(2)}, u32[]{:S(2)}) collective-permute-start(f32[200,50]{1,0:T(8,128)} %slice_select_fusion), channel_id=1, source_target_pairs={{1,0},{0,1},{3,2},{2,3},{5,4},{4,5},{7,6},{6,7},{9,8},{8,9},{11,10... | collective-permute-start | bytes 120008 | tf_op jit(solution)/shard_map/ppermute | solution.py:28
  907.1 19.9 %collective-permute-start.51 = (bf16[128,896]{1,0:T(8,128)(2,1)S(1)}, bf16[128,896]{1,0:T(8,128)(2,1)S(1)}, u32[]{:S(2)}, u32[]{:S(2)}) collective-permute-start(bf16[128,896]{1,0:T(8,128)(2,1)S(1)} %get-tuple-element.345), channel_id=1, source_target_pairs={{1,0},{0,1},{3,2},{2,3},{5,4},{4,5},{7,6},{6,7},{9,8},{8,9},{11,10... | collective-permute-start | bytes 688136 | tf_op jit(solution)/shard_map/ppermute | solution.py:28
  945.4 46.2 %collective-permute-start.73 = (bf16[256,896]{1,0:T(8,128)(2,1)S(1)}, bf16[256,896]{1,0:T(8,128)(2,1)S(1)}, u32[]{:S(2)}, u32[]{:S(2)}) collective-permute-start(bf16[256,896]{1,0:T(8,128)(2,1)S(1)} %pad_maximum_fusion.20.right_ref), channel_id=1, source_target_pairs={{0,4},{2,6},{4,0},{6,2},{8,12},{10,14},{12,8},{14,10},{16,20},{18,... | collective-permute-start | bytes 1376264 | tf_op jit(solution)/shard_map/ppermute | solution.py:88
  946.1 53.0 %collective-permute-start.76 = (bf16[256,896]{1,0:T(8,128)(2,1)S(1)}, bf16[256,896]{1,0:T(8,128)(2,1)S(1)}, u32[]{:S(2)}, u32[]{:S(2)}) collective-permute-start(bf16[256,896]{1,0:T(8,128)(2,1)S(1)} %pad_maximum_fusion.21.right_ref), channel_id=1, source_target_pairs={{0,4},{2,6},{4,0},{6,2},{8,12},{10,14},{12,8},{14,10},{16,20},{18,... | collective-permute-start | bytes 1376264 | tf_op jit(solution)/shard_map/ppermute | solution.py:88
  955.6 49.1 %collective-permute-start.79 = (bf16[256,896]{1,0:T(8,128)(2,1)S(1)}, bf16[256,896]{1,0:T(8,128)(2,1)S(1)}, u32[]{:S(2)}, u32[]{:S(2)}) collective-permute-start(bf16[256,896]{1,0:T(8,128)(2,1)S(1)} %pad_maximum_fusion.22.right_ref), channel_id=1, source_target_pairs={{0,4},{2,6},{4,0},{6,2},{8,12},{10,14},{12,8},{14,10},{16,20},{18,... | collective-permute-start | bytes 1376264 | tf_op jit(solution)/shard_map/ppermute | solution.py:88
  960.2 21.5 %collective-permute-start.65 = (f32[144,128]{1,0:T(8,128)S(1)}, f32[144,128]{1,0:T(8,128)S(1)}, u32[]{:S(2)}, u32[]{:S(2)}) collective-permute-start(f32[144,128]{1,0:T(8,128)S(1)} %fusion.102), channel_id=1, source_target_pairs={{0,4},{2,6},{4,0},{6,2},{8,12},{10,14},{12,8},{14,10},{16,20},{18,... | collective-permute-start | bytes 221192 | tf_op jit(solution)/shard_map/ppermute | solution.py:478
  968.1 45.8 %collective-permute-start.84 = (bf16[100,512]{1,0:T(8,128)(2,1)}, bf16[100,512]{1,0:T(8,128)(2,1)}, u32[]{:S(2)}, u32[]{:S(2)}) collective-permute-start(bf16[100,512]{1,0:T(8,128)(2,1)} %slice.500), channel_id=1, source_target_pairs={{0,16},{2,18},{4,20},{6,22},{8,24},{10,26},{12,28},{14,30},{16,0},... | collective-permute-start | bytes 307208 | tf_op jit(solution)/shard_map/ppermute | solution.py:88
  986.8 24.6 %collective-permute-start.67 = (f32[144,128]{1,0:T(8,128)}, f32[144,128]{1,0:T(8,128)}, u32[]{:S(2)}, u32[]{:S(2)}) collective-permute-start(f32[144,128]{1,0:T(8,128)} %add.581), channel_id=1, source_target_pairs={{0,16},{2,18},{4,20},{6,22},{8,24},{10,26},{12,28},{14,30},{16,0},... | collective-permute-start | bytes 221192 | tf_op jit(solution)/shard_map/ppermute | solution.py:478
  997.0 21.8 %collective-permute-start.74 = (bf16[200,896]{1,0:T(8,128)(2,1)}, bf16[200,896]{1,0:T(8,128)(2,1)}, u32[]{:S(2)}, u32[]{:S(2)}) collective-permute-start(bf16[200,896]{1,0:T(8,128)(2,1)} %get-tuple-element.167), channel_id=1, source_target_pairs={{0,8},{2,10},{4,12},{6,14},{8,0},{10,2},{12,4},{14,6},{16,24},{18,... | collective-permute-start | bytes 1075208 | tf_op jit(solution)/shard_map/ppermute | solution.py:88
  1020.1 20.6 %collective-permute-start.75 = (bf16[100,896]{1,0:T(8,128)(2,1)S(1)}, bf16[100,896]{1,0:T(8,128)(2,1)S(1)}, u32[]{:S(2)}, u32[]{:S(2)}) collective-permute-start(bf16[100,896]{1,0:T(8,128)(2,1)S(1)} %slice.494), channel_id=1, source_target_pairs={{0,16},{2,18},{4,20},{6,22},{8,24},{10,26},{12,28},{14,30},{16,0},... | collective-permute-start | bytes 537608 | tf_op jit(solution)/shard_map/ppermute | solution.py:88
  1021.3 23.3 %collective-permute-start.78 = (bf16[100,896]{1,0:T(8,128)(2,1)S(1)}, bf16[100,896]{1,0:T(8,128)(2,1)S(1)}, u32[]{:S(2)}, u32[]{:S(2)}) collective-permute-start(bf16[100,896]{1,0:T(8,128)(2,1)S(1)} %slice.496), channel_id=1, source_target_pairs={{0,16},{2,18},{4,20},{6,22},{8,24},{10,26},{12,28},{14,30},{16,0},... | collective-permute-start | bytes 537608 | tf_op jit(solution)/shard_map/ppermute | solution.py:88
  1026.1 20.6 %collective-permute-start.81 = (bf16[100,896]{1,0:T(8,128)(2,1)S(1)}, bf16[100,896]{1,0:T(8,128)(2,1)S(1)}, u32[]{:S(2)}, u32[]{:S(2)}) collective-permute-start(bf16[100,896]{1,0:T(8,128)(2,1)S(1)} %slice.498), channel_id=1, source_target_pairs={{0,16},{2,18},{4,20},{6,22},{8,24},{10,26},{12,28},{14,30},{16,0},... | collective-permute-start | bytes 537608 | tf_op jit(solution)/shard_map/ppermute | solution.py:88
  (257 other events, 2997.9 us)
Sparse Core Ops, SparseCore 0:
  754.4 149.2 all-reduce.8

commit v2 on v1

--- a/solution.py
+++ b/solution.py
@@ -1,3 +1,5 @@
+import functools
+
 import jax
 import jax.numpy as jnp
 from jax import lax
@@ -76,11 +78,17 @@
     return total
 
 
-def own_columns_sum(value):
+def own_columns_sums(values):
     count = lax.axis_size("wt")
     place = lax.axis_index("wt")
-    owners = cut_evenly(value, 1)
-    return sum(swapped([picked(owners, (place + k) % count) for k in range(count)]))
+    widths = [value.shape[1] // count for value in values]
+    owners = [jnp.concatenate(parts, axis=1) for parts in zip(*(cut_evenly(value, 1) for value in values))]
+    total = sum(swapped([picked(owners, (place + k) % count) for k in range(count)]))
+    return [total[:, sum(widths[:i]) : sum(widths[: i + 1])] for i in range(len(widths))]
+
+
+def taking(microseconds):
+    return pl.CostEstimate(flops=0, transcendentals=0, bytes_accessed=microseconds * 30_000)
 
 
 def seq_swap(block, bit):
@@ -88,65 +96,75 @@
     return lax.ppermute(block, "seq", [(i, i ^ (1 << bit)) for i in range(count)])
 
 
-def features_first(value):
-    count = lax.axis_size("seq")
-    return value.T.reshape(count, value.shape[1] // count, value.shape[0])
-
-
 def reversed_bits(value, bits):
     return sum(((value >> bit) & 1) << (bits - 1 - bit) for bit in range(bits))
 
 
-def arrange_kernel(place_ref, left_ref, own_ref, across_ref, beside_ref, taken_ref):
-    count, group, _ = left_ref.shape
+def arrange_kernel(turned, pieces, place_ref, left_ref, own_ref, across_ref, beside_ref, groups_ref, taken_ref):
+    count, _, _ = groups_ref.shape
     bits = count.bit_length() - 1
+    left = left_ref[...].astype(f32)
+    left = left.T if turned else left
+    group = left.shape[0] // count
     for r in range(count):
-        taken_ref[r * group : (r + 1) * group, :] = left_ref[place_ref[0] ^ reversed_bits(r, bits)].astype(f32)
-    quarter = own_ref.shape[0]
+        groups_ref[r, :group, :] = left[r * group : (r + 1) * group]
+    quarter, unit = own_ref.shape[0], group // pieces
+    for r in range(count):
+        for piece in range(pieces):
+            begin = r // (count // 4) * quarter + piece * (quarter // pieces) + r % (count // 4) * unit
+            taken_ref[begin : begin + unit, :] = groups_ref[
+                place_ref[0] ^ reversed_bits(r, bits), piece * unit : (piece + 1) * unit, :
+            ]
     own_ref[...] = taken_ref[:quarter].astype(bf16)
     across_ref[:quarter] = taken_ref[quarter : 2 * quarter].astype(bf16)
     across_ref[quarter:] = taken_ref[3 * quarter :].astype(bf16)
     beside_ref[...] = taken_ref[2 * quarter : 3 * quarter].astype(bf16)
 
 
-def shared_features(left):
-    count, group, tokens = left.shape
-    quarter = count * group // 4
+def shared_features(left, model, turned=True, order=()):
+    count = lax.axis_size("seq")
+    tokens, features = left.shape if turned else left.shape[::-1]
+    quarter = features // 4
     place = lax.axis_index("seq").astype(jnp.int32).reshape(1)
-    whole = lambda rows: pl.BlockSpec((rows, tokens), lambda i, place: (0, 0))
-    sizes = [quarter, 2 * quarter, quarter]
+    whole = lambda shape: pl.BlockSpec(shape, lambda i, place: (0, 0))
+    shapes = [(quarter, tokens), (2 * quarter, tokens), (quarter, tokens)]
     own, across, beside = pl.pallas_call(
-        arrange_kernel,
+        ignoring(functools.partial(arrange_kernel, turned, features // model), 2, len(order)),
         grid_spec=pltpu.PrefetchScalarGridSpec(
             num_scalar_prefetch=1,
             grid=(1,),
-            in_specs=[pl.BlockSpec((count, group, tokens), lambda i, place: (0, 0, 0))],
-            out_specs=[whole(size) for size in sizes],
-            scratch_shapes=[pltpu.VMEM((count * group, tokens), f32)],
+            in_specs=[whole(left.shape)] + [pl.BlockSpec(memory_space=pl.ANY)] * len(order),
+            out_specs=[whole(shape) for shape in shapes],
+            scratch_shapes=[
+                pltpu.VMEM((count, -(-features // count // 8) * 8, tokens), f32),
+                pltpu.VMEM((features, tokens), f32),
+            ],
         ),
-        out_shape=[jax.ShapeDtypeStruct((size, tokens), bf16) for size in sizes],
-        compiler_params=pltpu.CompilerParams(vmem_limit_bytes=24 * 2**20),
-        cost_estimate=pl.CostEstimate(flops=0, transcendentals=0, bytes_accessed=8 * quarter * tokens * 2),
+        out_shape=[jax.ShapeDtypeStruct(shape, bf16) for shape in shapes],
+        compiler_params=pltpu.CompilerParams(vmem_limit_bytes=32 * 2**20),
+        cost_estimate=taking(2),
         name="arrange",
-    )(place, left)
+    )(place, left, *order)
     return own, beside, seq_swap(across, 1)
 
 
-def quarter_kernel(
-    own_ref, beside_ref, across_ref, right_ref, right_across_ref, keep_ref, send_ref, left_in, right_in, total, sent, got
-):
-    quarter, columns = total.shape
+def quarter_kernel(parts, counts, *refs):
+    lefts = [refs[3 * i : 3 * i + 3] for i in range(counts[0])]
+    rights = [refs[3 * counts[0] + 2 * i :][:2] for i in range(counts[1])]
+    keep_ref, send_ref, *scratch = refs[3 * counts[0] + 2 * counts[1] :]
+    lefts_in, rights_in = scratch[: counts[0]], scratch[counts[0] : sum(counts)]
+    total, sent, got = scratch[sum(counts) :]
     place = lax.axis_index("seq")
     partner = {"seq": place + 1 - 2 * (place % 2)}
     barrier = pltpu.get_barrier_semaphore()
     pl.semaphore_signal(barrier, inc=1, device_id=partner, device_id_type=pl.DeviceIdType.MESH)
     pl.semaphore_wait(barrier, 1)
-    moves = [
-        (right_ref, right_in.at[0]),
-        (right_across_ref, right_in.at[1]),
-        (beside_ref, left_in.at[0]),
-        (across_ref.at[pl.ds(quarter, quarter)], left_in.at[1]),
-    ]
+    moves = []
+    for (right, across), arrived in zip(rights, rights_in):
+        moves += [(right, arrived.at[0]), (across, arrived.at[1])]
+    for (own, beside, across), arrived in zip(lefts, lefts_in):
+        rows = own.shape[0]
+        moves += [(beside, arrived.at[0]), (across.at[pl.ds(rows, rows)], arrived.at[1])]
     copies = [
         pltpu.make_async_remote_copy(
             src_ref=source,
@@ -160,46 +178,64 @@
     ]
     for copy in copies:
         copy.start()
-    chunks = [slice(at, min(at + 512, columns)) for at in range(0, columns, 512)]
-    for chunk in chunks:
-        total[:, chunk] = jnp.dot(
-            own_ref[...], right_ref[:, chunk], preferred_element_type=f32
-        ) + jnp.dot(across_ref[:quarter], right_across_ref[:, chunk], preferred_element_type=f32)
+    unit = total.shape[0]
+    pieces = []
+    begin = 0
+    for left, right, at in parts:
+        columns = rights[right][0].shape[2]
+        for piece in range(lefts[left][0].shape[0] // unit):
+            rows = slice(piece * unit, (piece + 1) * unit)
+            for first in range(0, columns, 512):
+                chunk = slice(first, min(first + 512, columns))
+                pieces.append((left, right, at, rows, chunk, slice(begin + chunk.start, begin + chunk.stop)))
+            if columns % LANES:
+                blank = slice(begin + columns, begin + -(-columns // LANES) * LANES)
+                keep_ref[:, blank] = jnp.zeros((unit // 2, blank.stop - blank.start), bf16)
+                send_ref[:, blank] = jnp.zeros((unit // 2, blank.stop - blank.start), bf16)
+            begin += -(-columns // LANES) * LANES
+    for left, right, at, rows, chunk, out in pieces:
+        total[:, out] = jnp.dot(
+            lefts[left][0][rows], rights[right][0][at, :, chunk], preferred_element_type=f32
+        ) + jnp.dot(lefts[left][2][rows], rights[right][1][at, :, chunk], preferred_element_type=f32)
     for copy in copies:
         copy.wait()
-    half = quarter // 2
-    for chunk in chunks:
+    for left, right, at, rows, chunk, out in pieces:
         result = (
-            total[:, chunk]
-            + jnp.dot(left_in[0], right_in[0, :, chunk], preferred_element_type=f32)
-            + jnp.dot(left_in[1], right_in[1, :, chunk], preferred_element_type=f32)
+            total[:, out]
+            + jnp.dot(lefts_in[left][0, rows], rights_in[right][0, at, :, chunk], preferred_element_type=f32)
+            + jnp.dot(lefts_in[left][1, rows], rights_in[right][1, at, :, chunk], preferred_element_type=f32)
         )
-        keep_ref[:, chunk] = result[:half].astype(bf16)
-        send_ref[:, chunk] = result[half:].astype(bf16)
-
-
-def quarter_gradient(left, right, collective):
-    rows, tokens = left[0].shape
-    columns = right[0].shape[1]
+        keep_ref[:, out] = result[: unit // 2].astype(bf16)
+        send_ref[:, out] = result[unit // 2 :].astype(bf16)
+
+
+def quarter_gradient(lefts, rights, parts, collective, order=()):
+    unit = min(left[0].shape[0] for left in lefts)
+    columns = sum(
+        lefts[left][0].shape[0] // unit * -(-rights[right][0].shape[2] // LANES) * LANES
+        for left, right, _ in parts
+    )
     vmem = pl.BlockSpec(memory_space=pltpu.VMEM)
+    counts = (len(lefts), len(rights))
+    inputs = [array for group in lefts + rights for array in group]
     return pl.pallas_call(
-        quarter_kernel,
-        in_specs=[vmem] * 5,
+        ignoring(functools.partial(quarter_kernel, parts, counts), len(inputs), len(order)),
+        in_specs=[vmem] * len(inputs) + [pl.BlockSpec(memory_space=pl.ANY)] * len(order),
         out_specs=[vmem] * 2,
-        out_shape=[jax.ShapeDtypeStruct((rows // 2, columns), bf16)] * 2,
-        scratch_shapes=[
-            pltpu.VMEM((2, rows, tokens), bf16),
-            pltpu.VMEM((2, tokens, columns), bf16),
-            pltpu.VMEM((rows, columns), f32),
-            pltpu.SemaphoreType.DMA((4,)),
-            pltpu.SemaphoreType.DMA((4,)),
+        out_shape=[jax.ShapeDtypeStruct((unit // 2, columns), bf16)] * 2,
+        scratch_shapes=[pltpu.VMEM((2,) + left[0].shape, bf16) for left in lefts]
+        + [pltpu.VMEM((2,) + right[0].shape, bf16) for right in rights]
+        + [
+            pltpu.VMEM((unit, columns), f32),
+            pltpu.SemaphoreType.DMA((2 * sum(counts),)),
+            pltpu.SemaphoreType.DMA((2 * sum(counts),)),
         ],
         compiler_params=pltpu.CompilerParams(
-            vmem_limit_bytes=40 * 2**20, collective_id=collective, has_side_effects=True
+            vmem_limit_bytes=56 * 2**20, collective_id=collective, has_side_effects=True
         ),
-        cost_estimate=pl.CostEstimate(flops=0, transcendentals=0, bytes_accessed=1 << 20),
+        cost_estimate=taking(columns // 320),
         name="gradient",
-    )(*left, *right)
+    )(*inputs, *order)
 
 
 def added(keep, received):
@@ -208,9 +244,14 @@
     return total[:half].astype(bf16), total[half:].astype(bf16)
 
 
+def shared_rows(right):
+    return right, seq_swap(right, 1)
+
+
 class Gradient:
-    def __init__(self, left, right, collective):
-        self.left, self.right, self.collective = left, (right, seq_swap(right, 1)), collective
+    def __init__(self, lefts, rights, parts, collective, order=()):
+        self.lefts, self.parts, self.collective, self.order = lefts, parts, collective, order
+        self.rights = [right if isinstance(right, tuple) else shared_rows(right) for right in rights]
         self.bits = lax.axis_size("seq").bit_length() - 1
         self.bit = 2
         self.total = None
@@ -221,40 +262,52 @@
 
     def finish(self):
         if self.bit == 2:
-            self.keep, self.send = quarter_gradient(self.left, self.right, self.collective)
+            self.keep, self.send = quarter_gradient(
+                self.lefts, self.rights, self.parts, self.collective, self.order
+            )
         elif self.bit < self.bits:
             self.keep, self.send = added(self.keep, self.received)
         else:
             self.total = self.keep.astype(f32) + self.received.astype(f32)
 
-    def state(self):
-        return (self.keep, self.send) if self.total is None else self.total
-
-    def set_state(self, state):
-        if self.total is None:
-            self.keep, self.send = state
-        else:
-            self.total = state
-
-
-def advance(chain, gradients):
-    for gradient in gradients:
-        gradient.finish()
-    chain, states = lax.optimization_barrier((chain, [g.state() for g in gradients]))
-    for gradient, state in zip(gradients, states):
-        gradient.set_state(state)
-        if gradient.total is None:
-            gradient.start()
-    return chain
+    def results(self):
+        unit = min(left[0].shape[0] for left in self.lefts)
+        found, begin = [], 0
+        for left, right, _ in self.parts:
+            columns = self.rights[right][0].shape[2]
+            blocks = []
+            for _ in range(self.lefts[left][0].shape[0] // unit):
+                blocks.append(self.total[:, begin : begin + columns])
+                begin += -(-columns // LANES) * LANES
+            found.append(blocks[0] if len(blocks) == 1 else jnp.concatenate(blocks, axis=0))
+        return found
+
+
+def after(value, *others):
+    for other in others:
+        value = value + (other.reshape(-1)[0] * 0).astype(value.dtype)
+    return value
+
+
+def finished(gradient):
+    gradient.finish()
+    arrays = [gradient.total] if gradient.total is not None else [gradient.keep, gradient.send]
+    if gradient.total is None:
+        gradient.start()
+    return arrays
+
+
+def ignoring(body, used, unused):
+    return lambda *refs: body(*refs[:used], *refs[used + unused :])
 
 
 def completed_all(gradients):
     while any(gradient.total is None for gradient in gradients):
         for gradient in gradients:
-            gradient.finish()
             if gradient.total is None:
-                gradient.start()
-    return [gradient.total for gradient in gradients]
+                gradient.finish()
+                if gradient.total is None:
+                    gradient.start()
 
 
 def column_chunks(value, chunks):
@@ -265,14 +318,6 @@
         to_own_columns(jnp.concatenate([owner[:, at : at + piece] for owner in owners], axis=1))
         for at in range(0, width, piece)
     ]
-
-
-def completed(gradient):
-    while gradient.total is None:
-        gradient.finish()
-        if gradient.total is None:
-            gradient.start()
-    return gradient.total
 
 
 def lane_blocks(inner):
@@ -424,7 +469,7 @@
     decay_back_ref[...] = jnp.concatenate(total, axis=1)
 
 
-def scan_call(body, name, token_args, wide_args, state_args, outs, scratch=False, flops=0):
+def scan_call(body, name, token_args, wide_args, state_args, outs, scratch=False, flops=0, order=()):
     rows, inner = token_args[0].shape
     states = state_args[0].shape[0]
     width = lane_blocks(inner) * LANES
@@ -438,51 +483,119 @@
     }
     size = rows * states * inner
     results = pl.pallas_call(
-        body,
+        ignoring(body, len(token_args) + len(wide_args) + len(state_args), len(order)),
         grid=(inner // width,),
-        in_specs=[token] * len(token_args) + [wide] * len(wide_args) + [state] * len(state_args),
+        in_specs=[token] * len(token_args)
+        + [wide] * len(wide_args)
+        + [state] * len(state_args)
+        + [pl.BlockSpec(memory_space=pl.ANY)] * len(order),
         out_specs=[kinds[k][0] for k in outs],
         out_shape=[kinds[k][1] for k in outs],
         scratch_shapes=[pltpu.VMEM((rows, states, width), f32)] if scratch else [],
         compiler_params=pltpu.CompilerParams(vmem_limit_bytes=40 * 2**20),
-        cost_estimate=pl.CostEstimate(flops=0, transcendentals=0, bytes_accessed=flops << 18),
+        cost_estimate=taking(flops * 3 // 2),
         name=name,
-    )(*[arg.reshape(rows // 8, 8, inner) for arg in token_args], *wide_args, *state_args)
+    )(*[arg.reshape(rows // 8, 8, inner) for arg in token_args], *wide_args, *state_args, *order)
     return [r.reshape(rows, inner) if k == "token" else r for k, r in zip(outs, results)]
 
 
-def entering(total, part, rate, reverse):
+def entering_kernel(sign, hops, total_ref, part_ref, rate_ref, out_ref, totals, parts, totals_in, parts_in, sent, got):
     count = lax.axis_size("seq")
-    sign = -1 if reverse else 1
-    packed = jnp.concatenate([total[None], part], axis=0)
-    near = passed_along(packed, "seq", sign)
-    far = passed_along(packed, "seq", 2 * sign)
-    total, part = near[0] + far[0], jnp.exp2(near[0] * rate) * far[1:] + near[1:]
-    distance = 2
-    while distance < count:
-        received = passed_along(jnp.concatenate([total[None], part], axis=0), "seq", distance * sign)
-        part = jnp.exp2(total * rate) * received[1:] + part
-        total = total + received[0]
-        distance *= 2
-    return part
-
-
-def summed_everywhere(parts):
-    sizes = [part.size for part in parts]
-    packed = jnp.concatenate([part.reshape(-1) for part in parts])
-    packed = jnp.pad(packed, (0, -packed.size % 1024)).reshape(-1, 128)
-    for axis in ("seq", "wt"):
+    place = lax.axis_index("seq")
+    barrier = pltpu.get_barrier_semaphore()
+    reaches = sorted({distance for _, distance in hops})
+    for distance in reaches:
+        pl.semaphore_signal(
+            barrier,
+            inc=1,
+            device_id={"seq": (place + count - sign * distance) % count},
+            device_id_type=pl.DeviceIdType.MESH,
+        )
+    pl.semaphore_wait(barrier, len(reaches))
+
+    def send(turn):
+        buffer, distance = hops[turn]
+        copies = [
+            pltpu.make_async_remote_copy(
+                src_ref=source,
+                dst_ref=target,
+                send_sem=sent.at[turn, i],
+                recv_sem=got.at[turn, i],
+                device_id={"seq": (place + count + sign * distance) % count},
+                device_id_type=pl.DeviceIdType.MESH,
+            )
+            for i, (source, target) in enumerate(
+                [(totals.at[buffer], totals_in.at[turn]), (parts.at[buffer], parts_in.at[turn])]
+            )
+        ]
+        for copy in copies:
+            copy.start()
+        return copies
+
+    def joined(near, far):
+        (total, part), (far_total, far_part) = near, far
+        passed = [
+            jnp.exp2(total[k : k + 1] * rate_ref[:, k * LANES : (k + 1) * LANES])
+            for k in range(total.shape[0])
+        ]
+        return total + far_total, jnp.concatenate(passed, axis=1) * far_part + part
+
+    def received(turn, copies):
+        for copy in copies:
+            copy.wait()
+        distance = hops[turn][1]
+        there = place >= distance if sign > 0 else place < count - distance
+        return jnp.where(there, totals_in[turn], 0.0), jnp.where(there, parts_in[turn].astype(f32), 0.0)
+
+    totals[0] = total_ref[...]
+    parts[0] = part_ref[...].astype(bf16)
+    first = [send(0), send(1)]
+    state = joined(received(0, first[0]), received(1, first[1]))
+    for turn in range(2, len(hops)):
+        buffer = hops[turn][0]
+        totals[buffer] = state[0]
+        parts[buffer] = state[1].astype(bf16)
+        state = joined(state, received(turn, send(turn)))
+    out_ref[...] = state[1]
+
+
+def entering(total, part, rate, reverse, order):
+    count = lax.axis_size("seq")
+    states, inner = part.shape
+    total = total.reshape(-1, LANES)
+    hops = [(0, 1), (0, 2)] + [(bit, 1 << bit) for bit in range(1, count.bit_length() - 1)]
+    buffers = len(hops) - 1
+    vmem = pl.BlockSpec(memory_space=pltpu.VMEM)
+    return pl.pallas_call(
+        ignoring(functools.partial(entering_kernel, -1 if reverse else 1, hops), 3, len(order)),
+        in_specs=[vmem] * 3 + [pl.BlockSpec(memory_space=pl.ANY)] * len(order),
+        out_specs=vmem,
+        out_shape=jax.ShapeDtypeStruct(part.shape, f32),
+        scratch_shapes=[
+            pltpu.VMEM((buffers,) + total.shape, f32),
+            pltpu.VMEM((buffers, states, inner), bf16),
+            pltpu.VMEM((len(hops),) + total.shape, f32),
+            pltpu.VMEM((len(hops), states, inner), bf16),
+            pltpu.SemaphoreType.DMA((len(hops), 2)),
+            pltpu.SemaphoreType.DMA((len(hops), 2)),
+        ],
+        compiler_params=pltpu.CompilerParams(
+            vmem_limit_bytes=24 * 2**20, collective_id=10 if reverse else 9, has_side_effects=True
+        ),
+        cost_estimate=taking(24),
+        name="entering",
+    )(total, part, rate, *order)
+
+
+def summed_everywhere(values):
+    for axis in ("wt", "seq"):
         count = lax.axis_size(axis)
         bit = 1
         while bit < count:
-            packed = packed + lax.ppermute(packed, axis, [(i, i ^ bit) for i in range(count)])
+            received = lax.ppermute(values, axis, [(i, i ^ bit) for i in range(count)])
+            values = (values.astype(f32) + received.astype(f32)).astype(values.dtype)
             bit *= 2
-    packed = packed.reshape(-1)
-    result, begin = [], 0
-    for part, size in zip(parts, sizes):
-        result.append(packed[begin : begin + size].reshape(part.shape))
-        begin += size
-    return result
+    return values
 
 
 def product(left, right):
@@ -525,46 +638,52 @@
     return raised * (1.0 / jnp.sum(raised, axis=0, keepdims=True))
 
 
-def attend_kernel(query_ref, keys_ref, values_ref, bias_ref, out_ref):
+def attend_kernel(query_ref, near_ref, bias_ref, out_ref):
     query = heads_beside(query_ref[...]) * bf16(0.125)
-    chances = chance_table(query, keys_ref[...], bias_ref[...]).astype(bf16)
-    store_heads(out_ref, jnp.dot(values_ref[...], chances, preferred_element_type=f32))
-
-
-def attend_back_kernel(query_ref, keys_ref, values_ref, back_ref, bias_ref, query_back_ref, keys_back_ref, values_back_ref):
+    chances = chance_table(query, near_ref[0], bias_ref[...]).astype(bf16)
+    store_heads(out_ref, jnp.dot(near_ref[1], chances, preferred_element_type=f32))
+
+
+def attend_back_kernel(query_ref, near_ref, back_ref, bias_ref, query_back_ref, kept_ref, sent_ref):
     query = heads_beside(query_ref[...]) * bf16(0.125)
     back = heads_beside(back_ref[...])
-    weights = chance_table(query, keys_ref[...], bias_ref[...])
-    values_back_ref[...] = right_product(back, weights.astype(bf16))
-    delta = transposed_dot(values_ref[...], back)
+    weights = chance_table(query, near_ref[0], bias_ref[...])
+    values_back = right_product(back, weights.astype(bf16))
+    delta = transposed_dot(near_ref[1], back)
     weighted = weights * delta
     scores_back = (weighted - weights * jnp.sum(weighted, axis=0, keepdims=True)).astype(bf16)
-    store_heads(query_back_ref, jnp.dot(keys_ref[...], scores_back, preferred_element_type=f32) * 0.125)
-    keys_back_ref[...] = right_product(query, scores_back)
-
-
-def attention_call(body, name, wide, near, bias, outs, flops):
+    store_heads(query_back_ref, jnp.dot(near_ref[0], scores_back, preferred_element_type=f32) * 0.125)
+    half = kept_ref.shape[2]
+    for place, near_back in enumerate((right_product(query, scores_back), values_back)):
+        kept_ref[place] = near_back[:, :half]
+        sent_ref[place] = near_back[:, half:].astype(bf16)
+
+
+def attention_call(body, name, wide, near, bias, outs, flops, order=()):
     span, rows = bias.shape
-    key_heads = near[0].shape[0] // HEAD_SIZE
+    key_heads = near.shape[1] // HEAD_SIZE
     width = wide[0].shape[0] // key_heads
     wide_spec = pl.BlockSpec((width, rows), lambda k: (k, 0))
-    near_spec = pl.BlockSpec((HEAD_SIZE, span), lambda k: (k, 0))
+    near_spec = lambda size: pl.BlockSpec((2, HEAD_SIZE, size), lambda k: (0, k, 0))
+    half = near.shape[:2] + (span // 2,)
     kinds = {
         "wide": (wide_spec, jax.ShapeDtypeStruct(wide[0].shape, bf16)),
-        "near": (near_spec, jax.ShapeDtypeStruct(near[0].shape, f32)),
+        "kept": (near_spec(span // 2), jax.ShapeDtypeStruct(half, f32)),
+        "sent": (near_spec(span // 2), jax.ShapeDtypeStruct(half, bf16)),
     }
-    size = key_heads * span * rows * (width // HEAD_SIZE)
     return pl.pallas_call(
-        body,
+        ignoring(body, len(wide) + 2, len(order)),
         grid=(key_heads,),
-        in_specs=[wide_spec] + [near_spec] * 2 + [wide_spec] * (len(wide) - 1)
-        + [pl.BlockSpec((span, rows), lambda k: (0, 0))],
+        in_specs=[wide_spec, near_spec(span)]
+        + [wide_spec] * (len(wide) - 1)
+        + [pl.BlockSpec((span, rows), lambda k: (0, 0))]
+        + [pl.BlockSpec(memory_space=pl.ANY)] * len(order),
         out_specs=[kinds[k][0] for k in outs],
         out_shape=[kinds[k][1] for k in outs],
         compiler_params=pltpu.CompilerParams(vmem_limit_bytes=56 * 2**20),
-        cost_estimate=pl.CostEstimate(flops=0, transcendentals=0, bytes_accessed=flops << 19),
+        cost_estimate=taking(flops * 4),
         name=name,
-    )(wide[0], *near, *wide[1:], bias)
+    )(wide[0], near, *wide[1:], bias, *order)
 
 
 def outer_product(left, right):
@@ -592,17 +711,79 @@
     return in_order([turned] + [from_ahead(turned, k) for k in range(1, count)], 0)
 
 
-def feed_block(second_rows, back_rows, gate_cols, up_cols, down_cols):
-    gate_raw = product(second_rows, gate_cols)
-    up_raw = product(second_rows, up_cols)
-    sigma_gate = jax.nn.sigmoid(gate_raw)
-    activated = (gate_raw * sigma_gate * up_raw).astype(jnp.bfloat16)
-    feed_out = right_product(activated, down_cols)
-    delta_act = product(back_rows, down_cols)
-    delta_gate = (delta_act * up_raw * silu_slope(gate_raw)).astype(jnp.bfloat16)
-    delta_up = (delta_act * gate_raw * sigma_gate).astype(jnp.bfloat16)
-    delta_second = right_product(delta_gate, gate_cols) + right_product(delta_up, up_cols)
-    return (feed_out, delta_second, activated, delta_gate, delta_up)
+def feed_kernel(
+    columns,
+    second_ref,
+    back_ref,
+    gate_ref,
+    up_ref,
+    down_ref,
+    out_ref,
+    second_back_ref,
+    activated_ref,
+    hidden_back_ref,
+    out_sum,
+    second_back_sum,
+):
+    width = gate_ref.shape[1]
+    step, last = pl.program_id(0), pl.num_programs(0) - 1
+
+    def part(width, begin):
+        gate, up, down = (ref[:, :width] for ref in (gate_ref, up_ref, down_ref))
+        gate_raw = product(second_ref[...], gate)
+        up_raw = product(second_ref[...], up)
+        act_back = product(back_ref[...], down)
+        sigma = jax.nn.sigmoid(gate_raw)
+        swish = gate_raw * sigma
+        activated = (swish * up_raw).astype(bf16)
+        gate_back = (act_back * up_raw * (sigma * (1.0 + gate_raw * (1.0 - sigma)))).astype(bf16)
+        up_back = (act_back * swish).astype(bf16)
+        activated_ref[:, :width] = activated
+        hidden_back_ref[0, :, :width] = gate_back
+        hidden_back_ref[1, :, :width] = up_back
+        out = right_product(down, activated)
+        second_back = right_product(gate, gate_back) + right_product(up, up_back)
+        if begin:
+            out_sum[...] = out
+            second_back_sum[...] = second_back
+        else:
+            out_sum[...] += out
+            second_back_sum[...] += second_back
+
+    pl.when(step == 0)(lambda: part(width, True))
+    pl.when((step > 0) & (step < last))(lambda: part(width, False))
+
+    @pl.when(step == last)
+    def _():
+        left = columns - (-(-columns // width) - 1) * width
+        part(left, False)
+        if left < width:
+            activated_ref[:, left:] = jnp.zeros((activated_ref.shape[0], width - left), bf16)
+            hidden_back_ref[:, :, left:] = jnp.zeros((2, activated_ref.shape[0], width - left), bf16)
+        out_ref[...] = out_sum[...].T
+        second_back_ref[...] = second_back_sum[...].T
+
+
+def feed_block(second, back, gate, up, down, order, width=512):
+    rows, model = second.shape
+    columns = gate.shape[1]
+    padded = -(-columns // LANES) * LANES
+    whole = pl.BlockSpec((rows, model), lambda i: (0, 0))
+    weight = pl.BlockSpec((model, width), lambda i: (0, i))
+    hidden = pl.BlockSpec((rows, width), lambda i: (0, i))
+    return pl.pallas_call(
+        ignoring(functools.partial(feed_kernel, columns), 5, len(order)),
+        grid=(-(-columns // width),),
+        in_specs=[whole, whole, weight, weight, weight]
+        + [pl.BlockSpec(memory_space=pl.ANY)] * len(order),
+        out_specs=[whole, whole, hidden, pl.BlockSpec((2, rows, width), lambda i: (0, 0, i))],
+        out_shape=[jax.ShapeDtypeStruct((rows, model), f32)] * 2
+        + [jax.ShapeDtypeStruct(shape, bf16) for shape in ((rows, padded), (2, rows, padded))],
+        scratch_shapes=[pltpu.VMEM((model, rows), f32)] * 2,
+        compiler_params=pltpu.CompilerParams(vmem_limit_bytes=48 * 2**20),
+        cost_estimate=taking(22),
+        name="feed",
+    )(second, back, gate, up, down, *order)
 
 
 def per_device(
@@ -644,25 +825,23 @@
     both_tokens = gather_tokens(tokens[0])
     select_full = gather_columns(select_weight)
     step_full = gather_columns(step_weight)
-    both_back = gather_tokens(cotangent[0])
     rank = step_full.shape[0]
     first_scale = inverse_norm(inputs)
     both_inputs = both_tokens.astype(jnp.float32)
     both_normed = (both_inputs * inverse_norm(both_inputs) * norm_gain).astype(jnp.bfloat16)
-    normed_shared = shared_features(features_first(both_normed))
-    back_shared = shared_features(features_first(both_back))
+    normed_shared = shared_features(both_normed, model)
     pairs = jnp.stack(
         [outer_product(weight, both_normed).astype(bf16) for weight in (key_weight, value_weight)]
     )
     pairs = to_own_tokens(pairs, 2, 1)
     entered = to_own_tokens(product(both_normed, input_weight).astype(jnp.bfloat16))
+    both_back = gather_tokens(after(cotangent[0], entered))
+    back_shared = shared_features(both_back, model)
     query = to_own_tokens(outer_product(query_weight, both_normed).astype(jnp.bfloat16), 1, 0)
     hops = -(-WINDOW // (4 * rows))
     near = jnp.concatenate(
         [pairs] + [passed_along(pairs, "seq", 4 * hop) for hop in range(1, hops + 1)], axis=2
     )
-    for bit in (1, 0):
-        near = jnp.concatenate([near, seq_swap(near, bit)], axis=2)
     seq_place = lax.axis_index("seq")
     block_places = jnp.stack(
         [(seq_place ^ other) - 4 * hop for other in (0, 2, 1, 3) for hop in range(hops + 1)]
@@ -676,13 +855,9 @@
     distance = start + jnp.arange(rows, dtype=jnp.int32)[None, :] - near_place[:, None]
     allowed = (distance >= 0) & (distance < WINDOW) & (segment[None, :] == near_segment[:, None])
     bias = jnp.where(allowed, 0.0, masked)
-    (attended,) = attention_call(attend_kernel, "attend", [query], [near[0], near[1]], bias, ["wide"], 2)
-    both_attended = gather_tokens(attended, 1)
-    attended_shared = shared_features(
-        both_attended.reshape(lax.axis_size("seq"), -1, both_attended.shape[1])
-    )
-    head_out = to_own_tokens(left_product(both_attended, head_weight).astype(bf16)).astype(f32)
     inner_rows = entered[:, :inner]
+    select_full = after(select_full, entered)
+    step_full = after(step_full, entered)
     gate_input = entered[:, inner:].astype(jnp.float32)
     before = passed_along(inner_rows[rows - kernel + 1 :], "seq", 1)
     extended = jnp.concatenate([before, inner_rows], axis=0).astype(jnp.float32)
@@ -701,9 +876,10 @@
         filtered = filtered + filter_weight[tap] * kept_rows
     smoothed = (filtered * jax.nn.sigmoid(filtered)).astype(jnp.bfloat16)
     scan_input_rows = smoothed.astype(jnp.float32)
-    smoothed_shared = shared_features(features_first(smoothed))
+    smoothed_shared = shared_features(smoothed, model)
     projected = right_product(smoothed, select_full)
     step_low = projected[:, :rank].astype(jnp.bfloat16)
+    step_low_shared = shared_rows(step_low[None])
     entry = projected[:, rank : rank + states]
     read = projected[:, rank + states :]
     unsquashed_step = product(step_low, step_full) + step_offset
@@ -717,17 +893,23 @@
     entry_wide = jnp.broadcast_to(entry[:, :, None], (rows, states, LANES))
     read_wide = jnp.broadcast_to(read[:, :, None], (rows, states, LANES))
     total = jnp.sum(size, axis=0)
-    (last,) = scan_call(state_kernel, "scan_state", [size, inject], [entry_wide], [rate], ["state"], flops=4)
-    begin_state = entering(total, last, rate, False)
+    (last,) = scan_call(state_kernel, "scan_state", [size, inject], [entry_wide], [rate], ["state"], flops=4, order=[normed_shared[2]])
+    for bit in (1, 0):
+        near = jnp.concatenate([near, seq_swap(near, bit)], axis=2)
+    (attended,) = attention_call(attend_kernel, "attend", [query], near, bias, ["wide"], 2, order=[back_shared[2]])
+    begin_state = entering(total, last, rate, False, [])
+    both_attended = gather_tokens(attended, 1)
+    attended_shared = shared_features(both_attended, model, turned=False)
+    head_out = to_own_tokens(left_product(both_attended, head_weight).astype(bf16)).astype(f32)
     (scanned,) = scan_call(
-        output_kernel, "scan_output", [size, inject], [entry_wide, read_wide], [rate, begin_state], ["token"], flops=6
+        output_kernel, "scan_output", [size, inject], [entry_wide, read_wide], [rate, begin_state], ["token"], flops=6, order=[both_back, attended, smoothed_shared[2], step_low_shared[1]]
     )
     scan_result_rows = scanned + direct_skip_weight * scan_input_rows
     sigma_input = jax.nn.sigmoid(gate_input)
     silu_input = gate_input * sigma_input
     gated = (scan_result_rows * silu_input).astype(jnp.bfloat16)
     both_gated = gather_tokens(gated)
-    gated_shared = shared_features(features_first(both_gated))
+    gated_shared = shared_features(both_gated, model)
     branch = to_own_tokens(product(both_gated, mixer_weight).astype(jnp.bfloat16)).astype(f32)
     head_scale = inverse_norm(head_out)
     branch_scale = inverse_norm(branch)
@@ -737,13 +919,15 @@
     second_scale = inverse_norm(hidden)
     second = (hidden * second_scale * feed_gain).astype(jnp.bfloat16)
     both_second = gather_tokens(second)
-    feed_part, second_part, activated, feed_gate, feed_up = feed_block(
-        both_second, both_back, gate_weight, up_weight, down_weight
-    )
-    second_shared = shared_features(features_first(both_second))
-    down = Gradient(back_shared, activated, 1)
-    gate = Gradient(second_shared, feed_gate, 1)
-    up = Gradient(second_shared, feed_up, 1)
+    feed_part, second_part, activated, hidden_back = feed_block(
+        both_second,
+        both_back,
+        gate_weight,
+        up_weight,
+        down_weight,
+        [attended_shared[2], gated_shared[2]],
+    )
+    second_shared = shared_features(both_second, model)
     delta_second = summed_tokens(second_part)
     feed_out = summed_tokens(feed_part)
     result = (hidden + feed_out).astype(jnp.bfloat16)
@@ -754,21 +938,58 @@
     state_sum = jnp.sum(half * branch * branch_scale, axis=0)
     delta_head = norm_back(head_out, head_scale, half * attend_gain).astype(jnp.bfloat16)
     delta_branch = norm_back(branch, branch_scale, half * state_gain).astype(jnp.bfloat16)
-    delta_head, delta_branch = advance((delta_head, delta_branch), [down])
-    both_delta_head = to_own_columns(delta_head)
-    both_delta_branch = to_own_columns(delta_branch)
-    head = Gradient(attended_shared, both_delta_head, 2)
-    mixer = Gradient(gated_shared, both_delta_branch, 3)
+    both_deltas = to_own_columns(jnp.stack([delta_head, delta_branch]), 1, 2)
+    both_delta_head, both_delta_branch = both_deltas[0], both_deltas[1]
     delta_gated = summed_tokens(right_product(both_delta_branch, mixer_weight))
     delta_attended = summed_tokens(right_product(head_weight, both_delta_head), 1).astype(bf16)
-    delta_query, key_near, value_near = attention_call(
-        attend_back_kernel, "attend_back", [query, delta_attended], [near[0], near[1]], bias, ["wide", "near", "near"], 5
-    )
-    delta_near = jnp.stack([key_near, value_near])
-    for bit in (0, 1):
-        half = delta_near.shape[2] // 2
-        received = seq_swap(delta_near[:, :, half:].astype(bf16), bit)
-        delta_near = delta_near[:, :, :half] + received.astype(f32)
+    delta_scan_output = delta_gated * silu_input
+    delta_gate = (delta_gated * scan_result_rows * silu_slope(gate_input)).astype(jnp.bfloat16)
+    skip_sum = jnp.sum(delta_scan_output * scan_input_rows, axis=0)
+    hidden_shared = shared_rows(hidden_back)
+    (first,) = scan_call(
+        adjoint_kernel,
+        "scan_adjoint",
+        [size, delta_scan_output],
+        [read_wide],
+        [rate],
+        ["state"],
+        flops=4,
+        order=[hidden_shared[1]],
+    )
+    end_state = entering(total, first, rate, True, [])
+    middle_sums = Gradient(
+        [second_shared, attended_shared, gated_shared],
+        [hidden_shared, both_deltas],
+        [(0, 0, 0), (0, 0, 1), (1, 1, 0), (2, 1, 1)],
+        2,
+        order=[end_state],
+    )
+    through, sized, entry_back, read_back, decay_acc = scan_call(
+        gradient_kernel,
+        "scan_gradient",
+        [size, inject, delta_scan_output],
+        [entry_wide, read_wide],
+        [rate, decay, begin_state, end_state],
+        ["token", "token", "wide", "wide", "state"],
+        scratch=True,
+        flops=20,
+        order=finished(middle_sums),
+    )
+    down = Gradient([back_shared], [after(activated, end_state)[None]], [(0, 0, 0)], 1, order=[through])
+    delta_query, delta_near, sent_near = attention_call(
+        attend_back_kernel,
+        "attend_back",
+        [query, delta_attended],
+        near,
+        bias,
+        ["wide", "kept", "sent"],
+        5,
+        order=[through],
+    )
+    delta_near = delta_near + seq_swap(sent_near, 0).astype(f32)
+    middle = delta_near.shape[2] // 2
+    received = seq_swap(delta_near[:, :, middle:].astype(bf16), 1)
+    delta_near = delta_near[:, :, :middle] + received.astype(f32)
     delta_pairs = delta_near[:, :, :rows]
     for hop in range(1, hops + 1):
         piece = delta_near[:, :, hop * rows : (hop + 1) * rows].astype(bf16)
@@ -782,24 +1003,7 @@
         ],
         axis=0,
     ).T
-    qkv_sums = Gradient(normed_shared, both_qkv, 4)
-    delta_scan_output = delta_gated * silu_input
-    delta_gate = (delta_gated * scan_result_rows * silu_slope(gate_input)).astype(jnp.bfloat16)
-    skip_sum = jnp.sum(delta_scan_output * scan_input_rows, axis=0)
-    (first,) = scan_call(adjoint_kernel, "scan_adjoint", [size, delta_scan_output], [read_wide], [rate], ["state"], flops=4)
-    end_state = entering(total, first, rate, True)
-    end_state = advance(end_state, [down, gate, up, head, mixer])
-    through, sized, entry_back, read_back, decay_acc = scan_call(
-        gradient_kernel,
-        "scan_gradient",
-        [size, inject, delta_scan_output],
-        [entry_wide, read_wide],
-        [rate, decay, begin_state, end_state],
-        ["token", "token", "wide", "wide", "state"],
-        scratch=True,
-        flops=20,
-    )
-    through, sized, decay_acc = advance((through, sized, decay_acc), [down, gate, up, head, mixer])
+    qkv_shared = shared_rows(both_qkv[None])
     decay_sum = decay_acc * decay
     delta_scan_input = delta_scan_output * direct_skip_weight + through * step
     delta_unsquashed_step = (sized + through * scan_input_rows) * jax.nn.sigmoid(unsquashed_step)
@@ -829,7 +1033,6 @@
     delta_inner = sum(jnp.pad(share[tap:], ((0, tap), (0, 0))) for tap, share in enumerate(shares))
     delta_inner = delta_inner + jnp.pad(arrived, ((rows - kernel + 1, 0), (0, 0)))
     delta_entered = jnp.concatenate([delta_inner.astype(jnp.bfloat16), delta_gate], axis=1)
-    delta_entered = advance(delta_entered, [up, head, mixer])
     both_entered = column_chunks(delta_entered, 4)
     widths = (query_weight.shape[1], key_weight.shape[1], value_weight.shape[1])
     cuts = (0, widths[0], widths[0] + widths[1], sum(widths))
@@ -839,25 +1042,51 @@
     delta_normed = summed_tokens(delta_normed)
     norm_sum = jnp.sum(delta_normed * inputs * first_scale, axis=0)
     delta_tokens = delta_hidden + norm_back(inputs, first_scale, delta_normed * norm_gain)
-    select_sums = Gradient(smoothed_shared, delta_projected, 5)
-    step_sums = Gradient(shared_features(features_first(raw_low)), step_low, 6)
+    raw_shared = shared_features(raw_low, model, order=[both_entered[0]])
+    late_sums = Gradient(
+        [normed_shared, smoothed_shared, raw_shared],
+        [qkv_shared, after(delta_projected, both_entered[0])[None], step_low_shared],
+        [(0, 0, 0), (1, 1, 0), (2, 2, 0)],
+        3,
+        order=[both_entered[0]],
+    )
+    middle_placed = finished(middle_sums)
     input_sums = [
-        Gradient(normed_shared, part, 7 if part.shape == both_entered[0].shape else 8) for part in both_entered
+        Gradient([normed_shared], [part[None]], [(0, 0, 0)], 4 if part.shape == both_entered[0].shape else 5, middle_placed)
+        for part in both_entered
     ]
-    qkv_gradient = completed(qkv_sums)
+    for gradient in input_sums:
+        finished(gradient)
+    input_placed = input_sums[-1].keep
+    late_sums.order = [input_placed]
+    completed_all(input_sums + [late_sums, down, middle_sums])
+    qkv_gradient, select_sum, step_sum = late_sums.results()
     query_gradient, key_gradient, value_gradient = (
         qkv_gradient[:, cuts[place] : cuts[place + 1]] for place in range(3)
     )
-    select_gradient = own_columns_sum(completed(select_sums))
-    step_gradient = own_columns_sum(completed(step_sums))
-    input_gradient = jnp.concatenate(completed_all(input_sums), axis=1)
-    down_gradient, gate_gradient, up_gradient, head_gradient, mixer_gradient = (
-        completed(gradient) for gradient in (down, gate, up, head, mixer)
-    )
-    feed_total, attend_total, state_total, skip_total, decay_total, offset_total = lax.psum(
-        (feed_sum, attend_sum, state_sum, skip_sum, decay_sum, offset_sum), ("seq", "wt")
-    )
-    norm_total, filter_total, bias_total = summed_everywhere((norm_sum, filter_sums, bias_sum))
+    select_gradient, step_gradient = own_columns_sums((select_sum, step_sum))
+    input_gradient = jnp.concatenate([gradient.results()[0] for gradient in input_sums], axis=1)
+    gate_gradient, up_gradient, head_gradient, mixer_gradient = middle_sums.results()
+    (down_gradient,) = down.results()
+    hidden_width = gate_weight.shape[1]
+    gate_gradient, up_gradient, down_gradient = (
+        gradient[:, :hidden_width] for gradient in (gate_gradient, up_gradient, down_gradient)
+    )
+    early = jnp.concatenate(
+        [
+            decay_sum,
+            filter_sums,
+            jnp.stack([bias_sum, offset_sum, skip_sum, jnp.concatenate([attend_sum, state_sum])]),
+            jnp.concatenate([feed_sum, norm_sum])[None],
+        ],
+        axis=0,
+    )
+    early_total = summed_everywhere(after(early, input_placed).astype(bf16)).astype(f32)
+    decay_total = early_total[:states]
+    filter_total = early_total[states : states + kernel]
+    bias_total, offset_total, skip_total, pair_total, last_total = early_total[states + kernel :]
+    attend_total, state_total = pair_total[:model], pair_total[model:]
+    feed_total, norm_total = last_total[:model], last_total[model:]
     return (
         result[None],
         delta_tokens[None],

time: 1070 us -> 823 us (0.77)
  Pallas kernels: 158 us -> 230 us
  local copies, waits for them, and re-layouts: 160 us -> 96 us
  waiting for transfers between devices: 332 us -> 270 us
  starting transfers between devices: 146 us -> 85.8 us
  matrix products: 85.8 us -> 42.4 us
  blocking collectives: 40.9 us -> 0 us
  other arithmetic: 116 us -> 84.2 us
  between operations: 17.4 us -> 6.28 us
    pallas_call x25 -> x23, Pallas kernels: 158 us -> 230 us  [the longest x7 68.9 us: quarter_gradient(): pl.pallas_call(ignoring(functools.partial(quarter_kernel, parts, counts),...]
    psum x1 -> x0, blocking collectives: 40.9 us -> none  [per_device(): lax.psum((feed_sum, attend_sum, state_sum, skip_sum, decay_sum, offset_su...]
    ppermute x47 -> x35, starting transfers between devices: 69 us -> 34.6 us  [seq_swap(): return lax.ppermute(block, 'seq', [(i, i ^ 1 << bit) for i in range(count)])]
    unnamed x466 -> x374, local copies, waits for them, and re-layouts: 68.2 us -> 35.1 us
    ppermute x16 -> x6, waiting for transfers between devices: 40.8 us -> 12.4 us  [passed_along(): return lax.ppermute(block, axis, route)]
    ppermute x47 -> x35, waiting for transfers between devices: 197 us -> 169 us  [seq_swap(): return lax.ppermute(block, 'seq', [(i, i ^ 1 << bit) for i in range(count)])]
    ppermute x16 -> x6, starting transfers between devices: 40.2 us -> 15.2 us  [passed_along(): return lax.ppermute(block, axis, route)]
    dot_general x7 -> x4, matrix products: 44 us -> 22.8 us  [product(): return jnp.dot(left, right, preferred_element_type=jnp.float32)]
  transfers between devices with their start and end apart: 97 -> 72, of which waited for: 39 -> 29; matrix products, arithmetic and copies ran while one was open for 30% -> 23% of each run, Pallas kernels for 15% -> 22%
where the time goes in v2:
time: 823 us; the launch traced here: 814 us
  waiting for transfers between devices  270 us (33%)
  Pallas kernels  230 us (28%)
  local copies, waits for them, and re-layouts  96 us (12%)
  starting transfers between devices  85.8 us (10%)
  other arithmetic  84.2 us (10%)
  matrix products  42.4 us (5%)
    ppermute x35, waiting for transfers between devices, seq_swap(): return lax.ppermute(block, 'seq', [(i, i ^ 1 << bit) for i in range(count)])  169 us
    pallas_call x7, Pallas kernels, quarter_gradient(): pl.pallas_call(ignoring(functools.partial(quarter_kernel, parts, counts),...  68.9 us
    ppermute x26, waiting for transfers between devices, from_ahead(): lax.ppermute(block, 'wt', [((i + distance) % count, i) for i in range(cou...  62.4 us
    pallas_call x4, Pallas kernels, scan_call(): pl.pallas_call(ignoring(body, len(token_args) + len(wide_args) + len(stat...  51.4 us
    pallas_call x2, Pallas kernels, entering(): pl.pallas_call(ignoring(functools.partial(entering_kernel, -1 if reverse...  49.3 us
    unnamed x374, local copies, waits for them, and re-layouts  35.1 us
    ppermute x35, starting transfers between devices, seq_swap(): return lax.ppermute(block, 'seq', [(i, i ^ 1 << bit) for i in range(count)])  34.6 us
    pallas_call x2, Pallas kernels, attention_call(): pl.pallas_call(ignoring(body, len(wide) + 2, len(order)), grid=(key_heads...  32.8 us
  transfers between devices with their start and end apart: 72, of which 29 were waited for; matrix products, arithmetic and copies ran while one was open for 23% of the time, Pallas kernels for 22%

profile of v2, /device:TPU:0, one launch (start us, length us, event | category | flops | bytes accessed | tf_op | source)
XLA Modules:
  0.0 814.4 jit_solution(9802590500091702292)
XLA Ops:
  0.7 3.0 collective-permute-start.14
  16.8 2.4 fusion.63.refs_2_.refs_3_
  30.6 7.2 convolution_convert_fusion
  39.8 3.5 collective-permute-start.3
  43.3 4.5 collective-permute-start.4
  53.5 7.6 collective-permute-done.5
  63.9 3.2 collective-permute-start.12
  68.4 4.5 reshape.729
  78.7 2.6 multiply_convert_fusion.1
  87.7 2.7 convolution_add_fusion
  97.4 2.3 select_reduce_fusion
  100.2 6.2 scan_state.1.refs_1_
  106.4 24.1 %entering.2.refs_5_.refs_7_ = f32[16,3200]{1,0:T(8,128)S(1)} custom-call(f32[25,128]{1,0:T(8,128)S(1)} %bitcast.154, f32[16,3200]{1,0:T(8,128)S(1)} %scan_state.1.refs_1_, f32[16,3200]{1,0:T(8,128)S(1)} %copy-done.20), custom_call_target="tpu_custom_call" | custom-call | bytes 720000 | tf_op jit(solution)/shard_map/entering/pallas_call | solution.py:569
  130.5 2.4 constant_dynamic-update-slice_fusion.refs_1_
  132.9 10.8 %attend.1.refs_7_ = bf16[1600,128]{1,0:T(8,128)(2,1)} custom-call(bf16[1600,128]{1,0:T(8,128)(2,1)} %pad_maximum_fusion.16.refs_0_, bf16[2,320,1536]{2,1,0:T(8,128)(2,1)} %constant_dynamic-update-slice_fusion.refs_1_, f32[1536,128]{1,0:T(8,128)} %fusion.63.refs_2_.refs_3_, bf16[800,256]{1,0:T(8,128)(2,1)} %collective-permute-done.9.refs_3_.refs_2_), custom_call_target="tpu_custom_call" | custom-call | bytes 240000 | tf_op jit(solution)/shard_map/attend/pallas_call | solution.py:674
  146.8 10.6 %scan_output.1 = f32[16,8,3200]{2,1,0:T(8,128)S(1)} custom-call(f32[16,8,3200]{2,1,0:T(8,128)S(1)} %get-tuple-element.239.refs_0_, f32[16,8,3200]{2,1,0:T(8,128)S(1)} %get-tuple-element.248.refs_1_, f32[128,16,128]{2,1,0:T(8,128)S(1)} %broadcast_in_dim.74.refs_2_.refs_3_, f32[128,16,128]{2,1,0:T(8,128)S(1)} %broadcast_in_dim.75.refs_3_.refs_2_.refs_4_, ...), custom_call_target="tpu_custom_call" | custom-call | bytes 270000 | tf_op jit(solution)/shard_map/scan_output/pallas_call | solution.py:485
  162.0 21.1 %collective-permute-done.11 = bf16[128,800]{1,0:T(8,128)(2,1)S(1)} collective-permute-done((bf16[128,800]{1,0:T(8,128)(2,1)S(1)}, bf16[128,800]{1,0:T(8,128)(2,1)S(1)}, u32[]{:S(2)}, u32[]{:S(2)}) %collective-permute-start.11) | collective-permute-done | bytes 204832 | tf_op jit(solution)/shard_map/ppermute | solution.py:30
  184.0 4.4 convolution_convert_fusion.2
  191.7 2.7 collective-permute-done.19
  200.1 6.3 collective-permute-done.20
  206.5 11.3 %collective-permute-done.21.refs_5_ = bf16[800,256]{1,0:T(8,128)(2,1)S(1)} collective-permute-done((bf16[800,256]{1,0:T(8,128)(2,1)S(1)}, bf16[800,256]{1,0:T(8,128)(2,1)S(1)}, u32[]{:S(2)}, u32[]{:S(2)}) %collective-permute-start.21) | collective-permute-done | bytes 409632 | tf_op jit(solution)/shard_map/ppermute | solution.py:96
  217.8 22.4 %feed.1 = (f32[256,1600]{1,0:T(8,128)S(1)}, f32[256,1600]{1,0:T(8,128)}, bf16[256,2816]{1,0:T(8,128)(2,1)S(1)}, bf16[2,256,2816]{2,1,0:T(8,128)(2,1)}) custom-call(bf16[256,1600]{1,0:T(8,128)(2,1)S(1)} %pad_maximum_fusion.7.refs_0_.refs_1_, bf16[256,1600]{1,0:T(8,128)(2,1)S(1)} %copy-done.19, bf16[1600,2752]{1,0:T(8,128)(2,1)} %refs_2_.1, ...), custom_call_target="tpu_custom_call" | custom-call | bytes 660000 | tf_op jit(solution)/shard_map/feed/pallas_call | solution.py:774
  249.7 7.9 collective-permute-done.24
  257.6 2.4 multiply_reduce_fusion.4
  260.0 2.8 collective-permute-done.23
  262.9 4.0 fusion.51
  269.2 7.9 collective-permute-done.25
  290.3 2.3 copy.105
  295.8 8.4 %collective-permute-done.26 = bf16[128,3200]{1,0:T(8,128)(2,1)} collective-permute-done((bf16[128,3200]{1,0:T(8,128)(2,1)}, bf16[128,3200]{1,0:T(8,128)(2,1)}, u32[]{:S(2)}, u32[]{:S(2)}) %collective-permute-start.26) | collective-permute-done | bytes 819232 | tf_op jit(solution)/shard_map/ppermute | solution.py:30
  304.2 4.3 fusion.14
  309.1 27.3 %collective-permute-done.29 = bf16[2,256,800]{1,2,0:T(8,128)(2,1)} collective-permute-done((bf16[2,256,800]{1,2,0:T(8,128)(2,1)}, bf16[2,256,800]{1,2,0:T(8,128)(2,1)}, u32[]{:S(2)}, u32[]{:S(2)}) %collective-permute-start.29) | collective-permute-done | bytes 819232 | tf_op jit(solution)/shard_map/ppermute | solution.py:96
  341.3 6.5 scan_adjoint.1.refs_1_
  347.8 25.2 %entering.3.refs_13_.refs_8_ = f32[16,3200]{1,0:T(8,128)S(1)} custom-call(f32[25,128]{1,0:T(8,128)S(1)} %bitcast.155, f32[16,3200]{1,0:T(8,128)S(1)} %scan_adjoint.1.refs_1_, f32[16,3200]{1,0:T(8,128)S(1)} %copy-done.21), custom_call_target="tpu_custom_call" | custom-call | bytes 720000 | tf_op jit(solution)/shard_map/entering/pallas_call | solution.py:569
  373.7 25.4 %gradient.7 = (bf16[200,8320]{1,0:T(8,128)(2,1)}, bf16[200,8320]{1,0:T(8,128)(2,1)}) custom-call(bf16[400,256]{1,0:T(8,128)(2,1)} %copy-done.46, bf16[400,256]{1,0:T(8,128)(2,1)} %copy-done.47, bf16[800,256]{1,0:T(8,128)(2,1)} %collective-permute-done.28.refs_2_, bf16[400,256]{1,0:T(8,128)(2,1)} %copy-done.44, bf16[400,256]{1,0:T(8,128)(2,1)} %copy-done.45, ...), custom_call_target="tpu_custom_call" | custom-call | bytes 780000 | tf_op jit(solution)/shard_map/gradient/pallas_call | solution.py:221
  401.6 28.1 %scan_gradient.1 = (f32[16,8,3200]{2,1,0:T(8,128)S(1)}, f32[16,8,3200]{2,1,0:T(8,128)S(1)}, f32[128,16,128]{2,1,0:T(8,128)S(1)}, f32[128,16,128]{2,1,0:T(8,128)S(1)}, f32[16,3200]{1,0:T(8,128)S(1)}) custom-call(f32[16,8,3200]{2,1,0:T(8,128)S(1)} %copy-done.3, f32[16,8,3200]{2,1,0:T(8,128)S(1)} %copy-done.5, f32[16,8,3200]{2,1,0:T(8,128)S(1)} %bitcast.153, ...), custom_call_target="tpu_custom_call" | custom-call | bytes 900000 | tf_op jit(solution)/shard_map/scan_gradient/pallas_call | solution.py:485
  431.9 22.1 %attend_back.1 = (bf16[1600,128]{1,0:T(8,128)(2,1)}, f32[2,320,768]{2,1,0:T(8,128)}, bf16[2,320,768]{2,1,0:T(8,128)(2,1)}) custom-call(bf16[1600,128]{1,0:T(8,128)(2,1)} %pad_maximum_fusion.16.refs_0_, bf16[2,320,1536]{2,1,0:T(8,128)(2,1)} %constant_dynamic-update-slice_fusion.refs_1_, bf16[1600,128]{1,0:T(8,128)(2,1)} %fusion.60.refs_2_, ...), custom_call_target="tpu_custom_call" | custom-call | bytes 600000 | tf_op jit(solution)/shard_map/attend_back/pallas_call | solution.py:674
  459.4 8.5 %multiply_reduce_fusion = (f32[3200]{0:T(1024)S(1)}, f32[3200]{0:T(1024)S(1)}, f32[3200]{0:T(1024)S(1)}, f32[3200]{0:T(1024)S(1)}, f32[3200]{0:T(1024)S(1)}, /*i...) fusion(f32[131,3200]{1,0:T(8,128)} %copy-done.59, ...), kind=kOutput, calls=%fused_computation.72 | convolution fusion | flops 123451776 | bytes 20656642 | tf_op jit(solution)/shard_map/dot_general | solution.py:602
  491.7 3.5 add_convert_fusion.2
  497.7 28.3 %collective-permute-done.38 = bf16[2,320,384]{2,1,0:T(8,128)(2,1)} collective-permute-done((bf16[2,320,384]{2,1,0:T(8,128)(2,1)}, bf16[2,320,384]{2,1,0:T(8,128)(2,1)}, u32[]{:S(2)}, u32[]{:S(2)}) %collective-permute-start.38) | collective-permute-done | bytes 491552 | tf_op jit(solution)/shard_map/ppermute | solution.py:96
  535.1 2.6 collective-permute-done.39
  538.6 9.0 %collective-permute-done.40 = bf16[2,320,128]{1,2,0:T(8,128)(2,1)S(1)} collective-permute-done((bf16[2,320,128]{1,2,0:T(8,128)(2,1)S(1)}, bf16[2,320,128]{1,2,0:T(8,128)(2,1)S(1)}, u32[]{:S(2)}, u32[]{:S(2)}) %collective-permute-start.40) | collective-permute-done | bytes 163872 | tf_op jit(solution)/shard_map/ppermute | solution.py:25
  551.0 10.8 %gradient.13 = (bf16[200,2816]{1,0:T(8,128)(2,1)}, bf16[200,2816]{1,0:T(8,128)(2,1)}) custom-call(bf16[400,256]{1,0:T(8,128)(2,1)} %copy-done.54, bf16[400,256]{1,0:T(8,128)(2,1)} %copy-done.55, bf16[800,256]{1,0:T(8,128)(2,1)} %collective-permute-done.9.refs_3_.refs_2_, bf16[1,256,2816]{2,1,0:T(8,128)(2,1)} %add_bitcast_fusion.refs_3_, ...), custom_call_target="tpu_custom_call" | custom-call | bytes 240000 | tf_op jit(solution)/shard_map/gradient/pallas_call | solution.py:221
  562.9 3.2 collective-permute-done.41
  568.2 3.3 fusion.72
  572.4 8.3 %convolution_add_fusion.3 = f32[256,1600]{0,1:T(8,128)} fusion(f32[256,1600]{0,1:T(8,128)S(1)} %fusion.72, bf16[1600,3200]{1,0:T(8,128)(2,1)} %param.31, bf16[128,512]{1,0:T(8,128)(2,1)S(1)} %copy-done.132, bf16[128,512]{1,0:T(8,128)(2,1)S(1)} %copy-done.115, bf16[128,896]{1,0:T(8,128)(2,1)S(1)} %collective-permute-done.33, ...), kind=kOutput, calls=%fused_computation.12 | convolution fusion | flops 2634956800 | bytes 15155200 | tf_op jit(solution)/shard_map/dot_general | solution.py:612
  605.1 4.4 collective-permute-done.52
  612.7 15.5 %collective-permute-done.71 = bf16[100,2816]{1,0:T(8,128)(2,1)} collective-permute-done((bf16[100,2816]{1,0:T(8,128)(2,1)}, bf16[100,2816]{1,0:T(8,128)(2,1)}, u32[]{:S(2)}, u32[]{:S(2)}) %collective-permute-start.71) | collective-permute-done | bytes 563232 | tf_op jit(solution)/shard_map/ppermute | solution.py:96
  632.5 3.7 add_convert_fusion
  639.6 5.0 gradient.8
  647.0 6.1 gradient.11
  654.9 6.0 gradient.10
  662.0 6.0 gradient.12
  670.2 9.6 %gradient.9 = (bf16[200,1920]{1,0:T(8,128)(2,1)}, bf16[200,1920]{1,0:T(8,128)(2,1)}) custom-call(bf16[400,256]{1,0:T(8,128)(2,1)} %copy-done.24, bf16[400,256]{1,0:T(8,128)(2,1)} %copy-done.25, bf16[800,256]{1,0:T(8,128)(2,1)} %collective-permute-done.15.refs_4_.refs_2_, bf16[800,128]{1,0:T(8,128)(2,1)} %copy-done.50, bf16[800,128]{1,0:T(8,128)(2,1)} %copy-done.51, ...), custom_call_target="tpu_custom_call" | custom-call | bytes 180000 | tf_op jit(solution)/shard_map/gradient/pallas_call | solution.py:221
  680.7 2.6 collective-permute-start.67
  683.3 52.2 %collective-permute-done.67 = bf16[100,512]{1,0:T(8,128)(2,1)S(1)} collective-permute-done((bf16[100,512]{1,0:T(8,128)(2,1)S(1)}, bf16[100,512]{1,0:T(8,128)(2,1)S(1)}, u32[]{:S(2)}, u32[]{:S(2)}) %collective-permute-start.67) | collective-permute-done | bytes 102432 | tf_op jit(solution)/shard_map/ppermute | solution.py:96
  739.0 2.3 collective-permute-start.62
  746.5 11.9 %collective-permute-done.62 = bf16[100,896]{1,0:T(8,128)(2,1)S(1)} collective-permute-done((bf16[100,896]{1,0:T(8,128)(2,1)S(1)}, bf16[100,896]{1,0:T(8,128)(2,1)S(1)}, u32[]{:S(2)}, u32[]{:S(2)}) %collective-permute-start.62) | collective-permute-done | bytes 179232 | tf_op jit(solution)/shard_map/ppermute | solution.py:96
  758.5 2.7 collective-permute-start.49
  762.5 3.9 collective-permute-done.65
  767.7 4.9 collective-permute-done.49
  773.5 2.4 collective-permute-start.55
  776.0 17.0 %collective-permute-done.50 = bf16[25,3200]{1,0:T(8,128)(2,1)S(1)} collective-permute-done((bf16[25,3200]{1,0:T(8,128)(2,1)S(1)}, bf16[25,3200]{1,0:T(8,128)(2,1)S(1)}, u32[]{:S(2)}, u32[]{:S(2)}) %collective-permute-start.50) | collective-permute-done | bytes 160032 | tf_op jit(solution)/shard_map/ppermute | solution.py:595
  795.7 5.6 collective-permute-done.55
  808.3 2.3 convert_add_fusion
  (675 shorter events, 225.8 us)
Async XLA Ops:
  0.7 19.2 %collective-permute-start.14 = (bf16[50,3200]{1,0:T(8,128)(2,1)}, bf16[50,3200]{1,0:T(8,128)(2,1)}, u32[]{:S(2)}, u32[]{:S(2)}) collective-permute-start(bf16[50,3200]{1,0:T(8,128)(2,1)} %bitcast.170), channel_id=1, source_target_pairs={{1,0},{0,1},{3,2},{2,3},{5,4},{4,5},{7,6},{6,7},{9,8},{8,9},{11,10... | collective-permute-start | bytes 960008 | tf_op jit(solution)/shard_map/ppermute | solution.py:30
  5.0 17.3 %collective-permute-start = (bf16[128,1600]{1,0:T(8,128)(2,1)S(1)}, bf16[128,1600]{1,0:T(8,128)(2,1)S(1)}, u32[]{:S(2)}, u32[]{:S(2)}) collective-permute-start(bf16[128,1600]{1,0:T(8,128)(2,1)S(1)} %bitcast.156), channel_id=1, source_target_pairs={{1,0},{0,1},{3,2},{2,3},{5,4},{4,5},{7,6},{6,7},{9,8},{8,9},{11,10... | collective-permute-start | bytes 1228808 | tf_op jit(solution)/shard_map/ppermute | solution.py:30
  5.2 38.0 %collective-permute-start.13 = (bf16[66,3200]{1,0:T(8,128)(2,1)}, bf16[66,3200]{1,0:T(8,128)(2,1)}, u32[]{:S(2)}, u32[]{:S(2)}) collective-permute-start(bf16[66,3200]{1,0:T(8,128)(2,1)} %bitcast.169), channel_id=1, source_target_pairs={{1,0},{0,1},{3,2},{2,3},{5,4},{4,5},{7,6},{6,7},{9,8},{8,9},{11,10... | collective-permute-start | bytes 1267208 | tf_op jit(solution)/shard_map/ppermute | solution.py:30
  25.0 14.0 %collective-permute-start.2 = (bf16[2,160,128]{2,1,0:T(8,128)(2,1)S(1)}, bf16[2,160,128]{2,1,0:T(8,128)(2,1)S(1)}, u32[]{:S(2)}, u32[]{:S(2)}) collective-permute-start(bf16[2,160,128]{2,1,0:T(8,128)(2,1)S(1)} %fusion.86), channel_id=1, source_target_pairs={{1,0},{0,1},{3,2},{2,3},{5,4},{4,5},{7,6},{6,7},{9,8},{8,9},{11,10... | collective-permute-start | bytes 245768 | tf_op jit(solution)/shard_map/ppermute | solution.py:30
  28.1 23.2 %collective-permute-start.1 = (bf16[800,128]{1,0:T(8,128)(2,1)S(1)}, bf16[800,128]{1,0:T(8,128)(2,1)S(1)}, u32[]{:S(2)}, u32[]{:S(2)}) collective-permute-start(bf16[800,128]{1,0:T(8,128)(2,1)S(1)} %split.133), channel_id=1, source_target_pairs={{1,0},{0,1},{3,2},{2,3},{5,4},{4,5},{7,6},{6,7},{9,8},{8,9},{11,10... | collective-permute-start | bytes 614408 | tf_op jit(solution)/shard_map/ppermute | solution.py:30
  29.1 70.7 %collective-permute-start.15 = (bf16[800,256]{1,0:T(8,128)(2,1)}, bf16[800,256]{1,0:T(8,128)(2,1)}, u32[]{:S(2)}, u32[]{:S(2)}) collective-permute-start(bf16[800,256]{1,0:T(8,128)(2,1)} %get-tuple-element.70), channel_id=1, source_target_pairs={{0,4},{2,6},{4,0},{6,2},{8,12},{10,14},{12,8},{14,10},{16,20},{18,... | collective-permute-start | bytes 1228808 | tf_op jit(solution)/shard_map/ppermute | solution.py:96
  37.8 25.2 %collective-permute-start.7 = (bf16[128,3200]{1,0:T(8,128)(2,1)S(1)}, bf16[128,3200]{1,0:T(8,128)(2,1)S(1)}, u32[]{:S(2)}, u32[]{:S(2)}) collective-permute-start(bf16[128,3200]{1,0:T(8,128)(2,1)S(1)} %split.137), channel_id=1, source_target_pairs={{1,0},{0,1},{3,2},{2,3},{5,4},{4,5},{7,6},{6,7},{9,8},{8,9},{11,10... | collective-permute-start | bytes 2457608 | tf_op jit(solution)/shard_map/ppermute | solution.py:30
  39.8 10.1 %collective-permute-start.3 = (bf16[2,320,128]{2,1,0:T(8,128)(2,1)S(1)}, bf16[2,320,128]{2,1,0:T(8,128)(2,1)S(1)}, u32[]{:S(2)}, u32[]{:S(2)}) collective-permute-start(bf16[2,320,128]{2,1,0:T(8,128)(2,1)S(1)} %get-tuple-element.287), channel_id=1, source_target_pairs={{0,8},{2,10},{4,12},{6,14},{8,16},{10,18},{12,20},{14,22},{16,24},... | collective-permute-start | bytes 491528 | tf_op jit(solution)/shard_map/ppermute | solution.py:25
  50.7 10.4 %collective-permute-start.5 = (bf16[2,320,384]{2,1,0:T(8,128)(2,1)S(1)}, bf16[2,320,384]{2,1,0:T(8,128)(2,1)S(1)}, u32[]{:S(2)}, u32[]{:S(2)}) collective-permute-start(bf16[2,320,384]{2,1,0:T(8,128)(2,1)S(1)} %pad_maximum_fusion.10), channel_id=1, source_target_pairs={{0,4},{2,6},{4,0},{6,2},{8,12},{10,14},{12,8},{14,10},{16,20},{18,... | collective-permute-start | bytes 1474568 | tf_op jit(solution)/shard_map/ppermute | solution.py:96
  62.2 68.3 %collective-permute-start.6 = (bf16[2,320,768]{2,1,0:T(8,128)(2,1)}, bf16[2,320,768]{2,1,0:T(8,128)(2,1)}, u32[]{:S(2)}, u32[]{:S(2)}) collective-permute-start(bf16[2,320,768]{2,1,0:T(8,128)(2,1)} %pad_maximum_fusion.4), channel_id=1, source_target_pairs={{0,2},{2,0},{4,6},{6,4},{8,10},{10,8},{12,14},{14,12},{16,18},{18,... | collective-permute-start | bytes 2949128 | tf_op jit(solution)/shard_map/ppermute | solution.py:96
  63.9 13.7 %collective-permute-start.12 = (bf16[3,3200]{1,0:T(4,128)(2,1)}, bf16[3,3200]{1,0:T(4,128)(2,1)}, u32[]{:S(2)}, u32[]{:S(2)}) collective-permute-start(bf16[3,3200]{1,0:T(4,128)(2,1)} %slice.400), channel_id=1, source_target_pairs={{0,2},{2,4},{4,6},{6,8},{8,10},{10,12},{12,14},{14,16},{16,18},{18... | collective-permute-start | bytes 57608 | tf_op jit(solution)/shard_map/ppermute | solution.py:25
  76.6 13.8 %collective-permute-start.8 = (bf16[128,1600]{1,0:T(8,128)(2,1)}, bf16[128,1600]{1,0:T(8,128)(2,1)}, u32[]{:S(2)}, u32[]{:S(2)}) collective-permute-start(bf16[128,1600]{1,0:T(8,128)(2,1)} %add_bitcast_fusion.1), channel_id=1, source_target_pairs={{1,0},{0,1},{3,2},{2,3},{5,4},{4,5},{7,6},{6,7},{9,8},{8,9},{11,10... | collective-permute-start | bytes 1228808 | tf_op jit(solution)/shard_map/ppermute | solution.py:30
  85.7 58.9 %collective-permute-start.17 = (bf16[1,128,100]{2,1,0:T(8,128)(2,1)}, bf16[1,128,100]{2,1,0:T(8,128)(2,1)S(1)}, u32[]{:S(2)}, u32[]{:S(2)}) collective-permute-start(bf16[1,128,100]{2,1,0:T(8,128)(2,1)} %bitcast.172), channel_id=1, source_target_pairs={{0,4},{2,6},{4,0},{6,2},{8,12},{10,14},{12,8},{14,10},{16,20},{18,... | collective-permute-start | bytes 76808 | tf_op jit(solution)/shard_map/ppermute | solution.py:96
  85.7 58.9 %collective-permute-start.16 = (bf16[1600,128]{1,0:T(8,128)(2,1)}, bf16[1600,128]{1,0:T(8,128)(2,1)}, u32[]{:S(2)}, u32[]{:S(2)}) collective-permute-start(bf16[1600,128]{1,0:T(8,128)(2,1)} %copy-done.57), channel_id=1, source_target_pairs={{0,4},{2,6},{4,0},{6,2},{8,12},{10,14},{12,8},{14,10},{16,20},{18,... | collective-permute-start | bytes 1228808 | tf_op jit(solution)/shard_map/ppermute | solution.py:96
  95.2 37.7 %collective-permute-start.9 = (bf16[800,256]{1,0:T(8,128)(2,1)}, bf16[800,256]{1,0:T(8,128)(2,1)}, u32[]{:S(2)}, u32[]{:S(2)}) collective-permute-start(bf16[800,256]{1,0:T(8,128)(2,1)} %get-tuple-element.69), channel_id=1, source_target_pairs={{0,4},{2,6},{4,0},{6,2},{8,12},{10,14},{12,8},{14,10},{16,20},{18,... | collective-permute-start | bytes 1228808 | tf_op jit(solution)/shard_map/ppermute | solution.py:96
  143.6 16.2 %collective-permute-start.10 = (bf16[1600,128]{1,0:T(8,128)(2,1)}, bf16[1600,128]{1,0:T(8,128)(2,1)S(1)}, u32[]{:S(2)}, u32[]{:S(2)}) collective-permute-start(bf16[1600,128]{1,0:T(8,128)(2,1)} %attend.1.refs_7_), channel_id=1, source_target_pairs={{1,0},{0,1},{3,2},{2,3},{5,4},{4,5},{7,6},{6,7},{9,8},{8,9},{11,10... | collective-permute-start | bytes 1228808 | tf_op jit(solution)/shard_map/ppermute | solution.py:30
  158.7 25.2 %collective-permute-start.18 = (bf16[128,3200]{1,0:T(8,128)(2,1)S(1)}, bf16[128,3200]{1,0:T(8,128)(2,1)S(1)}, u32[]{:S(2)}, u32[]{:S(2)}) collective-permute-start(bf16[128,3200]{1,0:T(8,128)(2,1)S(1)} %multiply_convert_fusion), channel_id=1, source_target_pairs={{1,0},{0,1},{3,2},{2,3},{5,4},{4,5},{7,6},{6,7},{9,8},{8,9},{11,10... | collective-permute-start | bytes 2457608 | tf_op jit(solution)/shard_map/ppermute | solution.py:30
  161.0 22.1 %collective-permute-start.11 = (bf16[128,800]{1,0:T(8,128)(2,1)S(1)}, bf16[128,800]{1,0:T(8,128)(2,1)S(1)}, u32[]{:S(2)}, u32[]{:S(2)}) collective-permute-start(bf16[128,800]{1,0:T(8,128)(2,1)S(1)} %split.139), channel_id=1, source_target_pairs={{1,0},{0,1},{3,2},{2,3},{5,4},{4,5},{7,6},{6,7},{9,8},{8,9},{11,10... | collective-permute-start | bytes 614408 | tf_op jit(solution)/shard_map/ppermute | solution.py:30
  190.6 27.1 %collective-permute-start.22 = (bf16[1600,256]{1,0:T(8,128)(2,1)S(1)}, bf16[1600,256]{1,0:T(8,128)(2,1)S(1)}, u32[]{:S(2)}, u32[]{:S(2)}) collective-permute-start(bf16[1600,256]{1,0:T(8,128)(2,1)S(1)} %get-tuple-element.73), channel_id=1, source_target_pairs={{0,4},{2,6},{4,0},{6,2},{8,12},{10,14},{12,8},{14,10},{16,20},{18,... | collective-permute-start | bytes 2457608 | tf_op jit(solution)/shard_map/ppermute | solution.py:96
  197.4 9.1 %collective-permute-start.20 = (bf16[128,1600]{1,0:T(8,128)(2,1)S(1)}, bf16[128,1600]{1,0:T(8,128)(2,1)S(1)}, u32[]{:S(2)}, u32[]{:S(2)}) collective-permute-start(bf16[128,1600]{1,0:T(8,128)(2,1)S(1)} %multiply_convert_fusion.2), channel_id=1, source_target_pairs={{1,0},{0,1},{3,2},{2,3},{5,4},{4,5},{7,6},{6,7},{9,8},{8,9},{11,10... | collective-permute-start | bytes 1228808 | tf_op jit(solution)/shard_map/ppermute | solution.py:30
  199.0 18.7 %collective-permute-start.21 = (bf16[800,256]{1,0:T(8,128)(2,1)S(1)}, bf16[800,256]{1,0:T(8,128)(2,1)S(1)}, u32[]{:S(2)}, u32[]{:S(2)}) collective-permute-start(bf16[800,256]{1,0:T(8,128)(2,1)S(1)} %get-tuple-element.72), channel_id=1, source_target_pairs={{0,4},{2,6},{4,0},{6,2},{8,12},{10,14},{12,8},{14,10},{16,20},{18,... | collective-permute-start | bytes 1228808 | tf_op jit(solution)/shard_map/ppermute | solution.py:96
  244.5 13.1 %collective-permute-start.24 = (bf16[128,1600]{1,0:T(8,128)(2,1)}, bf16[128,1600]{1,0:T(8,128)(2,1)}, u32[]{:S(2)}, u32[]{:S(2)}) collective-permute-start(bf16[128,1600]{1,0:T(8,128)(2,1)} %split.243), channel_id=1, source_target_pairs={{1,0},{0,1},{3,2},{2,3},{5,4},{4,5},{7,6},{6,7},{9,8},{8,9},{11,10... | collective-permute-start | bytes 1228808 | tf_op jit(solution)/shard_map/ppermute | solution.py:30
  247.6 15.2 %collective-permute-start.23 = (bf16[128,1600]{1,0:T(8,128)(2,1)S(1)}, bf16[128,1600]{1,0:T(8,128)(2,1)S(1)}, u32[]{:S(2)}, u32[]{:S(2)}) collective-permute-start(bf16[128,1600]{1,0:T(8,128)(2,1)S(1)} %split.244), channel_id=1, source_target_pairs={{1,0},{0,1},{3,2},{2,3},{5,4},{4,5},{7,6},{6,7},{9,8},{8,9},{11,10... | collective-permute-start | bytes 1228808 | tf_op jit(solution)/shard_map/ppermute | solution.py:30
  248.7 89.9 %collective-permute-start.27 = (bf16[2,256,2816]{2,1,0:T(8,128)(2,1)}, bf16[2,256,2816]{2,1,0:T(8,128)(2,1)}, u32[]{:S(2)}, u32[]{:S(2)}) collective-permute-start(bf16[2,256,2816]{2,1,0:T(8,128)(2,1)} %get-tuple-element.76.refs_9_), channel_id=1, source_target_pairs={{0,4},{2,6},{4,0},{6,2},{8,12},{10,14},{12,8},{14,10},{16,20},{18,... | collective-permute-start | bytes 8650760 | tf_op jit(solution)/shard_map/ppermute | solution.py:96
  279.4 14.4 %collective-permute-start.35 = (bf16[1600,128]{1,0:T(8,128)(2,1)}, bf16[1600,128]{1,0:T(8,128)(2,1)S(1)}, u32[]{:S(2)}, u32[]{:S(2)}) collective-permute-start(bf16[1600,128]{1,0:T(8,128)(2,1)} %split.245), channel_id=1, source_target_pairs={{1,0},{0,1},{3,2},{2,3},{5,4},{4,5},{7,6},{6,7},{9,8},{8,9},{11,10... | collective-permute-start | bytes 1228808 | tf_op jit(solution)/shard_map/ppermute | solution.py:30
  283.3 20.9 %collective-permute-start.26 = (bf16[128,3200]{1,0:T(8,128)(2,1)}, bf16[128,3200]{1,0:T(8,128)(2,1)}, u32[]{:S(2)}, u32[]{:S(2)}) collective-permute-start(bf16[128,3200]{1,0:T(8,128)(2,1)} %split.241), channel_id=1, source_target_pairs={{1,0},{0,1},{3,2},{2,3},{5,4},{4,5},{7,6},{6,7},{9,8},{8,9},{11,10... | collective-permute-start | bytes 2457608 | tf_op jit(solution)/shard_map/ppermute | solution.py:30
  286.8 86.8 %collective-permute-start.28 = (bf16[800,256]{1,0:T(8,128)(2,1)S(1)}, bf16[800,256]{1,0:T(8,128)(2,1)}, u32[]{:S(2)}, u32[]{:S(2)}) collective-permute-start(bf16[800,256]{1,0:T(8,128)(2,1)S(1)} %get-tuple-element.79), channel_id=1, source_target_pairs={{0,4},{2,6},{4,0},{6,2},{8,12},{10,14},{12,8},{14,10},{16,20},{18,... | collective-permute-start | bytes 1228808 | tf_op jit(solution)/shard_map/ppermute | solution.py:96
  292.6 43.8 %collective-permute-start.29 = (bf16[2,256,800]{1,2,0:T(8,128)(2,1)}, bf16[2,256,800]{1,2,0:T(8,128)(2,1)}, u32[]{:S(2)}, u32[]{:S(2)}) collective-permute-start(bf16[2,256,800]{1,2,0:T(8,128)(2,1)} %copy.105), channel_id=1, source_target_pairs={{0,4},{2,6},{4,0},{6,2},{8,12},{10,14},{12,8},{14,10},{16,20},{18,... | collective-permute-start | bytes 2457608 | tf_op jit(solution)/shard_map/ppermute | solution.py:96
  399.2 231.9 %collective-permute-start.45 = (bf16[200,8320]{1,0:T(8,128)(2,1)}, bf16[200,8320]{1,0:T(8,128)(2,1)}, u32[]{:S(2)}, u32[]{:S(2)}) collective-permute-start(bf16[200,8320]{1,0:T(8,128)(2,1)} %get-tuple-element.85.refs_10_), channel_id=1, source_target_pairs={{0,8},{2,10},{4,12},{6,14},{8,0},{10,2},{12,4},{14,6},{16,24},{18,... | collective-permute-start | bytes 9984008 | tf_op jit(solution)/shard_map/ppermute | solution.py:96
  469.4 22.3 %collective-permute-start.30 = (bf16[3,3200]{1,0:T(4,128)(2,1)S(1)}, bf16[3,3200]{1,0:T(4,128)(2,1)S(1)}, u32[]{:S(2)}, u32[]{:S(2)}) collective-permute-start(bf16[3,3200]{1,0:T(4,128)(2,1)S(1)} %pad_maximum_fusion.23), channel_id=1, source_target_pairs={{2,0},{4,2},{6,4},{8,6},{10,8},{12,10},{14,12},{16,14},{18,16},{20... | collective-permute-start | bytes 57608 | tf_op jit(solution)/shard_map/ppermute | solution.py:25
  471.4 13.4 %collective-permute-start.37 = (bf16[2,320,768]{2,1,0:T(8,128)(2,1)}, bf16[2,320,768]{2,1,0:T(8,128)(2,1)S(1)}, u32[]{:S(2)}, u32[]{:S(2)}) collective-permute-start(bf16[2,320,768]{2,1,0:T(8,128)(2,1)} %get-tuple-element.92), channel_id=1, source_target_pairs={{0,2},{2,0},{4,6},{6,4},{8,10},{10,8},{12,14},{14,12},{16,18},{18,... | collective-permute-start | bytes 2949128 | tf_op jit(solution)/shard_map/ppermute | solution.py:96
  481.6 68.4 %collective-permute-start.69 = (bf16[1,256,2816]{2,1,0:T(8,128)(2,1)}, bf16[1,256,2816]{2,1,0:T(8,128)(2,1)}, u32[]{:S(2)}, u32[]{:S(2)}) collective-permute-start(bf16[1,256,2816]{2,1,0:T(8,128)(2,1)} %add_bitcast_fusion.refs_3_), channel_id=1, source_target_pairs={{0,4},{2,6},{4,0},{6,2},{8,12},{10,14},{12,8},{14,10},{16,20},{18,... | collective-permute-start | bytes 4325384 | tf_op jit(solution)/shard_map/ppermute | solution.py:96
  490.9 35.1 %collective-permute-start.38 = (bf16[2,320,384]{2,1,0:T(8,128)(2,1)}, bf16[2,320,384]{2,1,0:T(8,128)(2,1)}, u32[]{:S(2)}, u32[]{:S(2)}) collective-permute-start(bf16[2,320,384]{2,1,0:T(8,128)(2,1)} %copy.112), channel_id=1, source_target_pairs={{0,4},{2,6},{4,0},{6,2},{8,12},{10,14},{12,8},{14,10},{16,20},{18,... | collective-permute-start | bytes 1474568 | tf_op jit(solution)/shard_map/ppermute | solution.py:96
  496.7 36.4 %collective-permute-start.34 = (bf16[128,512]{1,0:T(8,128)(2,1)S(1)}, bf16[128,512]{1,0:T(8,128)(2,1)S(1)}, u32[]{:S(2)}, u32[]{:S(2)}) collective-permute-start(bf16[128,512]{1,0:T(8,128)(2,1)S(1)} %get-tuple-element.247), channel_id=1, source_target_pairs={{1,0},{0,1},{3,2},{2,3},{5,4},{4,5},{7,6},{6,7},{9,8},{8,9},{11,10... | collective-permute-start | bytes 393224 | tf_op jit(solution)/shard_map/ppermute | solution.py:30
  530.9 16.7 %collective-permute-start.40 = (bf16[2,320,128]{1,2,0:T(8,128)(2,1)S(1)}, bf16[2,320,128]{1,2,0:T(8,128)(2,1)S(1)}, u32[]{:S(2)}, u32[]{:S(2)}) collective-permute-start(bf16[2,320,128]{1,2,0:T(8,128)(2,1)S(1)} %get-tuple-element.273), channel_id=1, source_target_pairs={{16,0},{18,2},{20,4},{22,6},{24,8},{26,10},{28,12},{30,14},{17,1},... | collective-permute-start | bytes 491528 | tf_op jit(solution)/shard_map/ppermute | solution.py:25
  533.1 15.6 %collective-permute-start.36 = (bf16[800,128]{0,1:T(8,128)(2,1)S(1)}, bf16[800,128]{0,1:T(8,128)(2,1)S(1)}, u32[]{:S(2)}, u32[]{:S(2)}) collective-permute-start(bf16[800,128]{0,1:T(8,128)(2,1)S(1)} %copy-done.127), channel_id=1, source_target_pairs={{1,0},{0,1},{3,2},{2,3},{5,4},{4,5},{7,6},{6,7},{9,8},{8,9},{11,10... | collective-permute-start | bytes 614408 | tf_op jit(solution)/shard_map/ppermute | solution.py:30
  537.7 33.9 %collective-permute-start.31 = (bf16[128,896]{1,0:T(8,128)(2,1)}, bf16[128,896]{1,0:T(8,128)(2,1)}, u32[]{:S(2)}, u32[]{:S(2)}) collective-permute-start(bf16[128,896]{1,0:T(8,128)(2,1)} %get-tuple-element.241), channel_id=1, source_target_pairs={{1,0},{0,1},{3,2},{2,3},{5,4},{4,5},{7,6},{6,7},{9,8},{8,9},{11,10... | collective-permute-start | bytes 688136 | tf_op jit(solution)/shard_map/ppermute | solution.py:30
  547.6 24.0 %collective-permute-start.32 = (bf16[128,896]{1,0:T(8,128)(2,1)}, bf16[128,896]{1,0:T(8,128)(2,1)S(1)}, u32[]{:S(2)}, u32[]{:S(2)}) collective-permute-start(bf16[128,896]{1,0:T(8,128)(2,1)} %get-tuple-element.242), channel_id=1, source_target_pairs={{1,0},{0,1},{3,2},{2,3},{5,4},{4,5},{7,6},{6,7},{9,8},{8,9},{11,10... | collective-permute-start | bytes 688136 | tf_op jit(solution)/shard_map/ppermute | solution.py:30
  548.8 13.0 %collective-permute-start.42 = (bf16[160,128]{0,1:T(8,128)(2,1)S(1)}, bf16[160,128]{0,1:T(8,128)(2,1)S(1)}, u32[]{:S(2)}, u32[]{:S(2)}) collective-permute-start(bf16[160,128]{0,1:T(8,128)(2,1)S(1)} %get-tuple-element.284), channel_id=1, source_target_pairs={{1,0},{0,1},{3,2},{2,3},{5,4},{4,5},{7,6},{6,7},{9,8},{8,9},{11,10... | collective-permute-start | bytes 122888 | tf_op jit(solution)/shard_map/ppermute | solution.py:30
  550.0 21.7 %collective-permute-start.33 = (bf16[128,896]{1,0:T(8,128)(2,1)S(1)}, bf16[128,896]{1,0:T(8,128)(2,1)S(1)}, u32[]{:S(2)}, u32[]{:S(2)}) collective-permute-start(bf16[128,896]{1,0:T(8,128)(2,1)S(1)} %get-tuple-element.243), channel_id=1, source_target_pairs={{1,0},{0,1},{3,2},{2,3},{5,4},{4,5},{7,6},{6,7},{9,8},{8,9},{11,10... | collective-permute-start | bytes 688136 | tf_op jit(solution)/shard_map/ppermute | solution.py:30
  566.1 72.9 %collective-permute-start.44 = (bf16[1,256,512]{2,1,0:T(8,128)(2,1)S(1)}, bf16[1,256,512]{2,1,0:T(8,128)(2,1)}, u32[]{:S(2)}, u32[]{:S(2)}) collective-permute-start(bf16[1,256,512]{2,1,0:T(8,128)(2,1)S(1)} %maximum_bitcast_fusion.2.refs_3_), channel_id=1, source_target_pairs={{0,4},{2,6},{4,0},{6,2},{8,12},{10,14},{12,8},{14,10},{16,20},{18,... | collective-permute-start | bytes 786440 | tf_op jit(solution)/shard_map/ppermute | solution.py:96
  571.5 27.3 %collective-permute-start.70 = (bf16[200,2816]{1,0:T(8,128)(2,1)}, bf16[200,2816]{1,0:T(8,128)(2,1)}, u32[]{:S(2)}, u32[]{:S(2)}) collective-permute-start(bf16[200,2816]{1,0:T(8,128)(2,1)} %get-tuple-element.115), channel_id=1, source_target_pairs={{0,8},{2,10},{4,12},{6,14},{8,0},{10,2},{12,4},{14,6},{16,24},{18,... | collective-permute-start | bytes 3379208 | tf_op jit(solution)/shard_map/ppermute | solution.py:96
  585.1 10.7 %collective-permute-start.43 = (bf16[128,1600]{1,0:T(8,128)(2,1)}, bf16[128,1600]{1,0:T(8,128)(2,1)}, u32[]{:S(2)}, u32[]{:S(2)}) collective-permute-start(bf16[128,1600]{1,0:T(8,128)(2,1)} %split.242), channel_id=1, source_target_pairs={{1,0},{0,1},{3,2},{2,3},{5,4},{4,5},{7,6},{6,7},{9,8},{8,9},{11,10... | collective-permute-start | bytes 1228808 | tf_op jit(solution)/shard_map/ppermute | solution.py:30
  586.3 60.6 %collective-permute-start.60 = (bf16[1,256,896]{2,1,0:T(8,128)(2,1)S(1)}, bf16[1,256,896]{2,1,0:T(8,128)(2,1)}, u32[]{:S(2)}, u32[]{:S(2)}) collective-permute-start(bf16[1,256,896]{2,1,0:T(8,128)(2,1)S(1)} %maximum_bitcast_fusion.refs_3_), channel_id=1, source_target_pairs={{0,4},{2,6},{4,0},{6,2},{8,12},{10,14},{12,8},{14,10},{16,20},{18,... | collective-permute-start | bytes 1376264 | tf_op jit(solution)/shard_map/ppermute | solution.py:96
  595.8 13.8 %collective-permute-start.52 = (bf16[1,256,1120]{1,2,0:T(8,128)(2,1)}, bf16[1,256,1120]{1,2,0:T(8,128)(2,1)}, u32[]{:S(2)}, u32[]{:S(2)}) collective-permute-start(bf16[1,256,1120]{1,2,0:T(8,128)(2,1)} %copy.117), channel_id=1, source_target_pairs={{0,4},{2,6},{4,0},{6,2},{8,12},{10,14},{12,8},{14,10},{16,20},{18,... | collective-permute-start | bytes 1720328 | tf_op jit(solution)/shard_map/ppermute | solution.py:96
  601.5 26.8 %collective-permute-start.71 = (bf16[100,2816]{1,0:T(8,128)(2,1)}, bf16[100,2816]{1,0:T(8,128)(2,1)}, u32[]{:S(2)}, u32[]{:S(2)}) collective-permute-start(bf16[100,2816]{1,0:T(8,128)(2,1)} %get-tuple-element.250), channel_id=1, source_target_pairs={{0,16},{2,18},{4,20},{6,22},{8,24},{10,26},{12,28},{14,30},{16,0},... | collective-permute-start | bytes 1689608 | tf_op jit(solution)/shard_map/ppermute | solution.py:96
  609.6 51.4 %collective-permute-start.63 = (bf16[1,256,896]{2,1,0:T(8,128)(2,1)}, bf16[1,256,896]{2,1,0:T(8,128)(2,1)}, u32[]{:S(2)}, u32[]{:S(2)}) collective-permute-start(bf16[1,256,896]{2,1,0:T(8,128)(2,1)} %maximum_bitcast_fusion.1.refs_3_), channel_id=1, source_target_pairs={{0,4},{2,6},{4,0},{6,2},{8,12},{10,14},{12,8},{14,10},{16,20},{18,... | collective-permute-start | bytes 1376264 | tf_op jit(solution)/shard_map/ppermute | solution.py:96
  628.3 40.1 %collective-permute-start.51 = (bf16[1600,128]{1,0:T(8,128)(2,1)S(1)}, bf16[1600,128]{1,0:T(8,128)(2,1)S(1)}, u32[]{:S(2)}, u32[]{:S(2)}) collective-permute-start(bf16[1600,128]{1,0:T(8,128)(2,1)S(1)} %get-tuple-element.101), channel_id=1, source_target_pairs={{0,4},{2,6},{4,0},{6,2},{8,12},{10,14},{12,8},{14,10},{16,20},{18,... | collective-permute-start | bytes 1228808 | tf_op jit(solution)/shard_map/ppermute | solution.py:96
  631.0 37.0 %collective-permute-start.53 = (bf16[1,128,132]{2,1,0:T(8,128)(2,1)}, bf16[1,128,132]{2,1,0:T(8,128)(2,1)}, u32[]{:S(2)}, u32[]{:S(2)}) collective-permute-start(bf16[1,128,132]{2,1,0:T(8,128)(2,1)} %maximum_add_fusion.8.refs_11_), channel_id=1, source_target_pairs={{0,4},{2,6},{4,0},{6,2},{8,12},{10,14},{12,8},{14,10},{16,20},{18,... | collective-permute-start | bytes 101384 | tf_op jit(solution)/shard_map/ppermute | solution.py:96
  639.0 14.1 %collective-permute-start.57 = (bf16[1,256,896]{2,1,0:T(8,128)(2,1)S(1)}, bf16[1,256,896]{2,1,0:T(8,128)(2,1)}, u32[]{:S(2)}, u32[]{:S(2)}) collective-permute-start(bf16[1,256,896]{2,1,0:T(8,128)(2,1)S(1)} %copy-done.100), channel_id=1, source_target_pairs={{0,4},{2,6},{4,0},{6,2},{8,12},{10,14},{12,8},{14,10},{16,20},{18,... | collective-permute-start | bytes 1376264 | tf_op jit(solution)/shard_map/ppermute | solution.py:96
  646.8 33.0 %collective-permute-start.66 = (bf16[200,512]{1,0:T(8,128)(2,1)}, bf16[200,512]{1,0:T(8,128)(2,1)S(1)}, u32[]{:S(2)}, u32[]{:S(2)}) collective-permute-start(bf16[200,512]{1,0:T(8,128)(2,1)} %get-tuple-element.110), channel_id=1, source_target_pairs={{0,8},{2,10},{4,12},{6,14},{8,0},{10,2},{12,4},{14,6},{16,24},{18,... | collective-permute-start | bytes 614408 | tf_op jit(solution)/shard_map/ppermute | solution.py:96
  653.1 155.2 %collective-permute-start.56 = (bf16[100,8320]{1,0:T(8,128)(2,1)S(1)}, bf16[100,8320]{1,0:T(8,128)(2,1)}, u32[]{:S(2)}, u32[]{:S(2)}) collective-permute-start(bf16[100,8320]{1,0:T(8,128)(2,1)S(1)} %copy-done.58), channel_id=1, source_target_pairs={{0,16},{2,18},{4,20},{6,22},{8,24},{10,26},{12,28},{14,30},{16,0},... | collective-permute-start | bytes 4992008 | tf_op jit(solution)/shard_map/ppermute | solution.py:96
  661.0 19.7 %collective-permute-start.46 = (bf16[25,3200]{1,0:T(8,128)(2,1)S(1)}, bf16[25,3200]{1,0:T(8,128)(2,1)S(1)}, u32[]{:S(2)}, u32[]{:S(2)}) collective-permute-start(bf16[25,3200]{1,0:T(8,128)(2,1)S(1)} %add_convert_fusion.14), channel_id=1, source_target_pairs={{0,1},{1,0},{2,3},{3,2},{4,5},{5,4},{6,7},{7,6},{8,9},{9,8},{10,11... | collective-permute-start | bytes 480008 | tf_op jit(solution)/shard_map/ppermute | solution.py:595
  668.0 69.3 %collective-permute-start.61 = (bf16[200,896]{1,0:T(8,128)(2,1)S(1)}, bf16[200,896]{1,0:T(8,128)(2,1)S(1)}, u32[]{:S(2)}, u32[]{:S(2)}) collective-permute-start(bf16[200,896]{1,0:T(8,128)(2,1)S(1)} %copy-done.177), channel_id=1, source_target_pairs={{0,8},{2,10},{4,12},{6,14},{8,0},{10,2},{12,4},{14,6},{16,24},{18,... | collective-permute-start | bytes 1075208 | tf_op jit(solution)/shard_map/ppermute | solution.py:96
  668.4 70.6 %collective-permute-start.58 = (bf16[200,896]{1,0:T(8,128)(2,1)S(1)}, bf16[200,896]{1,0:T(8,128)(2,1)S(1)}, u32[]{:S(2)}, u32[]{:S(2)}) collective-permute-start(bf16[200,896]{1,0:T(8,128)(2,1)S(1)} %copy-done.176), channel_id=1, source_target_pairs={{0,8},{2,10},{4,12},{6,14},{8,0},{10,2},{12,4},{14,6},{16,24},{18,... | collective-permute-start | bytes 1075208 | tf_op jit(solution)/shard_map/ppermute | solution.py:96
  679.8 61.7 %collective-permute-start.64 = (bf16[200,896]{1,0:T(8,128)(2,1)S(1)}, bf16[200,896]{1,0:T(8,128)(2,1)S(1)}, u32[]{:S(2)}, u32[]{:S(2)}) collective-permute-start(bf16[200,896]{1,0:T(8,128)(2,1)S(1)} %copy-done.175), channel_id=1, source_target_pairs={{0,8},{2,10},{4,12},{6,14},{8,0},{10,2},{12,4},{14,6},{16,24},{18,... | collective-permute-start | bytes 1075208 | tf_op jit(solution)/shard_map/ppermute | solution.py:96
  680.7 54.9 %collective-permute-start.67 = (bf16[100,512]{1,0:T(8,128)(2,1)S(1)}, bf16[100,512]{1,0:T(8,128)(2,1)S(1)}, u32[]{:S(2)}, u32[]{:S(2)}) collective-permute-start(bf16[100,512]{1,0:T(8,128)(2,1)S(1)} %slice.455), channel_id=1, source_target_pairs={{0,16},{2,18},{4,20},{6,22},{8,24},{10,26},{12,28},{14,30},{16,0},... | collective-permute-start | bytes 307208 | tf_op jit(solution)/shard_map/ppermute | solution.py:96
  737.0 36.2 %collective-permute-start.54 = (bf16[200,1920]{1,0:T(8,128)(2,1)S(1)}, bf16[200,1920]{1,0:T(8,128)(2,1)S(1)}, u32[]{:S(2)}, u32[]{:S(2)}) collective-permute-start(bf16[200,1920]{1,0:T(8,128)(2,1)S(1)} %copy-done.174), channel_id=1, source_target_pairs={{0,8},{2,10},{4,12},{6,14},{8,0},{10,2},{12,4},{14,6},{16,24},{18,... | collective-permute-start | bytes 2304008 | tf_op jit(solution)/shard_map/ppermute | solution.py:96
  739.0 19.5 %collective-permute-start.62 = (bf16[100,896]{1,0:T(8,128)(2,1)S(1)}, bf16[100,896]{1,0:T(8,128)(2,1)S(1)}, u32[]{:S(2)}, u32[]{:S(2)}) collective-permute-start(bf16[100,896]{1,0:T(8,128)(2,1)S(1)} %slice.451), channel_id=1, source_target_pairs={{0,16},{2,18},{4,20},{6,22},{8,24},{10,26},{12,28},{14,30},{16,0},... | collective-permute-start | bytes 537608 | tf_op jit(solution)/shard_map/ppermute | solution.py:96
  741.5 21.0 %collective-permute-start.59 = (bf16[100,896]{1,0:T(8,128)(2,1)S(1)}, bf16[100,896]{1,0:T(8,128)(2,1)S(1)}, u32[]{:S(2)}, u32[]{:S(2)}) collective-permute-start(bf16[100,896]{1,0:T(8,128)(2,1)S(1)} %slice.449), channel_id=1, source_target_pairs={{0,16},{2,18},{4,20},{6,22},{8,24},{10,26},{12,28},{14,30},{16,0},... | collective-permute-start | bytes 537608 | tf_op jit(solution)/shard_map/ppermute | solution.py:96
  744.5 22.0 %collective-permute-start.65 = (bf16[100,896]{1,0:T(8,128)(2,1)S(1)}, bf16[100,896]{1,0:T(8,128)(2,1)S(1)}, u32[]{:S(2)}, u32[]{:S(2)}) collective-permute-start(bf16[100,896]{1,0:T(8,128)(2,1)S(1)} %slice.453), channel_id=1, source_target_pairs={{0,16},{2,18},{4,20},{6,22},{8,24},{10,26},{12,28},{14,30},{16,0},... | collective-permute-start | bytes 537608 | tf_op jit(solution)/shard_map/ppermute | solution.py:96
  758.5 14.1 %collective-permute-start.49 = (bf16[25,3200]{1,0:T(8,128)(2,1)S(1)}, bf16[25,3200]{1,0:T(8,128)(2,1)S(1)}, u32[]{:S(2)}, u32[]{:S(2)}) collective-permute-start(bf16[25,3200]{1,0:T(8,128)(2,1)S(1)} %add_convert_fusion.11), channel_id=1, source_target_pairs={{0,8},{2,10},{4,12},{6,14},{8,0},{10,2},{12,4},{14,6},{16,24},{18,... | collective-permute-start | bytes 480008 | tf_op jit(solution)/shard_map/ppermute | solution.py:595
  772.6 20.3 %collective-permute-start.50 = (bf16[25,3200]{1,0:T(8,128)(2,1)S(1)}, bf16[25,3200]{1,0:T(8,128)(2,1)S(1)}, u32[]{:S(2)}, u32[]{:S(2)}) collective-permute-start(bf16[25,3200]{1,0:T(8,128)(2,1)S(1)} %add_convert_fusion.10), channel_id=1, source_target_pairs={{0,16},{2,18},{4,20},{6,22},{8,24},{10,26},{12,28},{14,30},{16,0},... | collective-permute-start | bytes 480008 | tf_op jit(solution)/shard_map/ppermute | solution.py:595
  773.5 27.8 %collective-permute-start.55 = (bf16[100,1920]{1,0:T(8,128)(2,1)S(1)}, bf16[100,1920]{1,0:T(8,128)(2,1)S(1)}, u32[]{:S(2)}, u32[]{:S(2)}) collective-permute-start(bf16[100,1920]{1,0:T(8,128)(2,1)S(1)} %slice.443), channel_id=1, source_target_pairs={{0,16},{2,18},{4,20},{6,22},{8,24},{10,26},{12,28},{14,30},{16,0},... | collective-permute-start | bytes 1152008 | tf_op jit(solution)/shard_map/ppermute | solution.py:96
  (188 other events, 1847.9 us)

commit v3 on v2

--- a/solution.py
+++ b/solution.py
@@ -88,7 +88,7 @@
 
 
 def taking(microseconds):
-    return pl.CostEstimate(flops=0, transcendentals=0, bytes_accessed=microseconds * 30_000)
+    return pl.CostEstimate(flops=0, transcendentals=0, bytes_accessed=microseconds * 30000)
 
 
 def seq_swap(block, bit):
@@ -928,6 +928,8 @@
         [attended_shared[2], gated_shared[2]],
     )
     second_shared = shared_features(both_second, model)
+    down = Gradient([back_shared], [activated[None]], [(0, 0, 0)], 1)
+    hidden_shared = shared_rows(hidden_back)
     delta_second = summed_tokens(second_part)
     feed_out = summed_tokens(feed_part)
     result = (hidden + feed_out).astype(jnp.bfloat16)
@@ -942,10 +944,19 @@
     both_delta_head, both_delta_branch = both_deltas[0], both_deltas[1]
     delta_gated = summed_tokens(right_product(both_delta_branch, mixer_weight))
     delta_attended = summed_tokens(right_product(head_weight, both_delta_head), 1).astype(bf16)
+    delta_query, delta_near, sent_near = attention_call(
+        attend_back_kernel,
+        "attend_back",
+        [query, delta_attended],
+        near,
+        bias,
+        ["wide", "kept", "sent"],
+        5,
+        order=finished(down),
+    )
     delta_scan_output = delta_gated * silu_input
     delta_gate = (delta_gated * scan_result_rows * silu_slope(gate_input)).astype(jnp.bfloat16)
     skip_sum = jnp.sum(delta_scan_output * scan_input_rows, axis=0)
-    hidden_shared = shared_rows(hidden_back)
     (first,) = scan_call(
         adjoint_kernel,
         "scan_adjoint",
@@ -954,15 +965,25 @@
         [rate],
         ["state"],
         flops=4,
-        order=[hidden_shared[1]],
+        order=[delta_query, hidden_shared[1]],
     )
     end_state = entering(total, first, rate, True, [])
+    delta_near = delta_near + seq_swap(sent_near, 0).astype(f32)
+    delta_near = after(delta_near, end_state)
+    middle = delta_near.shape[2] // 2
+    received = seq_swap(delta_near[:, :, middle:].astype(bf16), 1)
+    delta_near = delta_near[:, :, :middle] + received.astype(f32)
+    delta_pairs = delta_near[:, :, :rows]
+    for hop in range(1, hops + 1):
+        piece = delta_near[:, :, hop * rows : (hop + 1) * rows].astype(bf16)
+        delta_pairs = delta_pairs + passed_along(piece, "seq", -4 * hop).astype(f32)
+    delta_pairs = delta_pairs.astype(jnp.bfloat16)
     middle_sums = Gradient(
         [second_shared, attended_shared, gated_shared],
         [hidden_shared, both_deltas],
         [(0, 0, 0), (0, 0, 1), (1, 1, 0), (2, 1, 1)],
         2,
-        order=[end_state],
+        order=[end_state, delta_pairs],
     )
     through, sized, entry_back, read_back, decay_acc = scan_call(
         gradient_kernel,
@@ -975,26 +996,6 @@
         flops=20,
         order=finished(middle_sums),
     )
-    down = Gradient([back_shared], [after(activated, end_state)[None]], [(0, 0, 0)], 1, order=[through])
-    delta_query, delta_near, sent_near = attention_call(
-        attend_back_kernel,
-        "attend_back",
-        [query, delta_attended],
-        near,
-        bias,
-        ["wide", "kept", "sent"],
-        5,
-        order=[through],
-    )
-    delta_near = delta_near + seq_swap(sent_near, 0).astype(f32)
-    middle = delta_near.shape[2] // 2
-    received = seq_swap(delta_near[:, :, middle:].astype(bf16), 1)
-    delta_near = delta_near[:, :, :middle] + received.astype(f32)
-    delta_pairs = delta_near[:, :, :rows]
-    for hop in range(1, hops + 1):
-        piece = delta_near[:, :, hop * rows : (hop + 1) * rows].astype(bf16)
-        delta_pairs = delta_pairs + passed_along(piece, "seq", -4 * hop).astype(f32)
-    delta_pairs = delta_pairs.astype(jnp.bfloat16)
     both_qkv = jnp.concatenate(
         [
             to_own_columns(delta_query, 1, 0),
@@ -1032,8 +1033,9 @@
     arrived = passed_along(leaving.astype(jnp.bfloat16), "seq", -1).astype(jnp.float32)
     delta_inner = sum(jnp.pad(share[tap:], ((0, tap), (0, 0))) for tap, share in enumerate(shares))
     delta_inner = delta_inner + jnp.pad(arrived, ((rows - kernel + 1, 0), (0, 0)))
+    delta_inner = after(delta_inner, finished(middle_sums)[0])
     delta_entered = jnp.concatenate([delta_inner.astype(jnp.bfloat16), delta_gate], axis=1)
-    both_entered = column_chunks(delta_entered, 4)
+    both_entered = column_chunks(delta_entered, 2)
     widths = (query_weight.shape[1], key_weight.shape[1], value_weight.shape[1])
     cuts = (0, widths[0], widths[0] + widths[1], sum(widths))
     delta_normed = right_product(jnp.concatenate(both_entered, axis=1), input_weight)
@@ -1058,7 +1060,6 @@
     for gradient in input_sums:
         finished(gradient)
     input_placed = input_sums[-1].keep
-    late_sums.order = [input_placed]
     completed_all(input_sums + [late_sums, down, middle_sums])
     qkv_gradient, select_sum, step_sum = late_sums.results()
     query_gradient, key_gradient, value_gradient = (

time: 823 us -> 775 us (0.942)
  waiting for transfers between devices: 270 us -> 224 us
  local copies, waits for them, and re-layouts: 96 us -> 111 us
  starting transfers between devices: 85.8 us -> 73.6 us
    ppermute x35 -> x29, waiting for transfers between devices: 169 us -> 118 us  [seq_swap(): return lax.ppermute(block, 'seq', [(i, i ^ 1 << bit) for i in range(count)])]
    ppermute x5, waiting for transfers between devices: 25.4 us -> 37.4 us  [summed_everywhere(): received = lax.ppermute(values, axis, [(i, i ^ bit) for i in range(count)])]
    ppermute x35 -> x29, starting transfers between devices: 34.6 us -> 25.4 us  [seq_swap(): return lax.ppermute(block, 'seq', [(i, i ^ 1 << bit) for i in range(count)])]
    pallas_call x7 -> x5, Pallas kernels: 68.9 us -> 61.6 us  [quarter_gradient(): pl.pallas_call(ignoring(functools.partial(quarter_kernel, parts, counts),...]
    unnamed x374 -> x373, local copies, waits for them, and re-layouts: 35.1 us -> 38 us
    ppermute x26 -> x24, starting transfers between devices: 30.1 us -> 28.3 us  [from_ahead(): lax.ppermute(block, 'wt', [((i + distance) % count, i) for i in range(cou...]
    ppermute x26 -> x24, waiting for transfers between devices: 62.4 us -> 61.6 us  [from_ahead(): lax.ppermute(block, 'wt', [((i + distance) % count, i) for i in range(cou...]
  transfers between devices with their start and end apart: 72 -> 64, of which waited for: 29 -> 25; matrix products, arithmetic and copies ran while one was open for 23% -> 27% of each run, Pallas kernels for 22% -> 23%
where the time goes in v3:
time: 775 us; the launch traced here: 766 us
  waiting for transfers between devices  224 us (29%)
  Pallas kernels  224 us (29%)
  local copies, waits for them, and re-layouts  111 us (14%)
  other arithmetic  90.3 us (12%)
  starting transfers between devices  73.6 us (9%)
  matrix products  37 us (5%)
    ppermute x29, waiting for transfers between devices, seq_swap(): return lax.ppermute(block, 'seq', [(i, i ^ 1 << bit) for i in range(count)])  118 us
    pallas_call x5, Pallas kernels, quarter_gradient(): pl.pallas_call(ignoring(functools.partial(quarter_kernel, parts, counts),...  61.6 us
    ppermute x24, waiting for transfers between devices, from_ahead(): lax.ppermute(block, 'wt', [((i + distance) % count, i) for i in range(cou...  61.6 us
    pallas_call x4, Pallas kernels, scan_call(): pl.pallas_call(ignoring(body, len(token_args) + len(wide_args) + len(stat...  52 us
    pallas_call x2, Pallas kernels, entering(): pl.pallas_call(ignoring(functools.partial(entering_kernel, -1 if reverse...  49 us
    unnamed x373, local copies, waits for them, and re-layouts  38 us
    ppermute x5, waiting for transfers between devices, summed_everywhere(): received = lax.ppermute(values, axis, [(i, i ^ bit) for i in range(count)])  37.4 us
    pallas_call x2, Pallas kernels, attention_call(): pl.pallas_call(ignoring(body, len(wide) + 2, len(order)), grid=(key_heads...  32.8 us
  transfers between devices with their start and end apart: 64, of which 25 were waited for; matrix products, arithmetic and copies ran while one was open for 27% of the time, Pallas kernels for 23%

profile of v3, /device:TPU:0, one launch (start us, length us, event | category | flops | bytes accessed | tf_op | source)
XLA Modules:
  0.0 766.4 jit_solution(10444068794378529346)
XLA Ops:
  0.7 3.0 collective-permute-start.14
  16.7 2.4 fusion.58.refs_2_.refs_3_
  30.6 7.2 convolution_convert_fusion
  39.7 3.5 collective-permute-start.3
  43.2 4.5 collective-permute-start.4
  53.5 7.6 collective-permute-done.5
  63.9 3.5 collective-permute-start.12
  68.7 4.5 reshape.735
  78.9 2.6 multiply_convert_fusion.1
  88.0 2.8 convolution_add_fusion
  97.8 2.3 select_reduce_fusion
  100.5 6.2 scan_state.1.refs_1_
  106.7 24.1 %entering.2.refs_5_.refs_7_ = f32[16,3200]{1,0:T(8,128)S(1)} custom-call(f32[25,128]{1,0:T(8,128)S(1)} %bitcast.155, f32[16,3200]{1,0:T(8,128)S(1)} %scan_state.1.refs_1_, f32[16,3200]{1,0:T(8,128)S(1)} %copy-done.19), custom_call_target="tpu_custom_call" | custom-call | bytes 720000 | tf_op jit(solution)/shard_map/entering/pallas_call | solution.py:569
  133.8 10.8 %attend.1.refs_7_ = bf16[1600,128]{1,0:T(8,128)(2,1)} custom-call(bf16[1600,128]{1,0:T(8,128)(2,1)} %pad_maximum_fusion.16.refs_0_, bf16[2,320,1536]{2,1,0:T(8,128)(2,1)} %constant_dynamic-update-slice_fusion.refs_1_, f32[1536,128]{1,0:T(8,128)} %fusion.58.refs_2_.refs_3_, bf16[800,256]{1,0:T(8,128)(2,1)} %collective-permute-done.9.refs_3_.refs_2_), custom_call_target="tpu_custom_call" | custom-call | bytes 240000 | tf_op jit(solution)/shard_map/attend/pallas_call | solution.py:674
  147.8 10.6 %scan_output.1 = f32[16,8,3200]{2,1,0:T(8,128)S(1)} custom-call(f32[16,8,3200]{2,1,0:T(8,128)S(1)} %get-tuple-element.231.refs_0_, f32[16,8,3200]{2,1,0:T(8,128)S(1)} %get-tuple-element.236.refs_1_, f32[128,16,128]{2,1,0:T(8,128)S(1)} %broadcast_in_dim.70.refs_2_.refs_3_, f32[128,16,128]{2,1,0:T(8,128)S(1)} %broadcast_in_dim.71.refs_3_.refs_2_.refs_4_, ...), custom_call_target="tpu_custom_call" | custom-call | bytes 270000 | tf_op jit(solution)/shard_map/scan_output/pallas_call | solution.py:485
  163.0 21.1 %collective-permute-done.11 = bf16[128,800]{1,0:T(8,128)(2,1)S(1)} collective-permute-done((bf16[128,800]{1,0:T(8,128)(2,1)S(1)}, bf16[128,800]{1,0:T(8,128)(2,1)S(1)}, u32[]{:S(2)}, u32[]{:S(2)}) %collective-permute-start.11) | collective-permute-done | bytes 204832 | tf_op jit(solution)/shard_map/ppermute | solution.py:30
  190.3 2.7 collective-permute-done.19
  199.2 5.7 collective-permute-done.20
  205.0 11.3 %collective-permute-done.21.refs_5_ = bf16[800,256]{1,0:T(8,128)(2,1)S(1)} collective-permute-done((bf16[800,256]{1,0:T(8,128)(2,1)S(1)}, bf16[800,256]{1,0:T(8,128)(2,1)S(1)}, u32[]{:S(2)}, u32[]{:S(2)}) %collective-permute-start.21) | collective-permute-done | bytes 409632 | tf_op jit(solution)/shard_map/ppermute | solution.py:96
  216.3 22.4 %feed.1 = (f32[256,1600]{1,0:T(8,128)S(1)}, f32[256,1600]{1,0:T(8,128)}, bf16[256,2816]{1,0:T(8,128)(2,1)S(1)}, bf16[2,256,2816]{2,1,0:T(8,128)(2,1)}) custom-call(bf16[256,1600]{1,0:T(8,128)(2,1)S(1)} %pad_maximum_fusion.7.refs_0_.refs_1_, bf16[256,1600]{1,0:T(8,128)(2,1)S(1)} %copy-done.18, bf16[1600,2752]{1,0:T(8,128)(2,1)} %refs_2_.1, ...), custom_call_target="tpu_custom_call" | custom-call | bytes 660000 | tf_op jit(solution)/shard_map/feed/pallas_call | solution.py:774
  248.3 7.8 %collective-permute-done.24 = bf16[128,1600]{1,0:T(8,128)(2,1)} collective-permute-done((bf16[128,1600]{1,0:T(8,128)(2,1)}, bf16[128,1600]{1,0:T(8,128)(2,1)}, u32[]{:S(2)}, u32[]{:S(2)}) %collective-permute-start.24) | collective-permute-done | bytes 409632 | tf_op jit(solution)/shard_map/ppermute | solution.py:30
  256.2 2.4 multiply_reduce_fusion.4
  258.6 2.8 collective-permute-done.23
  261.5 4.0 fusion.46
  270.5 5.5 collective-permute-done.25
  285.3 10.9 %gradient.5 = (bf16[200,2816]{1,0:T(8,128)(2,1)}, bf16[200,2816]{1,0:T(8,128)(2,1)}) custom-call(bf16[400,256]{1,0:T(8,128)(2,1)} %copy-done.54, bf16[400,256]{1,0:T(8,128)(2,1)} %copy-done.55, bf16[800,256]{1,0:T(8,128)(2,1)} %collective-permute-done.9.refs_3_.refs_2_, bf16[1,256,2816]{2,1,0:T(8,128)(2,1)} %bitcast.154, bf16[1,256,2816]{2,1,0:T(8,128)(2,1)} %copy-done.111), custom_call_target="tpu_custom_call" | custom-call | bytes 240000 | tf_op jit(solution)/shard_map/gradient/pallas_call | solution.py:221
  298.7 22.0 %attend_back.1 = (bf16[1600,128]{1,0:T(8,128)(2,1)}, f32[2,320,768]{2,1,0:T(8,128)}, bf16[2,320,768]{2,1,0:T(8,128)(2,1)}) custom-call(bf16[1600,128]{1,0:T(8,128)(2,1)} %pad_maximum_fusion.16.refs_0_, bf16[2,320,1536]{2,1,0:T(8,128)(2,1)} %constant_dynamic-update-slice_fusion.refs_1_, bf16[1600,128]{1,0:T(8,128)(2,1)} %fusion.55.refs_2_, ...), custom_call_target="tpu_custom_call" | custom-call | bytes 600000 | tf_op jit(solution)/shard_map/attend_back/pallas_call | solution.py:674
  324.3 3.1 copy.108
  330.0 4.5 fusion.14
  335.1 26.4 %collective-permute-done.31 = bf16[2,256,800]{1,2,0:T(8,128)(2,1)} collective-permute-done((bf16[2,256,800]{1,2,0:T(8,128)(2,1)}, bf16[2,256,800]{1,2,0:T(8,128)(2,1)}, u32[]{:S(2)}, u32[]{:S(2)}) %collective-permute-start.31) | collective-permute-done | bytes 819232 | tf_op jit(solution)/shard_map/ppermute | solution.py:96
  364.6 2.7 copy.109
  367.4 3.0 add_convert_fusion.1
  371.8 6.3 scan_adjoint.1.refs_1_
  378.1 24.9 %entering.3.refs_13_.refs_8_ = f32[16,3200]{1,0:T(8,128)S(1)} custom-call(f32[25,128]{1,0:T(8,128)S(1)} %bitcast.156, f32[16,3200]{1,0:T(8,128)S(1)} %scan_adjoint.1.refs_1_, f32[16,3200]{1,0:T(8,128)S(1)} %copy-done.20), custom_call_target="tpu_custom_call" | custom-call | bytes 720000 | tf_op jit(solution)/shard_map/entering/pallas_call | solution.py:569
  404.2 2.6 add_add_fusion
  409.9 2.4 fusion.107
  414.1 4.5 collective-permute-done.33
  424.2 16.0 %collective-permute-done.63 = bf16[100,2816]{1,0:T(8,128)(2,1)} collective-permute-done((bf16[100,2816]{1,0:T(8,128)(2,1)}, bf16[100,2816]{1,0:T(8,128)(2,1)}, u32[]{:S(2)}, u32[]{:S(2)}) %collective-permute-start.63) | collective-permute-done | bytes 563232 | tf_op jit(solution)/shard_map/ppermute | solution.py:96
  442.4 6.0 collective-permute-done.35
  449.4 25.4 %gradient.6 = (bf16[200,8320]{1,0:T(8,128)(2,1)}, bf16[200,8320]{1,0:T(8,128)(2,1)}) custom-call(bf16[400,256]{1,0:T(8,128)(2,1)} %copy-done.52, bf16[400,256]{1,0:T(8,128)(2,1)} %copy-done.53, bf16[800,256]{1,0:T(8,128)(2,1)} %collective-permute-done.30.refs_2_, bf16[400,256]{1,0:T(8,128)(2,1)} %copy-done.50, bf16[400,256]{1,0:T(8,128)(2,1)} %copy-done.51, ...), custom_call_target="tpu_custom_call" | custom-call | bytes 780000 | tf_op jit(solution)/shard_map/gradient/pallas_call | solution.py:221
  476.4 28.9 %scan_gradient.1 = (f32[16,8,3200]{2,1,0:T(8,128)S(1)}, f32[16,8,3200]{2,1,0:T(8,128)S(1)}, f32[128,16,128]{2,1,0:T(8,128)S(1)}, f32[128,16,128]{2,1,0:T(8,128)S(1)}, f32[16,3200]{1,0:T(8,128)S(1)}) custom-call(f32[16,8,3200]{2,1,0:T(8,128)S(1)} %copy-done.3, f32[16,8,3200]{2,1,0:T(8,128)S(1)} %copy-done.5, f32[16,8,3200]{2,1,0:T(8,128)S(1)} %bitcast.152, ...), custom_call_target="tpu_custom_call" | custom-call | bytes 900000 | tf_op jit(solution)/shard_map/scan_gradient/pallas_call | solution.py:485
  513.6 3.3 fusion.101
  519.0 6.1 multiply_reduce_fusion
  532.8 3.9 collective-permute-done.41
  540.0 9.3 %collective-permute-done.37 = bf16[200,8320]{1,0:T(8,128)(2,1)} collective-permute-done((bf16[200,8320]{1,0:T(8,128)(2,1)}, bf16[200,8320]{1,0:T(8,128)(2,1)}, u32[]{:S(2)}, u32[]{:S(2)}) %collective-permute-start.37) | collective-permute-done | bytes 3328032 | tf_op jit(solution)/shard_map/ppermute | solution.py:96
  549.3 3.7 add_convert_fusion
  555.4 3.6 reshape.744
  560.9 3.4 add_convert_fusion.2
  575.4 3.1 collective-permute-done.39
  578.4 7.4 collective-permute-done.38
  585.8 8.4 %convolution_add_fusion.3 = f32[256,1600]{0,1:T(8,128)} fusion(f32[256,1600]{0,1:T(8,128)S(1)} %fusion.67, bf16[1600,3200]{1,0:T(8,128)(2,1)} %param.31, bf16[128,1536]{1,0:T(8,128)(2,1)} %collective-permute-done.39, bf16[128,1536]{1,0:T(8,128)(2,1)S(1)} %get-tuple-element.234, bf16[128,1664]{1,0:T(8,128)(2,1)} %collective-permute-done.38, ...), kind=kOutput, calls=%fused_computation.12 | convolution fusion | flops 2628403200 | bytes 15155200 | tf_op jit(solution)/shard_map/dot_general | solution.py:612
  594.3 2.3 copy.117
  614.3 18.7 %collective-permute-done.53.refs_12_ = bf16[1,128,132]{2,1,0:T(8,128)(2,1)S(1)} collective-permute-done((bf16[1,128,132]{2,1,0:T(8,128)(2,1)S(1)}, bf16[1,128,132]{2,1,0:T(8,128)(2,1)S(1)}, u32[]{:S(2)}, u32[]{:S(2)}) %collective-permute-start.53) | collective-permute-done | bytes 33824 | tf_op jit(solution)/shard_map/ppermute | solution.py:96
  633.7 9.7 %gradient.8 = (bf16[200,1920]{1,0:T(8,128)(2,1)}, bf16[200,1920]{1,0:T(8,128)(2,1)}) custom-call(bf16[400,256]{1,0:T(8,128)(2,1)} %copy-done.30, bf16[400,256]{1,0:T(8,128)(2,1)} %copy-done.31, bf16[800,256]{1,0:T(8,128)(2,1)} %collective-permute-done.15.refs_4_.refs_2_, bf16[800,128]{1,0:T(8,128)(2,1)} %copy-done.56, bf16[800,128]{1,0:T(8,128)(2,1)} %copy-done.57, ...), custom_call_target="tpu_custom_call" | custom-call | bytes 180000 | tf_op jit(solution)/shard_map/gradient/pallas_call | solution.py:221
  645.5 2.5 copy.123
  648.2 20.3 %collective-permute-done.54 = bf16[200,1920]{1,0:T(8,128)(2,1)} collective-permute-done((bf16[200,1920]{1,0:T(8,128)(2,1)}, bf16[200,1920]{1,0:T(8,128)(2,1)}, u32[]{:S(2)}, u32[]{:S(2)}) %collective-permute-start.54) | collective-permute-done | bytes 768032 | tf_op jit(solution)/shard_map/ppermute | solution.py:96
  670.7 4.1 convert_add_fusion.refs_5_
  674.8 7.6 gradient.7
  686.9 3.2 fusion.104
  690.0 2.9 collective-permute-done.46
  695.9 8.0 %gradient.9 = (bf16[200,1664]{1,0:T(8,128)(2,1)}, bf16[200,1664]{1,0:T(8,128)(2,1)}) custom-call(bf16[400,256]{1,0:T(8,128)(2,1)} %copy-done.30, bf16[400,256]{1,0:T(8,128)(2,1)} %copy-done.31, bf16[800,256]{1,0:T(8,128)(2,1)} %collective-permute-done.15.refs_4_.refs_2_, bf16[1,256,1664]{2,1,0:T(8,128)(2,1)} %get-tuple-element.241.refs_3_, ...), custom_call_target="tpu_custom_call" | custom-call | bytes 150000 | tf_op jit(solution)/shard_map/gradient/pallas_call | solution.py:221
  718.9 18.1 %collective-permute-done.49 = bf16[25,3200]{1,0:T(8,128)(2,1)S(1)} collective-permute-done((bf16[25,3200]{1,0:T(8,128)(2,1)S(1)}, bf16[25,3200]{1,0:T(8,128)(2,1)S(1)}, u32[]{:S(2)}, u32[]{:S(2)}) %collective-permute-start.49) | collective-permute-done | bytes 160032 | tf_op jit(solution)/shard_map/ppermute | solution.py:595
  740.4 16.4 %collective-permute-done.50 = bf16[25,3200]{1,0:T(8,128)(2,1)S(1)} collective-permute-done((bf16[25,3200]{1,0:T(8,128)(2,1)S(1)}, bf16[25,3200]{1,0:T(8,128)(2,1)S(1)}, u32[]{:S(2)}, u32[]{:S(2)}) %collective-permute-start.50) | collective-permute-done | bytes 160032 | tf_op jit(solution)/shard_map/ppermute | solution.py:595
  759.7 4.2 collective-permute-done.58
  (652 shorter events, 218.7 us)
Async XLA Ops:
  0.7 19.2 %collective-permute-start.14 = (bf16[50,3200]{1,0:T(8,128)(2,1)}, bf16[50,3200]{1,0:T(8,128)(2,1)}, u32[]{:S(2)}, u32[]{:S(2)}) collective-permute-start(bf16[50,3200]{1,0:T(8,128)(2,1)} %bitcast.170), channel_id=1, source_target_pairs={{1,0},{0,1},{3,2},{2,3},{5,4},{4,5},{7,6},{6,7},{9,8},{8,9},{11,10... | collective-permute-start | bytes 960008 | tf_op jit(solution)/shard_map/ppermute | solution.py:30
  5.0 17.3 %collective-permute-start = (bf16[128,1600]{1,0:T(8,128)(2,1)S(1)}, bf16[128,1600]{1,0:T(8,128)(2,1)S(1)}, u32[]{:S(2)}, u32[]{:S(2)}) collective-permute-start(bf16[128,1600]{1,0:T(8,128)(2,1)S(1)} %bitcast.157), channel_id=1, source_target_pairs={{1,0},{0,1},{3,2},{2,3},{5,4},{4,5},{7,6},{6,7},{9,8},{8,9},{11,10... | collective-permute-start | bytes 1228808 | tf_op jit(solution)/shard_map/ppermute | solution.py:30
  5.2 38.0 %collective-permute-start.13 = (bf16[66,3200]{1,0:T(8,128)(2,1)}, bf16[66,3200]{1,0:T(8,128)(2,1)}, u32[]{:S(2)}, u32[]{:S(2)}) collective-permute-start(bf16[66,3200]{1,0:T(8,128)(2,1)} %bitcast.169), channel_id=1, source_target_pairs={{1,0},{0,1},{3,2},{2,3},{5,4},{4,5},{7,6},{6,7},{9,8},{8,9},{11,10... | collective-permute-start | bytes 1267208 | tf_op jit(solution)/shard_map/ppermute | solution.py:30
  25.0 14.0 %collective-permute-start.2 = (bf16[2,160,128]{2,1,0:T(8,128)(2,1)S(1)}, bf16[2,160,128]{2,1,0:T(8,128)(2,1)S(1)}, u32[]{:S(2)}, u32[]{:S(2)}) collective-permute-start(bf16[2,160,128]{2,1,0:T(8,128)(2,1)S(1)} %fusion.81), channel_id=1, source_target_pairs={{1,0},{0,1},{3,2},{2,3},{5,4},{4,5},{7,6},{6,7},{9,8},{8,9},{11,10... | collective-permute-start | bytes 245768 | tf_op jit(solution)/shard_map/ppermute | solution.py:30
  28.1 23.2 %collective-permute-start.1 = (bf16[800,128]{1,0:T(8,128)(2,1)S(1)}, bf16[800,128]{1,0:T(8,128)(2,1)S(1)}, u32[]{:S(2)}, u32[]{:S(2)}) collective-permute-start(bf16[800,128]{1,0:T(8,128)(2,1)S(1)} %split.133), channel_id=1, source_target_pairs={{1,0},{0,1},{3,2},{2,3},{5,4},{4,5},{7,6},{6,7},{9,8},{8,9},{11,10... | collective-permute-start | bytes 614408 | tf_op jit(solution)/shard_map/ppermute | solution.py:30
  29.1 71.1 %collective-permute-start.15 = (bf16[800,256]{1,0:T(8,128)(2,1)}, bf16[800,256]{1,0:T(8,128)(2,1)}, u32[]{:S(2)}, u32[]{:S(2)}) collective-permute-start(bf16[800,256]{1,0:T(8,128)(2,1)} %get-tuple-element.66), channel_id=1, source_target_pairs={{0,4},{2,6},{4,0},{6,2},{8,12},{10,14},{12,8},{14,10},{16,20},{18,... | collective-permute-start | bytes 1228808 | tf_op jit(solution)/shard_map/ppermute | solution.py:96
  37.8 25.2 %collective-permute-start.7 = (bf16[128,3200]{1,0:T(8,128)(2,1)S(1)}, bf16[128,3200]{1,0:T(8,128)(2,1)S(1)}, u32[]{:S(2)}, u32[]{:S(2)}) collective-permute-start(bf16[128,3200]{1,0:T(8,128)(2,1)S(1)} %split.137), channel_id=1, source_target_pairs={{1,0},{0,1},{3,2},{2,3},{5,4},{4,5},{7,6},{6,7},{9,8},{8,9},{11,10... | collective-permute-start | bytes 2457608 | tf_op jit(solution)/shard_map/ppermute | solution.py:30
  39.7 10.1 %collective-permute-start.3 = (bf16[2,320,128]{2,1,0:T(8,128)(2,1)S(1)}, bf16[2,320,128]{2,1,0:T(8,128)(2,1)S(1)}, u32[]{:S(2)}, u32[]{:S(2)}) collective-permute-start(bf16[2,320,128]{2,1,0:T(8,128)(2,1)S(1)} %get-tuple-element.275), channel_id=1, source_target_pairs={{0,8},{2,10},{4,12},{6,14},{8,16},{10,18},{12,20},{14,22},{16,24},... | collective-permute-start | bytes 491528 | tf_op jit(solution)/shard_map/ppermute | solution.py:25
  43.2 7.4 collective-permute-start.4
  50.7 10.4 %collective-permute-start.5 = (bf16[2,320,384]{2,1,0:T(8,128)(2,1)S(1)}, bf16[2,320,384]{2,1,0:T(8,128)(2,1)S(1)}, u32[]{:S(2)}, u32[]{:S(2)}) collective-permute-start(bf16[2,320,384]{2,1,0:T(8,128)(2,1)S(1)} %pad_maximum_fusion.11), channel_id=1, source_target_pairs={{0,4},{2,6},{4,0},{6,2},{8,12},{10,14},{12,8},{14,10},{16,20},{18,... | collective-permute-start | bytes 1474568 | tf_op jit(solution)/shard_map/ppermute | solution.py:96
  62.1 69.4 %collective-permute-start.6 = (bf16[2,320,768]{2,1,0:T(8,128)(2,1)}, bf16[2,320,768]{2,1,0:T(8,128)(2,1)}, u32[]{:S(2)}, u32[]{:S(2)}) collective-permute-start(bf16[2,320,768]{2,1,0:T(8,128)(2,1)} %pad_maximum_fusion.4), channel_id=1, source_target_pairs={{0,2},{2,0},{4,6},{6,4},{8,10},{10,8},{12,14},{14,12},{16,18},{18,... | collective-permute-start | bytes 2949128 | tf_op jit(solution)/shard_map/ppermute | solution.py:96
  63.9 14.0 %collective-permute-start.12 = (bf16[3,3200]{1,0:T(4,128)(2,1)}, bf16[3,3200]{1,0:T(4,128)(2,1)}, u32[]{:S(2)}, u32[]{:S(2)}) collective-permute-start(bf16[3,3200]{1,0:T(4,128)(2,1)} %slice.368), channel_id=1, source_target_pairs={{0,2},{2,4},{4,6},{6,8},{8,10},{10,12},{12,14},{14,16},{16,18},{18... | collective-permute-start | bytes 57608 | tf_op jit(solution)/shard_map/ppermute | solution.py:25
  76.9 13.9 %collective-permute-start.8 = (bf16[128,1600]{1,0:T(8,128)(2,1)}, bf16[128,1600]{1,0:T(8,128)(2,1)}, u32[]{:S(2)}, u32[]{:S(2)}) collective-permute-start(bf16[128,1600]{1,0:T(8,128)(2,1)} %add_bitcast_fusion), channel_id=1, source_target_pairs={{1,0},{0,1},{3,2},{2,3},{5,4},{4,5},{7,6},{6,7},{9,8},{8,9},{11,10... | collective-permute-start | bytes 1228808 | tf_op jit(solution)/shard_map/ppermute | solution.py:30
  86.0 59.6 %collective-permute-start.17 = (bf16[1,128,100]{2,1,0:T(8,128)(2,1)}, bf16[1,128,100]{2,1,0:T(8,128)(2,1)S(1)}, u32[]{:S(2)}, u32[]{:S(2)}) collective-permute-start(bf16[1,128,100]{2,1,0:T(8,128)(2,1)} %bitcast.171), channel_id=1, source_target_pairs={{0,4},{2,6},{4,0},{6,2},{8,12},{10,14},{12,8},{14,10},{16,20},{18,... | collective-permute-start | bytes 76808 | tf_op jit(solution)/shard_map/ppermute | solution.py:96
  86.0 59.6 %collective-permute-start.16 = (bf16[1600,128]{1,0:T(8,128)(2,1)}, bf16[1600,128]{1,0:T(8,128)(2,1)}, u32[]{:S(2)}, u32[]{:S(2)}) collective-permute-start(bf16[1600,128]{1,0:T(8,128)(2,1)} %copy-done.61), channel_id=1, source_target_pairs={{0,4},{2,6},{4,0},{6,2},{8,12},{10,14},{12,8},{14,10},{16,20},{18,... | collective-permute-start | bytes 1228808 | tf_op jit(solution)/shard_map/ppermute | solution.py:96
  95.5 38.3 %collective-permute-start.9 = (bf16[800,256]{1,0:T(8,128)(2,1)}, bf16[800,256]{1,0:T(8,128)(2,1)}, u32[]{:S(2)}, u32[]{:S(2)}) collective-permute-start(bf16[800,256]{1,0:T(8,128)(2,1)} %get-tuple-element.65), channel_id=1, source_target_pairs={{0,4},{2,6},{4,0},{6,2},{8,12},{10,14},{12,8},{14,10},{16,20},{18,... | collective-permute-start | bytes 1228808 | tf_op jit(solution)/shard_map/ppermute | solution.py:96
  144.6 16.2 %collective-permute-start.10 = (bf16[1600,128]{1,0:T(8,128)(2,1)}, bf16[1600,128]{1,0:T(8,128)(2,1)S(1)}, u32[]{:S(2)}, u32[]{:S(2)}) collective-permute-start(bf16[1600,128]{1,0:T(8,128)(2,1)} %attend.1.refs_7_), channel_id=1, source_target_pairs={{1,0},{0,1},{3,2},{2,3},{5,4},{4,5},{7,6},{6,7},{9,8},{8,9},{11,10... | collective-permute-start | bytes 1228808 | tf_op jit(solution)/shard_map/ppermute | solution.py:30
  159.7 25.2 %collective-permute-start.18 = (bf16[128,3200]{1,0:T(8,128)(2,1)S(1)}, bf16[128,3200]{1,0:T(8,128)(2,1)S(1)}, u32[]{:S(2)}, u32[]{:S(2)}) collective-permute-start(bf16[128,3200]{1,0:T(8,128)(2,1)S(1)} %multiply_convert_fusion), channel_id=1, source_target_pairs={{1,0},{0,1},{3,2},{2,3},{5,4},{4,5},{7,6},{6,7},{9,8},{8,9},{11,10... | collective-permute-start | bytes 2457608 | tf_op jit(solution)/shard_map/ppermute | solution.py:30
  162.0 22.1 %collective-permute-start.11 = (bf16[128,800]{1,0:T(8,128)(2,1)S(1)}, bf16[128,800]{1,0:T(8,128)(2,1)S(1)}, u32[]{:S(2)}, u32[]{:S(2)}) collective-permute-start(bf16[128,800]{1,0:T(8,128)(2,1)S(1)} %split.139), channel_id=1, source_target_pairs={{1,0},{0,1},{3,2},{2,3},{5,4},{4,5},{7,6},{6,7},{9,8},{8,9},{11,10... | collective-permute-start | bytes 614408 | tf_op jit(solution)/shard_map/ppermute | solution.py:30
  186.9 6.1 collective-permute-start.19
  189.2 27.1 %collective-permute-start.22 = (bf16[1600,256]{1,0:T(8,128)(2,1)S(1)}, bf16[1600,256]{1,0:T(8,128)(2,1)S(1)}, u32[]{:S(2)}, u32[]{:S(2)}) collective-permute-start(bf16[1600,256]{1,0:T(8,128)(2,1)S(1)} %get-tuple-element.69), channel_id=1, source_target_pairs={{0,4},{2,6},{4,0},{6,2},{8,12},{10,14},{12,8},{14,10},{16,20},{18,... | collective-permute-start | bytes 2457608 | tf_op jit(solution)/shard_map/ppermute | solution.py:96
  195.8 9.1 %collective-permute-start.20 = (bf16[128,1600]{1,0:T(8,128)(2,1)S(1)}, bf16[128,1600]{1,0:T(8,128)(2,1)S(1)}, u32[]{:S(2)}, u32[]{:S(2)}) collective-permute-start(bf16[128,1600]{1,0:T(8,128)(2,1)S(1)} %multiply_convert_fusion.2), channel_id=1, source_target_pairs={{1,0},{0,1},{3,2},{2,3},{5,4},{4,5},{7,6},{6,7},{9,8},{8,9},{11,10... | collective-permute-start | bytes 1228808 | tf_op jit(solution)/shard_map/ppermute | solution.py:30
  198.2 18.1 %collective-permute-start.21 = (bf16[800,256]{1,0:T(8,128)(2,1)S(1)}, bf16[800,256]{1,0:T(8,128)(2,1)S(1)}, u32[]{:S(2)}, u32[]{:S(2)}) collective-permute-start(bf16[800,256]{1,0:T(8,128)(2,1)S(1)} %get-tuple-element.68), channel_id=1, source_target_pairs={{0,4},{2,6},{4,0},{6,2},{8,12},{10,14},{12,8},{14,10},{16,20},{18,... | collective-permute-start | bytes 1228808 | tf_op jit(solution)/shard_map/ppermute | solution.py:96
  243.1 13.1 %collective-permute-start.24 = (bf16[128,1600]{1,0:T(8,128)(2,1)}, bf16[128,1600]{1,0:T(8,128)(2,1)}, u32[]{:S(2)}, u32[]{:S(2)}) collective-permute-start(bf16[128,1600]{1,0:T(8,128)(2,1)} %split.243), channel_id=1, source_target_pairs={{1,0},{0,1},{3,2},{2,3},{5,4},{4,5},{7,6},{6,7},{9,8},{8,9},{11,10... | collective-permute-start | bytes 1228808 | tf_op jit(solution)/shard_map/ppermute | solution.py:30
  246.1 15.2 %collective-permute-start.23 = (bf16[128,1600]{1,0:T(8,128)(2,1)S(1)}, bf16[128,1600]{1,0:T(8,128)(2,1)S(1)}, u32[]{:S(2)}, u32[]{:S(2)}) collective-permute-start(bf16[128,1600]{1,0:T(8,128)(2,1)S(1)} %split.244), channel_id=1, source_target_pairs={{1,0},{0,1},{3,2},{2,3},{5,4},{4,5},{7,6},{6,7},{9,8},{8,9},{11,10... | collective-permute-start | bytes 1228808 | tf_op jit(solution)/shard_map/ppermute | solution.py:30
  247.3 36.9 %collective-permute-start.28 = (bf16[1,256,2816]{2,1,0:T(8,128)(2,1)}, bf16[1,256,2816]{2,1,0:T(8,128)(2,1)S(1)}, u32[]{:S(2)}, u32[]{:S(2)}) collective-permute-start(bf16[1,256,2816]{2,1,0:T(8,128)(2,1)} %bitcast.153), channel_id=1, source_target_pairs={{0,4},{2,6},{4,0},{6,2},{8,12},{10,14},{12,8},{14,10},{16,20},{18,... | collective-permute-start | bytes 4325384 | tf_op jit(solution)/shard_map/ppermute | solution.py:96
  266.8 9.3 %collective-permute-start.25 = (bf16[2,128,800]{2,1,0:T(8,128)(2,1)S(1)}, bf16[2,128,800]{2,1,0:T(8,128)(2,1)S(1)}, u32[]{:S(2)}, u32[]{:S(2)}) collective-permute-start(bf16[2,128,800]{2,1,0:T(8,128)(2,1)S(1)} %get-tuple-element.243), channel_id=1, source_target_pairs={{1,0},{0,1},{3,2},{2,3},{5,4},{4,5},{7,6},{6,7},{9,8},{8,9},{11,10... | collective-permute-start | bytes 1228808 | tf_op jit(solution)/shard_map/ppermute | solution.py:30
  269.7 100.7 %collective-permute-start.29 = (bf16[2,256,2816]{2,1,0:T(8,128)(2,1)}, bf16[2,256,2816]{2,1,0:T(8,128)(2,1)}, u32[]{:S(2)}, u32[]{:S(2)}) collective-permute-start(bf16[2,256,2816]{2,1,0:T(8,128)(2,1)} %get-tuple-element.78.refs_9_), channel_id=1, source_target_pairs={{0,4},{2,6},{4,0},{6,2},{8,12},{10,14},{12,8},{14,10},{16,20},{18,... | collective-permute-start | bytes 8650760 | tf_op jit(solution)/shard_map/ppermute | solution.py:96
  277.5 20.3 %collective-permute-start.27 = (bf16[1600,128]{1,0:T(8,128)(2,1)S(1)}, bf16[1600,128]{1,0:T(8,128)(2,1)S(1)}, u32[]{:S(2)}, u32[]{:S(2)}) collective-permute-start(bf16[1600,128]{1,0:T(8,128)(2,1)S(1)} %split.245), channel_id=1, source_target_pairs={{1,0},{0,1},{3,2},{2,3},{5,4},{4,5},{7,6},{6,7},{9,8},{8,9},{11,10... | collective-permute-start | bytes 1228808 | tf_op jit(solution)/shard_map/ppermute | solution.py:30
  283.1 45.5 %collective-permute-start.26 = (bf16[128,3200]{1,0:T(8,128)(2,1)}, bf16[128,3200]{1,0:T(8,128)(2,1)}, u32[]{:S(2)}, u32[]{:S(2)}) collective-permute-start(bf16[128,3200]{1,0:T(8,128)(2,1)} %split.241), channel_id=1, source_target_pairs={{1,0},{0,1},{3,2},{2,3},{5,4},{4,5},{7,6},{6,7},{9,8},{8,9},{11,10... | collective-permute-start | bytes 2457608 | tf_op jit(solution)/shard_map/ppermute | solution.py:30
  296.2 71.2 %collective-permute-start.62 = (bf16[200,2816]{1,0:T(8,128)(2,1)}, bf16[200,2816]{1,0:T(8,128)(2,1)}, u32[]{:S(2)}, u32[]{:S(2)}) collective-permute-start(bf16[200,2816]{1,0:T(8,128)(2,1)} %get-tuple-element.76.refs_5_), channel_id=1, source_target_pairs={{0,8},{2,10},{4,12},{6,14},{8,0},{10,2},{12,4},{14,6},{16,24},{18,... | collective-permute-start | bytes 3379208 | tf_op jit(solution)/shard_map/ppermute | solution.py:96
  320.7 43.9 %collective-permute-start.32 = (bf16[2,320,768]{2,1,0:T(8,128)(2,1)}, bf16[2,320,768]{2,1,0:T(8,128)(2,1)}, u32[]{:S(2)}, u32[]{:S(2)}) collective-permute-start(bf16[2,320,768]{2,1,0:T(8,128)(2,1)} %get-tuple-element.87), channel_id=1, source_target_pairs={{0,2},{2,0},{4,6},{6,4},{8,10},{10,8},{12,14},{14,12},{16,18},{18,... | collective-permute-start | bytes 2949128 | tf_op jit(solution)/shard_map/ppermute | solution.py:96
  323.7 37.8 %collective-permute-start.31 = (bf16[2,256,800]{1,2,0:T(8,128)(2,1)}, bf16[2,256,800]{1,2,0:T(8,128)(2,1)}, u32[]{:S(2)}, u32[]{:S(2)}) collective-permute-start(bf16[2,256,800]{1,2,0:T(8,128)(2,1)} %copy.107), channel_id=1, source_target_pairs={{0,4},{2,6},{4,0},{6,2},{8,12},{10,14},{12,8},{14,10},{16,20},{18,... | collective-permute-start | bytes 2457608 | tf_op jit(solution)/shard_map/ppermute | solution.py:96
  328.6 120.8 %collective-permute-start.30 = (bf16[800,256]{1,0:T(8,128)(2,1)}, bf16[800,256]{1,0:T(8,128)(2,1)}, u32[]{:S(2)}, u32[]{:S(2)}) collective-permute-start(bf16[800,256]{1,0:T(8,128)(2,1)} %get-tuple-element.81), channel_id=1, source_target_pairs={{0,4},{2,6},{4,0},{6,2},{8,12},{10,14},{12,8},{14,10},{16,20},{18,... | collective-permute-start | bytes 1228808 | tf_op jit(solution)/shard_map/ppermute | solution.py:96
  361.5 50.8 %collective-permute-start.40 = (bf16[800,128]{0,1:T(8,128)(2,1)}, bf16[800,128]{0,1:T(8,128)(2,1)}, u32[]{:S(2)}, u32[]{:S(2)}) collective-permute-start(bf16[800,128]{0,1:T(8,128)(2,1)} %get-tuple-element.265), channel_id=1, source_target_pairs={{1,0},{0,1},{3,2},{2,3},{5,4},{4,5},{7,6},{6,7},{9,8},{8,9},{11,10... | collective-permute-start | bytes 614408 | tf_op jit(solution)/shard_map/ppermute | solution.py:30
  409.4 9.1 %collective-permute-start.33 = (bf16[2,320,384]{2,1,0:T(8,128)(2,1)}, bf16[2,320,384]{2,1,0:T(8,128)(2,1)}, u32[]{:S(2)}, u32[]{:S(2)}) collective-permute-start(bf16[2,320,384]{2,1,0:T(8,128)(2,1)} %copy.110), channel_id=1, source_target_pairs={{0,4},{2,6},{4,0},{6,2},{8,12},{10,14},{12,8},{14,10},{16,20},{18,... | collective-permute-start | bytes 1474568 | tf_op jit(solution)/shard_map/ppermute | solution.py:96
  412.3 28.0 %collective-permute-start.63 = (bf16[100,2816]{1,0:T(8,128)(2,1)}, bf16[100,2816]{1,0:T(8,128)(2,1)}, u32[]{:S(2)}, u32[]{:S(2)}) collective-permute-start(bf16[100,2816]{1,0:T(8,128)(2,1)} %get-tuple-element.238), channel_id=1, source_target_pairs={{0,16},{2,18},{4,20},{6,22},{8,24},{10,26},{12,28},{14,30},{16,0},... | collective-permute-start | bytes 1689608 | tf_op jit(solution)/shard_map/ppermute | solution.py:96
  421.5 20.9 %collective-permute-start.34 = (bf16[2,320,128]{1,2,0:T(8,128)(2,1)S(1)}, bf16[2,320,128]{1,2,0:T(8,128)(2,1)S(1)}, u32[]{:S(2)}, u32[]{:S(2)}) collective-permute-start(bf16[2,320,128]{1,2,0:T(8,128)(2,1)S(1)} %get-tuple-element.262), channel_id=1, source_target_pairs={{8,0},{10,2},{12,4},{14,6},{16,8},{18,10},{20,12},{22,14},{24,16},... | collective-permute-start | bytes 491528 | tf_op jit(solution)/shard_map/ppermute | solution.py:25
  422.8 25.7 %collective-permute-start.35 = (bf16[2,320,128]{1,2,0:T(8,128)(2,1)S(1)}, bf16[2,320,128]{1,2,0:T(8,128)(2,1)S(1)}, u32[]{:S(2)}, u32[]{:S(2)}) collective-permute-start(bf16[2,320,128]{1,2,0:T(8,128)(2,1)S(1)} %get-tuple-element.263), channel_id=1, source_target_pairs={{16,0},{18,2},{20,4},{22,6},{24,8},{26,10},{28,12},{30,14},{17,1},... | collective-permute-start | bytes 491528 | tf_op jit(solution)/shard_map/ppermute | solution.py:25
  474.8 74.4 %collective-permute-start.37 = (bf16[200,8320]{1,0:T(8,128)(2,1)}, bf16[200,8320]{1,0:T(8,128)(2,1)}, u32[]{:S(2)}, u32[]{:S(2)}) collective-permute-start(bf16[200,8320]{1,0:T(8,128)(2,1)} %get-tuple-element.89.refs_10_), channel_id=1, source_target_pairs={{0,8},{2,10},{4,12},{6,14},{8,0},{10,2},{12,4},{14,6},{16,24},{18,... | collective-permute-start | bytes 9984008 | tf_op jit(solution)/shard_map/ppermute | solution.py:96
  525.3 7.5 collective-permute-start.42
  530.5 30.4 %collective-permute-start.36 = (bf16[3,3200]{1,0:T(4,128)(2,1)S(1)}, bf16[3,3200]{1,0:T(4,128)(2,1)S(1)}, u32[]{:S(2)}, u32[]{:S(2)}) collective-permute-start(bf16[3,3200]{1,0:T(4,128)(2,1)S(1)} %pad_maximum_fusion.23), channel_id=1, source_target_pairs={{2,0},{4,2},{6,4},{8,6},{10,8},{12,10},{14,12},{16,14},{18,16},{20... | collective-permute-start | bytes 57608 | tf_op jit(solution)/shard_map/ppermute | solution.py:25
  531.8 4.9 collective-permute-start.41
  538.4 34.9 %collective-permute-start.52 = (bf16[1,256,1120]{1,2,0:T(8,128)(2,1)}, bf16[1,256,1120]{1,2,0:T(8,128)(2,1)}, u32[]{:S(2)}, u32[]{:S(2)}) collective-permute-start(bf16[1,256,1120]{1,2,0:T(8,128)(2,1)} %copy.120), channel_id=1, source_target_pairs={{0,4},{2,6},{4,0},{6,2},{8,12},{10,14},{12,8},{14,10},{16,20},{18,... | collective-permute-start | bytes 1720328 | tf_op jit(solution)/shard_map/ppermute | solution.py:96
  566.1 12.4 %collective-permute-start.39 = (bf16[128,1536]{1,0:T(8,128)(2,1)}, bf16[128,1536]{1,0:T(8,128)(2,1)}, u32[]{:S(2)}, u32[]{:S(2)}) collective-permute-start(bf16[128,1536]{1,0:T(8,128)(2,1)} %get-tuple-element.235), channel_id=1, source_target_pairs={{1,0},{0,1},{3,2},{2,3},{5,4},{4,5},{7,6},{6,7},{9,8},{8,9},{11,10... | collective-permute-start | bytes 1179656 | tf_op jit(solution)/shard_map/ppermute | solution.py:30
  567.2 18.7 %collective-permute-start.38 = (bf16[128,1664]{1,0:T(8,128)(2,1)}, bf16[128,1664]{1,0:T(8,128)(2,1)}, u32[]{:S(2)}, u32[]{:S(2)}) collective-permute-start(bf16[128,1664]{1,0:T(8,128)(2,1)} %get-tuple-element.233), channel_id=1, source_target_pairs={{1,0},{0,1},{3,2},{2,3},{5,4},{4,5},{7,6},{6,7},{9,8},{8,9},{11,10... | collective-permute-start | bytes 1277960 | tf_op jit(solution)/shard_map/ppermute | solution.py:30
  575.3 95.4 %collective-permute-start.45 = (bf16[100,8320]{1,0:T(8,128)(2,1)}, bf16[100,8320]{1,0:T(8,128)(2,1)}, u32[]{:S(2)}, u32[]{:S(2)}) collective-permute-start(bf16[100,8320]{1,0:T(8,128)(2,1)} %get-tuple-element.221), channel_id=1, source_target_pairs={{0,16},{2,18},{4,20},{6,22},{8,24},{10,26},{12,28},{14,30},{16,0},... | collective-permute-start | bytes 4992008 | tf_op jit(solution)/shard_map/ppermute | solution.py:96
  599.0 13.0 %collective-permute-start.43 = (bf16[128,1600]{1,0:T(8,128)(2,1)}, bf16[128,1600]{1,0:T(8,128)(2,1)S(1)}, u32[]{:S(2)}, u32[]{:S(2)}) collective-permute-start(bf16[128,1600]{1,0:T(8,128)(2,1)} %split.242), channel_id=1, source_target_pairs={{1,0},{0,1},{3,2},{2,3},{5,4},{4,5},{7,6},{6,7},{9,8},{8,9},{11,10... | collective-permute-start | bytes 1228808 | tf_op jit(solution)/shard_map/ppermute | solution.py:30
  602.1 72.8 %collective-permute-start.44 = (bf16[1,256,1536]{2,1,0:T(8,128)(2,1)}, bf16[1,256,1536]{2,1,0:T(8,128)(2,1)}, u32[]{:S(2)}, u32[]{:S(2)}) collective-permute-start(bf16[1,256,1536]{2,1,0:T(8,128)(2,1)} %maximum_bitcast_fusion.refs_3_), channel_id=1, source_target_pairs={{0,4},{2,6},{4,0},{6,2},{8,12},{10,14},{12,8},{14,10},{16,20},{18,... | collective-permute-start | bytes 2359304 | tf_op jit(solution)/shard_map/ppermute | solution.py:96
  607.8 25.1 %collective-permute-start.51 = (bf16[1600,128]{1,0:T(8,128)(2,1)S(1)}, bf16[1600,128]{1,0:T(8,128)(2,1)S(1)}, u32[]{:S(2)}, u32[]{:S(2)}) collective-permute-start(bf16[1600,128]{1,0:T(8,128)(2,1)S(1)} %get-tuple-element.102), channel_id=1, source_target_pairs={{0,4},{2,6},{4,0},{6,2},{8,12},{10,14},{12,8},{14,10},{16,20},{18,... | collective-permute-start | bytes 1228808 | tf_op jit(solution)/shard_map/ppermute | solution.py:96
  610.6 22.4 %collective-permute-start.53 = (bf16[1,128,132]{2,1,0:T(8,128)(2,1)S(1)}, bf16[1,128,132]{2,1,0:T(8,128)(2,1)S(1)}, u32[]{:S(2)}, u32[]{:S(2)}) collective-permute-start(bf16[1,128,132]{2,1,0:T(8,128)(2,1)S(1)} %maximum_add_fusion.8.refs_11_), channel_id=1, source_target_pairs={{0,4},{2,6},{4,0},{6,2},{8,12},{10,14},{12,8},{14,10},{16,20},{18,... | collective-permute-start | bytes 101384 | tf_op jit(solution)/shard_map/ppermute | solution.py:96
  611.9 84.0 %collective-permute-start.56 = (bf16[1,256,1664]{2,1,0:T(8,128)(2,1)}, bf16[1,256,1664]{2,1,0:T(8,128)(2,1)}, u32[]{:S(2)}, u32[]{:S(2)}) collective-permute-start(bf16[1,256,1664]{2,1,0:T(8,128)(2,1)} %get-tuple-element.241.refs_3_), channel_id=1, source_target_pairs={{0,4},{2,6},{4,0},{6,2},{8,12},{10,14},{12,8},{14,10},{16,20},{18,... | collective-permute-start | bytes 2555912 | tf_op jit(solution)/shard_map/ppermute | solution.py:96
  643.4 25.1 %collective-permute-start.54 = (bf16[200,1920]{1,0:T(8,128)(2,1)}, bf16[200,1920]{1,0:T(8,128)(2,1)}, u32[]{:S(2)}, u32[]{:S(2)}) collective-permute-start(bf16[200,1920]{1,0:T(8,128)(2,1)} %get-tuple-element.104), channel_id=1, source_target_pairs={{0,8},{2,10},{4,12},{6,14},{8,0},{10,2},{12,4},{14,6},{16,24},{18,... | collective-permute-start | bytes 2304008 | tf_op jit(solution)/shard_map/ppermute | solution.py:96
  670.7 36.7 %collective-permute-start.55 = (bf16[100,1920]{1,0:T(8,128)(2,1)}, bf16[100,1920]{1,0:T(8,128)(2,1)S(1)}, u32[]{:S(2)}, u32[]{:S(2)}) collective-permute-start(bf16[100,1920]{1,0:T(8,128)(2,1)} %slice.409), channel_id=1, source_target_pairs={{0,16},{2,18},{4,20},{6,22},{8,24},{10,26},{12,28},{14,30},{16,0},... | collective-permute-start | bytes 1152008 | tf_op jit(solution)/shard_map/ppermute | solution.py:96
  685.7 7.2 collective-permute-start.46
  692.9 13.1 %collective-permute-start.47 = (bf16[25,3200]{1,0:T(8,128)(2,1)S(1)}, bf16[25,3200]{1,0:T(8,128)(2,1)S(1)}, u32[]{:S(2)}, u32[]{:S(2)}) collective-permute-start(bf16[25,3200]{1,0:T(8,128)(2,1)S(1)} %add_convert_fusion.11), channel_id=1, source_target_pairs={{0,2},{2,0},{4,6},{6,4},{8,10},{10,8},{12,14},{14,12},{16,18},{18,... | collective-permute-start | bytes 480008 | tf_op jit(solution)/shard_map/ppermute | solution.py:595
  695.0 20.3 %collective-permute-start.59 = (bf16[200,1536]{1,0:T(8,128)(2,1)}, bf16[200,1536]{1,0:T(8,128)(2,1)}, u32[]{:S(2)}, u32[]{:S(2)}) collective-permute-start(bf16[200,1536]{1,0:T(8,128)(2,1)} %get-tuple-element.107), channel_id=1, source_target_pairs={{0,8},{2,10},{4,12},{6,14},{8,0},{10,2},{12,4},{14,6},{16,24},{18,... | collective-permute-start | bytes 1843208 | tf_op jit(solution)/shard_map/ppermute | solution.py:96
  703.9 33.9 %collective-permute-start.57 = (bf16[200,1664]{1,0:T(8,128)(2,1)}, bf16[200,1664]{1,0:T(8,128)(2,1)S(1)}, u32[]{:S(2)}, u32[]{:S(2)}) collective-permute-start(bf16[200,1664]{1,0:T(8,128)(2,1)} %get-tuple-element.106), channel_id=1, source_target_pairs={{0,8},{2,10},{4,12},{6,14},{8,0},{10,2},{12,4},{14,6},{16,24},{18,... | collective-permute-start | bytes 1996808 | tf_op jit(solution)/shard_map/ppermute | solution.py:96
  706.1 8.2 %collective-permute-start.48 = (bf16[25,3200]{1,0:T(8,128)(2,1)S(1)}, bf16[25,3200]{1,0:T(8,128)(2,1)S(1)}, u32[]{:S(2)}, u32[]{:S(2)}) collective-permute-start(bf16[25,3200]{1,0:T(8,128)(2,1)S(1)} %add_convert_fusion.10), channel_id=1, source_target_pairs={{0,4},{2,6},{4,0},{6,2},{8,12},{10,14},{12,8},{14,10},{16,20},{18,... | collective-permute-start | bytes 480008 | tf_op jit(solution)/shard_map/ppermute | solution.py:595
  707.9 4.7 collective-permute-start.61
  714.4 22.6 %collective-permute-start.49 = (bf16[25,3200]{1,0:T(8,128)(2,1)S(1)}, bf16[25,3200]{1,0:T(8,128)(2,1)S(1)}, u32[]{:S(2)}, u32[]{:S(2)}) collective-permute-start(bf16[25,3200]{1,0:T(8,128)(2,1)S(1)} %add_convert_fusion.9), channel_id=1, source_target_pairs={{0,8},{2,10},{4,12},{6,14},{8,0},{10,2},{12,4},{14,6},{16,24},{18,... | collective-permute-start | bytes 480008 | tf_op jit(solution)/shard_map/ppermute | solution.py:595
  716.6 43.0 %collective-permute-start.60 = (bf16[100,1536]{1,0:T(8,128)(2,1)S(1)}, bf16[100,1536]{1,0:T(8,128)(2,1)S(1)}, u32[]{:S(2)}, u32[]{:S(2)}) collective-permute-start(bf16[100,1536]{1,0:T(8,128)(2,1)S(1)} %slice.417), channel_id=1, source_target_pairs={{0,16},{2,18},{4,20},{6,22},{8,24},{10,26},{12,28},{14,30},{16,0},... | collective-permute-start | bytes 921608 | tf_op jit(solution)/shard_map/ppermute | solution.py:96
  737.1 19.8 %collective-permute-start.50 = (bf16[25,3200]{1,0:T(8,128)(2,1)S(1)}, bf16[25,3200]{1,0:T(8,128)(2,1)S(1)}, u32[]{:S(2)}, u32[]{:S(2)}) collective-permute-start(bf16[25,3200]{1,0:T(8,128)(2,1)S(1)} %add_convert_fusion.8), channel_id=1, source_target_pairs={{0,16},{2,18},{4,20},{6,22},{8,24},{10,26},{12,28},{14,30},{16,0},... | collective-permute-start | bytes 480008 | tf_op jit(solution)/shard_map/ppermute | solution.py:595
  738.1 25.8 %collective-permute-start.58 = (bf16[100,1664]{1,0:T(8,128)(2,1)S(1)}, bf16[100,1664]{1,0:T(8,128)(2,1)S(1)}, u32[]{:S(2)}, u32[]{:S(2)}) collective-permute-start(bf16[100,1664]{1,0:T(8,128)(2,1)S(1)} %slice.415), channel_id=1, source_target_pairs={{0,16},{2,18},{4,20},{6,22},{8,24},{10,26},{12,28},{14,30},{16,0},... | collective-permute-start | bytes 998408 | tf_op jit(solution)/shard_map/ppermute | solution.py:96
  (180 other events, 1612.3 us)
